TPU v7x, 32 devices: a whole 2x2x4 slice. The times are simulated.
32 devices in a mesh: kf: 4 (over z), lat: 8 (over y, x, core).
Axes of the slice: x: 2, y: 2, z: 4, core: 2. Of those that a mesh axis runs over, the one named last changes fastest.
Arguments:
- tokens: bfloat16 [4, 4096, 256], P('kf', 'lat'), may hold values from -6 to 6
- frame_ids: int32 [4, 4096], P('kf', 'lat'), may hold values from 0 to 31, as said below
- episodes: int32 [4, 32], P('kf'), may hold values from 0 to 10
- master: float32 [5619712], P('lat'), may hold values from -8 to 8
- moment_one: float32 [5619712], P('lat'), may hold values from -6 to 6
- moment_two: float32 [5619712], P('lat'), may hold values from 0.0001 to 0.003
- latent_grad: bfloat16 [4, 32, 512, 512], P('kf', None, 'lat'), may hold values from -6 to 6
Outputs:
- latents_out: bfloat16 [4, 32, 512, 512], P('kf', None, 'lat')
- token_grad: bfloat16 [4, 4096, 256], P('kf', 'lat')
- param_grad: float32 [5619712], P('lat')
- lamb_update: float32 [5619712], P('lat')
- new_moment_one: float32 [5619712], P('lat')
- new_moment_two: float32 [5619712], P('lat')
- trust: float32 [13], replicated
- bias_grad: float32 [2, 2048], replicated
Inputs may be any that keep to these rules, and one draw needn't show every extreme that they name: `frame_ids`: every keyframe has 1 to 512 tokens in its group; in each group, exactly four keyframes have 512 tokens.
All inputs are finite; a program needn't handle non-finite values.
Results may differ from a plain program's by a relative error of at most 0.017.
Values may be sent and summed in bfloat16 or wider, within the bound.
A program may use at most 320 MiB of HBM per device.

v0:
```python
import functools
import math

import jax
import jax.numpy as jnp
from jax import lax
from jax.experimental import pallas as pl
from jax.experimental.pallas import tpu as pltpu
from jax.sharding import PartitionSpec as P

DIN = 256
D = 512
LAT = 512
CH = 64
HEADS = 8
HEAD_DIM = 64
FF = 2048
EPISODES = 11
NPARAM = 5619712
LANES = 128

norm_eps = 1e-05
masked_fill = -1e30
beta_one = 0.9
beta_two = 0.999
adam_eps = 1e-06
decay_rate = 0.01
clip_fraction = 0.5
lamb_step = 10.0

BF = jnp.bfloat16
F32 = jnp.float32
MIB = 1024 * 1024


def param_layout():
    return [
        ("latent", (LAT, D)),
        ("episode", (EPISODES, D)),
        ("tok_norm", (2, DIN)),
        ("lat_norms", (8, D)),
        ("w_kv", (DIN, 2 * CH)),
        ("w_q", (D, CH)),
        ("w_o", (CH, D)),
        ("w_qkv", (D, 3 * D)),
        ("w_so", (D, D)),
        ("w_up", (2, D, FF)),
        ("w_down", (2, FF, D)),
        ("hid_bias", (2, FF)),
        ("out_bias", (4, D)),
    ]


def split_flat(flat_vector):
    pieces = {}
    offset = 0
    for tensor_name, tensor_shape in param_layout():
        entries = math.prod(tensor_shape)
        pieces[tensor_name] = flat_vector[offset : offset + entries].reshape(tensor_shape)
        offset += entries
    return pieces


def layer_norm(inputs, norm_gain, norm_bias):
    row_mean = jnp.mean(inputs, axis=-1, keepdims=True)
    centered = inputs - row_mean
    row_var = jnp.mean(centered * centered, axis=-1, keepdims=True)
    return centered * lax.rsqrt(row_var + norm_eps) * norm_gain + norm_bias


def mm(left, right):
    return jnp.dot(left, right, preferred_element_type=F32)


def mm_t(left, right):
    return lax.dot_general(left, right, (((1,), (1,)), ((), ())), preferred_element_type=F32)


def t_mm(left, right):
    return lax.dot_general(left, right, (((0,), (0,)), ((), ())), preferred_element_type=F32)


def norm_stats(rows):
    mean = jnp.mean(rows, axis=-1, keepdims=True)
    centered = rows - mean
    var = jnp.mean(centered * centered, axis=-1, keepdims=True)
    rstd = lax.rsqrt(var + norm_eps)
    return centered * rstd, rstd


def norm_back(grad, xhat, rstd, gain):
    dxh = grad * gain
    first = jnp.mean(dxh, axis=-1, keepdims=True)
    second = jnp.mean(dxh * xhat, axis=-1, keepdims=True)
    return rstd * (dxh - first - xhat * second)


def col_sum(values):
    return jnp.sum(values, axis=0, keepdims=True)


def gelu_pair(x):
    size = jnp.abs(x)
    t = pl.reciprocal(1.0 + (0.3275911 / math.sqrt(2.0)) * size, approx=True)
    e = jnp.exp(x * x * -0.5)
    poly = 0.5 * 1.061405429
    for coef in (-1.453152027, 1.421413741, -0.284496736, 0.254829592):
        poly = poly * t + 0.5 * coef
    tail = poly * t * e
    cdf = jnp.where(x >= 0.0, 1.0 - tail, tail)
    return x * cdf, cdf + x * (e * (1.0 / math.sqrt(2.0 * math.pi)))


def accumulate(first, ref, value):
    @pl.when(first)
    def _():
        ref[...] = value

    @pl.when(jnp.logical_not(first))
    def _():
        ref[...] += value


def lane_half(shape, half):
    lane = lax.broadcasted_iota(jnp.int32, shape, 1)
    return (lane >= half * 64) & (lane < half * 64 + 64)


def keep_half(values, half):
    return jnp.where(lane_half(values.shape, half), values, jnp.zeros_like(values))


def select_tokens(rank_rows, cap):
    slot = lax.broadcasted_iota(jnp.int32, (cap, LANES), 0)
    parts = []
    for r in range(rank_rows.shape[0]):
        hit = slot == rank_rows[r : r + 1, :]
        parts.append(jnp.where(hit, 1.0, 0.0).astype(BF))
    return jnp.concatenate(parts, axis=1)


def cross_scores(kvf, queries_scaled, count):
    scores = mm_t(kvf, queries_scaled)
    slot = lax.broadcasted_iota(jnp.int32, scores.shape, 0)
    return jnp.where(slot < count, scores, masked_fill)


def cross_attend(start, norms, w_q, kvf, count):
    xhat, unused = norm_stats(start)
    query_in = (xhat * norms[0:1, :] + norms[1:2, :]).astype(BF)
    queries = mm(query_in, w_q[...]).astype(BF) * jnp.asarray(0.125, BF)
    scores = cross_scores(kvf, queries, count)
    top = jnp.max(scores, axis=0, keepdims=True)
    terms = jnp.exp(scores - top)
    total = jnp.sum(terms, axis=0, keepdims=True)
    prob = (terms * (1.0 / total)).astype(BF)
    return t_mm(kvf, prob).T.astype(BF), top + jnp.log(total)


def cross_fwd_kernel(latent, episode, norms, w_q, w_o, out_bias, kv, rank, count, h1, kvf_out, co_out, lse_out):
    cap = kvf_out.shape[1]
    start = latent[...].astype(F32) + episode[0]
    chunk = 8 * LANES
    chunks = kv.shape[0] // chunk

    def step(j, acc):
        sel = select_tokens(rank[0, pl.ds(pl.multiple_of(j * 8, 8), 8), :], cap)
        return acc + mm(sel, kv[pl.ds(pl.multiple_of(j * chunk, chunk), chunk), :])

    kvf = lax.fori_loop(0, chunks, step, jnp.zeros((cap, LANES), F32)).astype(BF)
    co, lse = cross_attend(start, norms, w_q, kvf, count[0, 0:1, 0:1])
    h1[...] = start + mm(co, w_o[...]) + out_bias[0:1, :]
    kvf_out[0] = kvf
    co_out[...] = co
    lse_out[0] = lse


def segment_hot(starts, ends, base, rows):
    row = lax.broadcasted_iota(jnp.int32, (16, rows), 1) + base
    return jnp.where((row >= starts[:, 0:1]) & (row < ends[:, 0:1]), 1.0, 0.0).astype(BF)


def segment_sums(hot, squares):
    high = squares.astype(BF)
    low = (squares - high.astype(F32)).astype(BF)
    return mm(hot, high) + mm(hot, low)


def grad_stats_kernel(base, starts, ends, summed, master, grad_sq, weight_sq):
    i = pl.program_id(0)
    rows = master.shape[0]
    hot = segment_hot(starts, ends, base[0] + i * rows, rows)
    grad = summed[...].astype(F32)
    accumulate(i == 0, grad_sq, col_sum(grad * grad))
    accumulate(i == 0, weight_sq, segment_sums(hot, master[...] * master[...]))


def lamb_kernel(base, stats, starts, ends, summed, master, one, two, grad_out, update_out, one_out, two_out, update_sq):
    i = pl.program_id(0)
    rows = master.shape[0]
    hot = segment_hot(starts, ends, base[0] + i * rows, rows)
    total_sq = jnp.sum(stats[0:1, :], axis=1, keepdims=True)
    clip = jnp.minimum(1.0, clip_fraction * math.sqrt(NPARAM) / (jnp.sqrt(total_sq) + 1e-06))
    grad = summed[...].astype(F32)
    grad_out[...] = grad
    clipped = clip * grad
    new_one = beta_one * one[...] + (1.0 - beta_one) * clipped
    new_two = beta_two * two[...] + (1.0 - beta_two) * clipped * clipped
    one_out[...] = new_one
    two_out[...] = new_two
    first_hat = new_one * (1.0 / (1.0 - beta_one**lamb_step))
    second_hat = new_two * (1.0 / (1.0 - beta_two**lamb_step))
    update = first_hat / (jnp.sqrt(second_hat) + adam_eps) + decay_rate * master[...]
    update_out[...] = update
    accumulate(i == 0, update_sq, segment_sums(hot, update * update))


BATCH = 256
HALF = 128
QUARTER = 64
MESH = pl.DeviceIdType.MESH


class Place:
    def __init__(self):
        self.z = lax.axis_index("kf")
        self.me = lax.axis_index("lat")
        self.core = lax.rem(self.me, 2)
        self.x = lax.rem(self.me // 2, 2)
        self.y = self.me // 4
        self.z_low = lax.rem(self.z, 2)
        self.z_high = self.z // 2
        self.sibling = (self.z, self.me + 1 - 2 * self.core)
        self.x_side = (self.z, self.me + 2 - 4 * self.x)
        self.y_side = (self.z, self.me + 4 - 8 * self.y)
        self.z_near = (self.z + 1 - 2 * self.z_low, self.me)
        self.z_far = (self.z + 2 - 4 * self.z_high, self.me)

    def z_other(self, step):
        return (lax.rem(self.z + step, 4), self.me)

    def lat_other(self, step):
        return (self.z, lax.rem(self.me + step, 8))


def remote(src, dst, send, recv, device):
    return pltpu.make_async_remote_copy(
        src_ref=src, dst_ref=dst, send_sem=send, recv_sem=recv, device_id=device, device_id_type=MESH
    )


def greet(devices):
    barrier = pltpu.get_barrier_semaphore()
    for device in devices:
        pl.semaphore_signal(barrier, inc=1, device_id=device, device_id_type=MESH)
    pl.semaphore_wait(barrier, len(devices))


def added(left, right):
    return (left.astype(F32) + right.astype(F32)).astype(BF)


class Reduction:
    lags = (0, 1, 3, 5, 7, 9, 11)

    def __init__(self, place, grads, out, bufs, sems):
        self.p = place
        self.grads = grads
        self.out = out
        self.own, self.rc, self.r1, self.r2, self.r3, self.r4, self.res = bufs
        self.own_sem, self.send, self.rc_sem, self.r1_sem, self.r2_sem, self.r3_sem, self.r4_sem, self.res_sem = sems
        self.shard = grads.shape[3]
        self.batches = pl.cdiv(self.shard, BATCH)
        self.back = self.batches * BATCH - self.shard

    @staticmethod
    def scratch(shard):
        n = pl.cdiv(shard, BATCH)
        bufs = [
            pltpu.VMEM((2, 2, 2, BATCH, LANES), BF),
            pltpu.VMEM((n, 2, 2, BATCH, LANES), BF),
            pltpu.VMEM((n, 2, 2, HALF, LANES), BF),
            pltpu.VMEM((n, 2, HALF, LANES), BF),
            pltpu.VMEM((n, HALF, LANES), BF),
            pltpu.VMEM((n, QUARTER, LANES), BF),
            pltpu.VMEM((n, BATCH, LANES), BF),
        ]
        dma = pltpu.SemaphoreType.DMA
        sems = [dma((2,)), dma((10, 4)), dma((n,)), dma((n, 2)), dma((n, 2)), dma((n,)), dma((n,)), dma((n, 3))]
        return bufs + sems

    def row(self, i):
        return pl.multiple_of(i * BATCH - (i // (self.batches - 1)) * self.back, 16)

    def own_copy(self, i):
        slot = lax.rem(i, 2)
        src = self.grads.at[:, :, self.p.core, pl.ds(self.row(i), BATCH), :]
        return pltpu.make_async_copy(src, self.own.at[slot], self.own_sem.at[slot])

    def copies(self, stage, i):
        p, slot = self.p, lax.rem(i, 4)
        if stage == 0:
            src = self.grads.at[:, :, 1 - p.core, pl.ds(self.row(i), BATCH), :]
            return [remote(src, self.rc.at[i], self.send.at[0, slot], self.rc_sem.at[i], p.sibling)]
        if stage == 1:
            to_x = self.rc.at[i, :, 1 - p.x, pl.ds(0, HALF), :]
            to_y = self.rc.at[i, 1 - p.y, :, pl.ds(HALF, HALF), :]
            return [
                remote(to_x, self.r1.at[i, 0], self.send.at[1, slot], self.r1_sem.at[i, 0], p.x_side),
                remote(to_y, self.r1.at[i, 1], self.send.at[2, slot], self.r1_sem.at[i, 1], p.y_side),
            ]
        if stage == 2:
            to_y = self.r1.at[i, 0, 1 - p.y]
            to_x = self.r1.at[i, 1, 1 - p.x]
            return [
                remote(to_y, self.r2.at[i, 0], self.send.at[3, slot], self.r2_sem.at[i, 0], p.y_side),
                remote(to_x, self.r2.at[i, 1], self.send.at[4, slot], self.r2_sem.at[i, 1], p.x_side),
            ]
        if stage == 3:
            src = self.r2.at[i, 1 - p.z_low]
            return [remote(src, self.r3.at[i], self.send.at[5, slot], self.r3_sem.at[i], p.z_near)]
        if stage == 4:
            src = self.r3.at[i, pl.ds(pl.multiple_of((1 - p.z_high) * QUARTER, QUARTER), QUARTER), :]
            return [remote(src, self.r4.at[i], self.send.at[6, slot], self.r4_sem.at[i], p.z_far)]
        mine = self.res.at[i, pl.ds(pl.multiple_of(p.z_low * HALF + p.z_high * QUARTER, QUARTER), QUARTER), :]
        return [
            remote(mine, mine, self.send.at[6 + d, slot], self.res_sem.at[i, d - 1], p.z_other(d))
            for d in (1, 2, 3)
        ]

    def launch(self, stage, i):
        @pl.when(i >= 4)
        def _():
            for copy in self.copies(stage, i - 4):
                copy.wait_send()

        for copy in self.copies(stage, i):
            copy.start()

    def landed(self, stage, i):
        for copy in self.copies(stage, i):
            copy.wait_recv()

    def work(self, stage, i):
        p = self.p
        if stage == 0:
            self.own_copy(i).start()
        elif stage == 1:
            self.landed(0, i)
            self.own_copy(i).wait()
            self.rc[i] = added(self.rc[i], self.own[lax.rem(i, 2)])
        elif stage == 2:
            self.landed(1, i)
            self.r1[i, 0] = added(self.r1[i, 0], self.rc[i, :, p.x, 0:HALF, :])
            self.r1[i, 1] = added(self.r1[i, 1], self.rc[i, p.y, :, HALF:BATCH, :])
        elif stage == 3:
            self.landed(2, i)
            self.r2[i, 0] = added(self.r2[i, 0], self.r1[i, 0, p.y])
            self.r2[i, 1] = added(self.r2[i, 1], self.r1[i, 1, p.x])
        elif stage == 4:
            self.landed(3, i)
            self.r3[i] = added(self.r3[i], self.r2[i, p.z_low])
        elif stage == 5:
            self.landed(4, i)
            part = self.r3[i, pl.ds(pl.multiple_of(p.z_high * QUARTER, QUARTER), QUARTER), :]
            at = pl.multiple_of(p.z_low * HALF + p.z_high * QUARTER, QUARTER)
            self.res[i, pl.ds(at, QUARTER), :] = added(self.r4[i], part)
        else:
            self.landed(5, i)
            self.out[pl.ds(self.row(i), BATCH), :] = self.res[i]
        if stage < 6:
            self.launch(stage, i)

    def tick(self, t):
        for stage, lag in enumerate(self.lags):
            i = t - lag

            @pl.when((i >= 0) & (i < self.batches))
            def _(stage=stage, i=i):
                self.work(stage, i)

    def ticks(self):
        return self.batches + self.lags[-1]

    def finish(self):
        for stage in range(6):
            for back in range(4):
                for copy in self.copies(stage, self.batches - 4 + back):
                    copy.wait_send()

    def partners(self):
        p = self.p
        return [p.sibling, p.x_side, p.y_side] + [p.z_other(d) for d in (1, 2, 3)]


def share_all(place, block, send, recv):
    mine = block.at[place.me]
    copies = [
        remote(mine, mine, send.at[d - 1], recv.at[d - 1], place.lat_other(d)) for d in range(1, 8)
    ]
    for copy in copies:
        copy.start()
    for copy in copies:
        copy.wait()


STAT_ROWS = 56


def reduce_kernel(bias_owner, bias_at, starts, ends, grads, master, summed, stats, *scratch):
    place = Place()
    block, block_send, block_recv = scratch[:3]
    red = Reduction(place, grads, summed, scratch[3:10], scratch[10:])
    greet([place.lat_other(d) for d in range(1, 8)] + [place.z_other(d) for d in (1, 2, 3)])
    lax.fori_loop(0, red.ticks(), lambda t, c: (red.tick(t), c)[1], 0)
    shard = master.shape[0]
    step = 784
    grad_sq = jnp.zeros((1, LANES), F32)
    weight_sq = jnp.zeros((16, LANES), F32)
    for j in range(shard // step):
        at = slice(j * step, (j + 1) * step)
        part = summed[at, :].astype(F32)
        grad_sq = grad_sq + col_sum(part * part)
        hot = segment_hot(starts, ends, place.me * shard + j * step, step)
        part = master[at, :]
        weight_sq = weight_sq + segment_sums(hot, part * part)
    bias = summed[bias_at : bias_at + 2 * FF // LANES, :].astype(F32)
    bias = jnp.where(place.me == bias_owner, bias, 0.0)
    head = jnp.concatenate([grad_sq, jnp.zeros((7, LANES), F32), weight_sq, bias], axis=0)
    block[pl.ds(place.me, 1)] = head[None]
    share_all(place, block, block_send, block_recv)
    total = block[0]
    for s in range(1, 8):
        total = total + block[s]
    stats[...] = total
    red.finish()


def trust_kernel(update_sq, stats, trust, block, send, recv):
    place = Place()
    greet([place.lat_other(d) for d in range(1, 8)])
    block[pl.ds(place.me, 1)] = update_sq[...][None]
    share_all(place, block, send, recv)
    total = block[0]
    for s in range(1, 8):
        total = total + block[s]
    update_norm = jnp.sqrt(jnp.sum(total, axis=1, keepdims=True))
    weight_norm = jnp.sqrt(jnp.sum(stats[8:24, :], axis=1, keepdims=True))
    trust[...] = jnp.broadcast_to(weight_norm / (update_norm + 1e-06), (16, LANES))


def relayout(whole, row, stage, dst, rows, cols):
    wide = cols // LANES
    block = min(rows, 2048 // wide // 128 * 128)

    def step(i, carry):
        at = pl.multiple_of(row + i * (block * wide), 16)
        stage[0 : block * wide, :] = whole[pl.ds(at, block * wide), :].astype(F32)
        for j in range(wide):
            part = stage[pl.ds(j, block, stride=wide), :]
            dst[pl.ds(pl.multiple_of(i * block, 16), block), j * LANES : (j + 1) * LANES] = part.astype(BF)
        return carry

    lax.fori_loop(0, rows // block, step, 0)


def small_matrix(whole, row, stage, rows, cols):
    wide = cols // LANES
    stage[0 : rows * wide, :] = whole[row : row + rows * wide, :].astype(F32)
    return jnp.concatenate([stage[pl.ds(j, rows, stride=wide), :] for j in range(wide)], axis=1)


class Gather:
    def __init__(self, place, whole, shard, chunks, send, recv):
        self.p, self.whole, self.shard, self.chunks, self.send, self.recv = place, whole, shard, chunks, send, recv
        p = place
        x_index, y_index = p.x_side[1], p.y_side[1]
        low = p.z_low
        self.first = x_index + low * (y_index - x_index)
        self.second = y_index + low * (x_index - y_index)
        self.diagonal = x_index + 4 - 8 * p.y

    def copy(self, kind, k):
        p = self.p
        block = (p.me, p.me, self.first, self.first, self.first, self.diagonal, self.second)[kind]
        target = (
            (p.z, self.first), p.sibling, (p.z, self.second), p.z_near, p.sibling, p.sibling, p.sibling
        )[kind]
        row, count = self.chunks[k]
        ref = self.whole.at[pl.ds(pl.multiple_of(block * self.shard + row, 16), count), :]
        return remote(ref, ref, self.send.at[kind, k], self.recv.at[kind, k], target)

    def tick(self, t):
        n = len(self.chunks)
        if t < n:
            self.copy(0, t).start()
            self.copy(1, t).start()
        if 0 <= t - 2 < n:
            self.copy(0, t - 2).wait_recv()
            for kind in (2, 3, 4):
                self.copy(kind, t - 2).start()
        if 0 <= t - 4 < n:
            self.copy(2, t - 4).wait_recv()
            self.copy(5, t - 4).start()
            self.copy(3, t - 4).wait_recv()
            self.copy(6, t - 4).start()
        if 0 <= t - 5 < n:
            for kind in (1, 4, 5, 6):
                self.copy(kind, t - 5).wait_recv()

    def ticks(self):
        return len(self.chunks) + 5

    def finish(self):
        for k in range(len(self.chunks)):
            for kind in range(7):
                self.copy(kind, k).wait_send()


class KeyExchange:
    def __init__(self, place, keys, send, recv):
        self.p, self.keys, self.send, self.recv = place, keys, send, recv
        self.x_index, self.y_index = place.x_side[1], place.y_side[1]
        self.diagonal = self.x_index + 4 - 8 * place.y

    def copy(self, kind):
        p = self.p
        half = self.keys.shape[1] // 2
        low, high, full = pl.ds(0, half), pl.ds(half, half), pl.ds(0, 2 * half)
        block, rows, target = (
            (p.me, full, p.x_side), (p.me, full, p.y_side), (p.me, full, p.sibling),
            (self.x_index, low, p.y_side), (self.y_index, high, p.x_side),
            (self.x_index, full, p.sibling), (self.y_index, full, p.sibling), (self.diagonal, full, p.sibling),
        )[kind]
        ref = self.keys.at[block, rows, :]
        return remote(ref, ref, self.send.at[kind], self.recv.at[kind], target)

    def step(self, s):
        if s == 0:
            waits, starts = (), (0, 1, 2)
        elif s == 1:
            waits, starts = (0, 1), (3, 4, 5, 6)
        elif s == 2:
            waits, starts = (3, 4), (7,)
        else:
            waits, starts = (2, 5, 6, 7), ()
        for kind in waits:
            self.copy(kind).wait_recv()
        for kind in starts:
            self.copy(kind).start()

    def finish(self):
        for kind in range(8):
            self.copy(kind).wait_send()


def flat_rows_of():
    rows, at = {}, 0
    for name, shape in param_layout():
        rows[name] = at // LANES
        at += math.prod(shape)
    return rows


def gather_chunks(shard):
    at = flat_rows_of()
    tail = at["hid_bias"] % shard // 16 * 16
    chunks = [(at["episode"], at["w_o"] - at["episode"]), (tail, shard - tail), (at["w_o"], at["w_qkv"] - at["w_o"])]
    for low, high in ((0, at["episode"]), (at["w_qkv"], tail)):
        while low < high:
            count = min(512, high - low)
            chunks.append((low, count))
            low += count
    return chunks


def begin_kernel(
    chunks, master, tokens, ids, hot,
    up_one, down_one, qkv_w, so_w, up_two, down_two,
    latent, norms, hid_bias, out_bias, w_q, w_o, w_kv, tok_norm, tok_normed, episode, rank, counts,
    kvf_out, co_out, lse_out, h1,
    whole, stage, all_ids, keys, m_up_one, m_down_one, m_qkv, m_so, m_up_two, m_down_two,
    send, recv, key_send, key_recv, id_send, id_recv, out_sem,
):
    place = Place()
    shard = master.shape[0]
    frames, cap = kvf_out.shape[0], kvf_out.shape[1]
    gather = Gather(place, whole, shard, chunks, send, recv)
    exchange = KeyExchange(place, keys, key_send, key_recv)
    at = flat_rows_of()
    greet([place.lat_other(d) for d in range(1, 8)] + [place.z_near])
    all_ids[pl.ds(place.me, 1)] = ids[...][None]
    id_copies = [
        remote(all_ids.at[place.me], all_ids.at[place.me], id_send.at[d - 1], id_recv.at[d - 1], place.lat_other(d))
        for d in range(1, 8)
    ]
    for copy in id_copies:
        copy.start()
    own_at = place.me * shard
    for row, count in chunks:
        whole[pl.ds(pl.multiple_of(own_at + row, 16), count), :] = master[row : row + count, :].astype(BF)
    for t in range(4):
        gather.tick(t)

    for copy in id_copies:
        copy.wait_recv()
    tags = jnp.concatenate([all_ids[s] for s in range(8)], axis=0)
    low = lax.broadcasted_iota(jnp.int32, (LANES, LANES), 0)
    high = lax.broadcasted_iota(jnp.int32, (LANES, LANES), 1)
    upto = jnp.where(low <= high, 1.0, 0.0).astype(BF)
    n = tags.shape[0]
    below = jnp.where(
        lax.broadcasted_iota(jnp.int32, (n, n), 1) < lax.broadcasted_iota(jnp.int32, (n, n), 0), 1.0, 0.0
    ).astype(BF)
    for f in range(frames):
        hit = tags == place.me * frames + f
        hit_low = jnp.where(hit, 1.0, 0.0).astype(BF)
        inside = mm(hit_low, upto)
        row_total = jnp.broadcast_to(inside[:, LANES - 1 : LANES], (n, LANES))
        before = mm(below, row_total.astype(BF))
        place_in = (inside + before).astype(jnp.int32) - 1
        rank[f] = jnp.where(hit, place_in, -1)
        total = jnp.sum(row_total[:, 0:1], axis=0, keepdims=True).astype(jnp.int32)
        counts[f] = jnp.broadcast_to(total, (8, LANES))
    for t in range(4, 7):
        gather.tick(t)

    pair = whole[at["tok_norm"] // 16 * 16 : at["lat_norms"], :].astype(F32)
    pair = pair[at["tok_norm"] % 16 : at["tok_norm"] % 16 + 4, :]
    tok_norm[...] = jnp.concatenate(
        [
            jnp.concatenate([pair[0:1], pair[1:2]], axis=1),
            jnp.concatenate([pair[2:3], pair[3:4]], axis=1),
        ],
        axis=0,
    )
    w_kv[...] = whole[at["w_kv"] : at["w_kv"] + DIN, :]
    xhat, unused = norm_stats(tokens[...].astype(F32))
    normed = (xhat * tok_norm[0:1, :] + tok_norm[1:2, :]).astype(BF)
    tok_normed[...] = normed
    keys[pl.ds(place.me, 1)] = mm(normed, w_kv[...]).astype(BF)[None]
    exchange.step(0)
    norms[...] = small_matrix(whole, at["lat_norms"], stage, 8, D)
    hid_bias[...] = small_matrix(whole, at["hid_bias"], stage, 2, FF)
    out_bias[...] = small_matrix(whole, at["out_bias"], stage, 4, D)
    episode_rows = mm(hot[...], small_matrix(whole, at["episode"], stage, 16, D).astype(BF))
    gather.tick(7)
    exchange.step(1)
    packed = whole[at["w_q"] : at["w_q"] + D // 2, :].astype(F32)
    stage[pl.ds(0, D // 2, stride=2), :] = packed
    stage[pl.ds(1, D // 2, stride=2), :] = pltpu.roll(packed, CH, 1)
    w_q[...] = keep_half(stage[0:D, :], 0).astype(BF)
    w_o[0:CH, :] = jnp.zeros((CH, D), BF)
    w_o[CH : 2 * CH, :] = small_matrix(whole, at["w_o"], stage, CH, D).astype(BF)
    gather.tick(8)
    exchange.step(2)
    for t in range(9, 12):
        gather.tick(t)
    exchange.step(3)
    relayout(whole, 0, stage, latent, LAT, D)

    tick = 12
    chunk = 8 * LANES
    for f in range(frames):
        start = latent[...].astype(F32) + episode_rows[f : f + 1, :]
        episode[f] = episode_rows[f : f + 1, :]
        kvf = jnp.zeros((cap, LANES), F32)
        for j in range(n // 8):
            sel = select_tokens(rank[f, 8 * j : 8 * j + 8, :], cap)
            rows = keys[2 * j : 2 * j + 2].reshape(chunk, LANES)
            kvf = kvf + mm(sel, rows)
        kvf = kvf.astype(BF)
        if tick < gather.ticks():
            gather.tick(tick)
            tick += 1
        co, lse = cross_attend(start, norms, w_q, kvf, counts[f, 0:1, 0:1])
        rows = slice(f * LAT, (f + 1) * LAT)
        h1[rows, :] = start + mm(co, w_o[...]) + out_bias[0:1, :]
        kvf_out[f] = kvf
        co_out[rows, :] = co
        lse_out[f] = lse
        if tick < gather.ticks():
            gather.tick(tick)
            tick += 1
    while tick < gather.ticks():
        gather.tick(tick)
        tick += 1

    big = (
        (up_one, m_up_one, at["w_up"], D, FF),
        (down_one, m_down_one, at["w_down"], FF, D),
        (qkv_w, m_qkv, at["w_qkv"], D, 3 * D),
        (so_w, m_so, at["w_so"], D, D),
        (up_two, m_up_two, at["w_up"] + D * FF // LANES, D, FF),
        (down_two, m_down_two, at["w_down"] + D * FF // LANES, FF, D),
    )
    outs = []
    for j, (out, held, row, rows, cols) in enumerate(big):
        relayout(whole, row, stage, held, rows, cols)
        outs.append(pltpu.make_async_copy(held, out, out_sem.at[j]))
        outs[-1].start()
    for copy in outs:
        copy.wait()
    for copy in id_copies:
        copy.wait_send()
    exchange.finish()
    gather.finish()


def begin_all(master_rows, token_rows, ids, hot, frames, cap):
    shard = master_rows.shape[0]
    tokens = token_rows.shape[0]
    total = 8 * tokens
    chunks = gather_chunks(shard)
    vmem = pl.BlockSpec(memory_space=pltpu.VMEM)
    anywhere = pl.BlockSpec(memory_space=pl.ANY)
    matrices = [(D, FF), (FF, D), (D, 3 * D), (D, D), (D, FF), (FF, D)]
    dma = pltpu.SemaphoreType.DMA
    return pl.pallas_call(
        functools.partial(begin_kernel, chunks),
        out_shape=[shaped(m, BF) for m in matrices]
        + [
            shaped((LAT, D), BF),
            shaped((8, D)),
            shaped((2, FF)),
            shaped((4, D)),
            shaped((D, LANES), BF),
            shaped((LANES, D), BF),
            shaped((DIN, LANES), BF),
            shaped((2, DIN)),
            shaped((tokens, DIN), BF),
            shaped((frames, 1, D)),
            shaped((frames, total // LANES, LANES), jnp.int32),
            shaped((frames, 8, LANES), jnp.int32),
            shaped((frames, cap, LANES), BF),
            shaped((frames * LAT, LANES), BF),
            shaped((frames, 1, LAT)),
            shaped((frames * LAT, D)),
        ],
        in_specs=[vmem] * 4,
        out_specs=[anywhere] * 6 + [vmem] * 16,
        scratch_shapes=[
            pltpu.VMEM((8 * shard, LANES), BF),
            pltpu.VMEM((2048, LANES), F32),
            pltpu.VMEM((8, tokens // LANES, LANES), jnp.int32),
            pltpu.VMEM((8, tokens, LANES), BF),
        ]
        + [pltpu.VMEM(m, BF) for m in matrices]
        + [
            dma((7, len(chunks))), dma((7, len(chunks))), dma((8,)), dma((8,)), dma((7,)), dma((7,)), dma((6,)),
        ],
        compiler_params=pltpu.CompilerParams(
            collective_id=3, has_side_effects=True, vmem_limit_bytes=56 * MIB
        ),
    )(master_rows, token_rows, ids, hot)


FCHUNK = 512


def add_flat(acc, row, part):
    wide = part.shape[1] // LANES
    for j in range(wide):
        at = pl.ds(row + j, part.shape[0], stride=wide)
        acc[at, :] = acc[at, :] + part[:, j * LANES : (j + 1) * LANES]


def to_flat(stage, matrix):
    rows, wide = matrix.shape[0], matrix.shape[1] // LANES
    for j in range(wide):
        stage[pl.ds(j, rows, stride=wide), :] = matrix[:, j * LANES : (j + 1) * LANES]
    return stage[0 : rows * wide, :]


def feed_forward(rows, gain, bias, up_bias, down_bias, w_up, w_down, act_ref, slope_ref):
    xhat, rstd = norm_stats(rows)
    normed = (xhat * gain + bias).astype(BF)
    total = rows + down_bias
    for c in range(FF // FCHUNK):
        at = slice(c * FCHUNK, (c + 1) * FCHUNK)
        act, slope = gelu_pair(mm(normed, w_up[:, at]) + up_bias[:, at])
        act = act.astype(BF)
        act_ref[:, at] = act
        slope_ref[:, at] = slope.astype(BF)
        total = total + mm(act, w_down[at, :])
    return total, normed, xhat, rstd


def feed_back(grad_low, grad_rows, normed, xhat, rstd, gain, act, slope, w_up, w_down, acc_up, acc_down, dhid, dnorm, dout):
    grad_normed = jnp.zeros(grad_rows.shape, F32)
    normed_t = normed.T
    for c in range(FF // FCHUNK):
        at = slice(c * FCHUNK, (c + 1) * FCHUNK)
        dpre = (mm_t(grad_low, w_down[at, :]) * slope[:, at].astype(F32)).astype(BF)
        dhid[:, at] += col_sum(dpre.astype(F32))
        grad_normed = grad_normed + mm_t(dpre, w_up[:, at])
        part = mm(normed_t, dpre)
        for j in range(FCHUNK // LANES):
            rows = pl.ds(c * (FCHUNK // LANES) + j, D, stride=FF // LANES)
            acc_up[rows, :] = acc_up[rows, :] + part[:, j * LANES : (j + 1) * LANES]
        add_flat(acc_down, c * FCHUNK * (D // LANES), mm(act[:, at].T, grad_low))
    dnorm[...] += jnp.concatenate([col_sum(grad_normed * xhat), col_sum(grad_normed)], axis=0)
    dout[...] += col_sum(grad_low.astype(F32))
    return grad_rows + norm_back(grad_normed, xhat, rstd, gain)


def clear(first, refs):
    @pl.when(first)
    def _():
        for ref in refs:
            ref[...] = jnp.zeros_like(ref)


def write_flat(flat, low, pieces, sems):
    copies = []
    for j, (acc, row) in enumerate(pieces):
        count = acc.shape[0]
        slot = j % 2
        if j >= 2:
            copies[j - 2].wait()
        low[slot, 0:count, :] = acc[...].astype(BF)
        copies.append(
            pltpu.make_async_copy(low.at[slot, pl.ds(0, count), :], flat.at[pl.ds(row, count), :], sems.at[slot])
        )
        copies[-1].start()
    for copy in copies[-2:]:
        copy.wait()


def forward_kernel(
    h1, grad, norms, hid_bias, out_bias, up_one, down_one, w_qkv, w_so, up_two, down_two,
    h2_out, qkv, lse_out, mixed_out, act_one, slope_one, latents, g3, dhid, dnorm, dout, flat,
    act_two, slope_two, acc_up, acc_down, low, sems,
):
    step = pl.program_id(0)
    clear(step == 0, (acc_up, acc_down, dhid, dnorm, dout))
    h2, unused, unused, unused = feed_forward(
        h1[...], norms[2:3, :], norms[3:4, :], hid_bias[0:1, :], out_bias[1:2, :], up_one, down_one, act_one, slope_one
    )
    h2_out[...] = h2
    xhat, unused = norm_stats(h2)
    sa_in = (xhat * norms[4:5, :] + norms[5:6, :]).astype(BF)
    for c in range(3):
        at = slice(c * D, (c + 1) * D)
        qkv[:, at] = mm(sa_in, w_qkv[:, at]).astype(BF)

    scale = jnp.asarray(0.125, BF)
    mixed_rows = []
    for pair in range(HEADS // 2):
        base = pair * LANES
        query_pair = qkv[:, base : base + LANES] * scale
        key_pair = qkv[:, D + base : D + base + LANES]
        value_t = qkv[:, 2 * D + base : 2 * D + base + LANES].T
        for half in range(2):
            scores = mm_t(key_pair, keep_half(query_pair, half))
            top = jnp.max(scores, axis=0, keepdims=True)
            terms = jnp.exp(scores - top)
            total = jnp.sum(terms, axis=0, keepdims=True)
            prob = (terms * (1.0 / total)).astype(BF)
            head = 2 * pair + half
            lse_out[0, head : head + 1, :] = top + jnp.log(total)
            mixed_rows.append(mm(value_t[half * 64 : half * 64 + 64, :], prob))
    mixed = jnp.concatenate(mixed_rows, axis=0).T.astype(BF)
    mixed_out[...] = mixed
    h3 = h2 + mm(mixed, w_so[...]) + out_bias[2:3, :]

    total, normed, xhat, rstd = feed_forward(
        h3, norms[6:7, :], norms[7:8, :], hid_bias[1:2, :], out_bias[3:4, :], up_two, down_two, act_two, slope_two
    )
    latents[...] = total.astype(BF)
    grad_low = grad[...]
    g3[...] = feed_back(
        grad_low, grad_low.astype(F32), normed, xhat, rstd, norms[6:7, :], act_two, slope_two, up_two, down_two,
        acc_up, acc_down, dhid, dnorm, dout,
    )

    @pl.when(step == pl.num_programs(0) - 1)
    def _():
        at = flat_rows_of()
        half = D * FF // LANES
        write_flat(flat, low, [(acc_up, at["w_up"] + half), (acc_down, at["w_down"] + half)], sems)


def backward_kernel(
    qkv, lse, mixed, g3, h2, h1, act_one, slope_one, kvf_in, co_in, cross_lse, rank, count, episode, hot,
    latent, norms, w_so, w_qkv, up_one, down_one, w_q, w_o, dhid_two, dnorm_two, dout_two, flat_in,
    dkv_t, flat,
    dqkv, acc_up, acc_down, acc_qkv, acc_so, acc_latent, acc_q, acc_o, acc_episode,
    dhid, dnorm_sa, dnorm_one, dnorm_cross, dout_so, dout_one, dout_cross, stage, low, sems,
):
    step = pl.program_id(0)
    clear(
        step == 0,
        (
            acc_up, acc_down, acc_qkv, acc_so, acc_latent, acc_q, acc_o, acc_episode, dhid, dnorm_sa, dnorm_one,
            dnorm_cross, dout_so, dout_one, dout_cross, dkv_t,
        ),
    )
    scale = jnp.asarray(0.125, BF)
    grad_three = g3[...]
    grad_low = grad_three.astype(BF)
    dout_so[...] += col_sum(grad_low.astype(F32))
    add_flat(acc_so, 0, t_mm(mixed[...], grad_low))
    grad_mixed = mm_t(grad_low, w_so[...]).astype(BF)
    for pair in range(HEADS // 2):
        base = pair * LANES
        query_pair = qkv[:, base : base + LANES] * scale
        key_pair = qkv[:, D + base : D + base + LANES]
        value_pair = qkv[:, 2 * D + base : 2 * D + base + LANES]
        grad_pair = grad_mixed[:, base : base + LANES]
        key_t = key_pair.T
        query_t = []
        grad_key = jnp.zeros((LAT, LANES), F32)
        grad_value = jnp.zeros((LAT, LANES), F32)
        for half in range(2):
            head = 2 * pair + half
            query = keep_half(query_pair, half)
            grad_head = keep_half(grad_pair, half)
            prob = jnp.exp(mm_t(key_pair, query) - lse[0, head : head + 1, :])
            grad_value = grad_value + mm(prob.astype(BF), grad_head)
            weighted = prob * mm_t(value_pair, grad_head)
            grad_score = (weighted - prob * col_sum(weighted)).astype(BF)
            grad_key = grad_key + mm(grad_score, query)
            query_t.append(mm(key_t[half * 64 : half * 64 + 64, :], grad_score))
        dqkv[:, base : base + LANES] = (jnp.concatenate(query_t, axis=0).T * 0.125).astype(BF)
        dqkv[:, D + base : D + base + LANES] = grad_key.astype(BF)
        dqkv[:, 2 * D + base : 2 * D + base + LANES] = grad_value.astype(BF)
    grad_in = mm_t(dqkv[...], w_qkv[...])
    xhat, rstd = norm_stats(h2[...])
    sa_t = (xhat * norms[4:5, :] + norms[5:6, :]).astype(BF).T
    for c in range(3):
        part = mm(sa_t, dqkv[:, c * D : (c + 1) * D])
        for j in range(D // LANES):
            rows = pl.ds(c * (D // LANES) + j, D, stride=3 * D // LANES)
            acc_qkv[rows, :] = acc_qkv[rows, :] + part[:, j * LANES : (j + 1) * LANES]
    dnorm_sa[...] += jnp.concatenate([col_sum(grad_in * xhat), col_sum(grad_in)], axis=0)
    grad_two = grad_three + norm_back(grad_in, xhat, rstd, norms[4:5, :])

    xhat, rstd = norm_stats(h1[...])
    normed = (xhat * norms[2:3, :] + norms[3:4, :]).astype(BF)
    grad_one = feed_back(
        grad_two.astype(BF), grad_two, normed, xhat, rstd, norms[2:3, :], act_one, slope_one, up_one, down_one,
        acc_up, acc_down, dhid, dnorm_one, dout_one,
    )

    cap = kvf_in.shape[1]
    start = latent[...].astype(F32) + episode[0]
    xhat, rstd = norm_stats(start)
    query_in = (xhat * norms[0:1, :] + norms[1:2, :]).astype(BF)
    queries = mm(query_in, w_q[...]).astype(BF) * scale
    kvf = kvf_in[0]
    branch = grad_one.astype(BF)
    grad_co = mm_t(branch, w_o[...]).astype(BF)
    acc_o[...] += t_mm(co_in[...], branch)
    dout_cross[...] += col_sum(branch.astype(F32))
    scores = cross_scores(kvf, queries, count[0, 0:1, 0:1])
    prob = jnp.exp(scores - cross_lse[0])
    weighted = prob * mm_t(kvf, grad_co)
    grad_score = (weighted - prob * col_sum(weighted)).astype(BF)
    grad_kv = (mm(grad_score, queries) + mm(prob.astype(BF), grad_co)).astype(BF)
    grad_query = (t_mm(kvf, grad_score).T * 0.125).astype(BF)
    acc_q[...] += t_mm(query_in, grad_query)
    grad_in = mm_t(grad_query, w_q[...])
    grad_start = grad_one + norm_back(grad_in, xhat, rstd, norms[0:1, :])
    dnorm_cross[...] += jnp.concatenate([col_sum(grad_in * xhat), col_sum(grad_in)], axis=0)
    add_flat(acc_latent, 0, grad_start)
    acc_episode[...] += hot[0, :, 0:1] * col_sum(grad_start)
    grad_kv_t = grad_kv.T
    chunk = 8 * LANES

    def scatter(j, carry):
        sel = select_tokens(rank[0, pl.ds(pl.multiple_of(j * 8, 8), 8), :], cap)
        dkv_t[:, pl.ds(pl.multiple_of(j * chunk, chunk), chunk)] += mm(grad_kv_t, sel)
        return carry

    lax.fori_loop(0, dkv_t.shape[1] // chunk, scatter, 0)

    @pl.when(step == pl.num_programs(0) - 1)
    def _():
        at = flat_rows_of()
        write_flat(
            flat, low,
            [
                (acc_up, at["w_up"]), (acc_down, at["w_down"]), (acc_qkv, at["w_qkv"]), (acc_so, at["w_so"]),
                (acc_latent, 0),
            ],
            sems,
        )
        small = at["w_qkv"] - at["w_q"]
        first = at["w_q"] - at["episode"]
        head = at["lat_norms"] - at["episode"]
        low[0, 0:first, :] = jnp.zeros((first, LANES), BF)
        norm_grads = jnp.concatenate([dnorm_cross[...], dnorm_one[...], dnorm_sa[...], dnorm_two[...]], axis=0)
        rows = jnp.concatenate([to_flat(stage, acc_episode[...])[0 : EPISODES * (D // LANES), :], jnp.zeros((head - EPISODES * (D // LANES), LANES), F32)], axis=0)
        rows = jnp.concatenate([rows, to_flat(stage, norm_grads)], axis=0)
        low[0, 0 : rows.shape[0], :] = rows.astype(BF)
        stage[0:D, :] = acc_q[...]
        even = stage[pl.ds(0, D // 2, stride=2), :]
        odd = pltpu.roll(stage[pl.ds(1, D // 2, stride=2), :], CH, 1)
        low[0, first : first + D // 2, :] = jnp.where(lane_half(even.shape, 0), even, odd).astype(BF)
        low[0, first + D // 2 : first + small, :] = to_flat(stage, acc_o[CH : 2 * CH, :]).astype(BF)
        hid = to_flat(stage, jnp.concatenate([dhid[...], dhid_two[...]], axis=0))
        low[1, 0 : hid.shape[0], :] = hid.astype(BF)
        outs = jnp.concatenate([dout_cross[...], dout_one[...], dout_so[...], dout_two[...]], axis=0)
        out_rows = 4 * D // LANES
        low[1, hid.shape[0] : hid.shape[0] + out_rows, :] = to_flat(stage, outs).astype(BF)
        total = hid.shape[0] + out_rows
        copies = [
            pltpu.make_async_copy(
                low.at[0, pl.ds(0, first + small), :], flat.at[pl.ds(at["episode"], first + small), :], sems.at[0]
            ),
            pltpu.make_async_copy(
                low.at[1, pl.ds(0, total), :], flat.at[pl.ds(at["hid_bias"], total), :], sems.at[1]
            ),
        ]
        for copy in copies:
            copy.start()
        for copy in copies:
            copy.wait()


def fixed(*shape):
    return pl.BlockSpec(shape, lambda i: (0,) * len(shape), pipeline_mode=pl.Buffered(1))


def kept(*shape):
    return pl.BlockSpec(shape, lambda i: (0,) * len(shape))


def rowed(rows, cols):
    return pl.BlockSpec((rows, cols), lambda i: (i, 0))


def framed(*shape):
    return pl.BlockSpec((1,) + shape, lambda i: (i,) + (0,) * len(shape))


def shaped(shape, dtype=F32):
    return jax.ShapeDtypeStruct(shape, dtype)


def call(kernel, grid, in_specs, outs, args, flops=0, trans=0, scratch=(), limit=56, aliases=None):
    out_specs, out_shapes = zip(*outs)
    moved = sum(math.prod(a.shape) * a.dtype.itemsize for a in args)
    moved += sum(math.prod(s.shape) * s.dtype.itemsize for s in out_shapes)
    return pl.pallas_call(
        kernel,
        grid=(grid,),
        in_specs=in_specs,
        out_specs=list(out_specs),
        out_shape=list(out_shapes),
        scratch_shapes=list(scratch),
        input_output_aliases=aliases or {},
        compiler_params=pltpu.CompilerParams(
            dimension_semantics=("arbitrary",), vmem_limit_bytes=limit * MIB
        ),
        cost_estimate=pl.CostEstimate(flops=flops, bytes_accessed=moved, transcendentals=trans),
    )(*args)


def reduce_all(local_flat, master_rows, starts, ends, bias_owner, bias_row):
    shard = master_rows.shape[0]
    vmem = pl.BlockSpec(memory_space=pltpu.VMEM)
    block = [
        pltpu.VMEM((8, STAT_ROWS, LANES), F32),
        pltpu.SemaphoreType.DMA((7,)),
        pltpu.SemaphoreType.DMA((7,)),
    ]
    return pl.pallas_call(
        functools.partial(reduce_kernel, bias_owner, bias_row),
        out_shape=[shaped((shard, LANES), BF), shaped((STAT_ROWS, LANES))],
        in_specs=[vmem, vmem, pl.BlockSpec(memory_space=pl.ANY), vmem],
        out_specs=[vmem, vmem],
        scratch_shapes=block + Reduction.scratch(shard),
        compiler_params=pltpu.CompilerParams(
            collective_id=1, has_side_effects=True, vmem_limit_bytes=48 * MIB
        ),
    )(starts, ends, local_flat.reshape(2, 2, 2, shard, LANES), master_rows)


def body(tokens, frame_ids, episodes, master, moment_one, moment_two, latent_grad):
    lat_count = lax.axis_size("lat")
    lat_index = lax.axis_index("lat")
    shard_len = master.shape[0]
    frame_total = episodes.shape[1]
    frames = frame_total // lat_count
    rows_total = frames * LAT
    total_keys = frame_ids.shape[1] * lat_count
    cap = total_keys // 8
    token_rows_count = total_keys // LANES

    reach = lat_count == 8 and lax.axis_size("kf") == 4
    shard_rows = shard_len // LANES
    master_rows = master.reshape(shard_rows, LANES)
    episode_index = jnp.arange(EPISODES, dtype=jnp.int32)
    own_episodes = lax.dynamic_slice_in_dim(episodes[0], lat_index * frames, frames, 0)
    episode_match = own_episodes[:, None] == episode_index[None, :]
    score_flops = rows_total * cap * LANES * 2
    select_flops = frames * cap * total_keys * LANES * 2
    if reach:
        hot = jnp.pad(episode_match.astype(BF), ((0, 16 - frames), (0, 16 - EPISODES)))
        (
            up_one, down_one, w_qkv, w_so, up_two, down_two,
            latent, norms, hid_bias, out_bias, w_q, w_o, w_kv, tok_norm, tok_normed, episode_rows, rank, counts,
            kvf, cross_out, cross_lse, h1,
        ) = begin_all(master_rows, tokens[0], frame_ids.reshape(-1, LANES), hot, frames, cap)
        latent_grad, h1 = lax.optimization_barrier((latent_grad, h1))
    else:
        weights = split_flat(lax.all_gather(master.astype(BF), "lat", axis=0, tiled=True))
        norms = weights["lat_norms"].astype(F32)
        out_bias = weights["out_bias"].astype(F32)
        hid_bias = weights["hid_bias"].astype(F32)
        tok_norm = weights["tok_norm"].astype(F32)
        w_kv, w_qkv, w_so, latent = (weights[name] for name in ("w_kv", "w_qkv", "w_so", "latent"))
        up_one, up_two = weights["w_up"]
        down_one, down_two = weights["w_down"]
        frame_tag = lax.all_gather(frame_ids[0].astype(BF), "lat", axis=0, tiled=True).astype(jnp.int32)
        own_frames = lat_index * frames + jnp.arange(frames, dtype=jnp.int32)
        own_hit = frame_tag[None, :] == own_frames[:, None]
        rank = jnp.cumsum(own_hit.astype(jnp.int32), axis=1) - 1
        counts = jnp.broadcast_to(rank[:, -1][:, None, None] + 1, (frames, 8, LANES))
        rank = jnp.where(own_hit, rank, -1).reshape(frames, token_rows_count, LANES)
        tok_normed = layer_norm(tokens[0].astype(F32), tok_norm[0], tok_norm[1]).astype(BF)
        key_value = mm(tok_normed, w_kv).astype(BF)
        all_keys = lax.all_gather(key_value, "lat", axis=0, tiled=True)
        episode_rows = mm(episode_match.astype(BF), weights["episode"]).reshape(frames, 1, D)
        w_q = jnp.pad(weights["w_q"], ((0, 0), (0, LANES - CH)))
        w_o = jnp.pad(weights["w_o"], ((LANES - CH, 0), (0, 0)))
        h1, kvf, cross_out, cross_lse = call(
            cross_fwd_kernel,
            frames,
            [
                fixed(LAT, D), framed(1, D), fixed(8, D), fixed(D, LANES), fixed(LANES, D), fixed(4, D),
                fixed(total_keys, LANES), framed(token_rows_count, LANES), framed(8, LANES),
            ],
            [
                (rowed(LAT, D), shaped((rows_total, D))),
                (framed(cap, LANES), shaped((frames, cap, LANES), BF)),
                (rowed(LAT, LANES), shaped((rows_total, LANES), BF)),
                (framed(1, LAT), shaped((frames, 1, LAT))),
            ],
            (latent, episode_rows, norms, w_q, w_o, out_bias, all_keys, rank, counts),
            flops=2 * score_flops + select_flops,
            trans=rows_total * cap,
        )
    grad_rows_in = lax.all_to_all(
        latent_grad[0], "lat", split_axis=0, concat_axis=1, tiled=True
    ).reshape(rows_total, D)

    mlp_flops = 4 * rows_total * D * FF
    attn_flops = 4 * rows_total * LAT * D
    flat_shape = (NPARAM // LANES, LANES)
    anywhere = pl.BlockSpec(memory_space=pl.ANY)
    slab = D * FF // LANES
    h2, qkv, self_lse, mixed, act_one, slope_one, latents, g3, dhid_two, dnorm_two, dout_two, flat = call(
        forward_kernel,
        frames,
        [
            rowed(LAT, D), rowed(LAT, D), fixed(8, D), fixed(2, FF), fixed(4, D), fixed(D, FF), fixed(FF, D),
            fixed(D, 3 * D), fixed(D, D), fixed(D, FF), fixed(FF, D),
        ],
        [
            (rowed(LAT, D), shaped((rows_total, D))),
            (rowed(LAT, 3 * D), shaped((rows_total, 3 * D), BF)),
            (framed(HEADS, LAT), shaped((frames, HEADS, LAT))),
            (rowed(LAT, D), shaped((rows_total, D), BF)),
            (rowed(LAT, FF), shaped((rows_total, FF), BF)),
            (rowed(LAT, FF), shaped((rows_total, FF), BF)),
            (rowed(LAT, D), shaped((rows_total, D), BF)),
            (rowed(LAT, D), shaped((rows_total, D))),
            (kept(1, FF), shaped((1, FF))),
            (kept(2, D), shaped((2, D))),
            (kept(1, D), shaped((1, D))),
            (anywhere, shaped(flat_shape, BF)),
        ],
        (h1, grad_rows_in, norms, hid_bias, out_bias, up_one, down_one, w_qkv, w_so, up_two, down_two),
        flops=4 * mlp_flops + 4 * attn_flops,
        trans=4 * rows_total * FF,
        scratch=[
            pltpu.VMEM((LAT, FF), BF), pltpu.VMEM((LAT, FF), BF), pltpu.VMEM((slab, LANES), F32),
            pltpu.VMEM((slab, LANES), F32), pltpu.VMEM((2, slab, LANES), BF), pltpu.SemaphoreType.DMA((2,)),
        ],
        limit=60,
    )
    latents_out = lax.all_to_all(
        latents.reshape(frames, LAT, D), "lat", split_axis=1, concat_axis=0, tiled=True
    )[None]
    hot_lanes = jnp.broadcast_to(
        jnp.pad(episode_match.astype(F32), ((0, 0), (0, 16 - EPISODES)))[:, :, None], (frames, 16, LANES)
    )
    dkv_t, flat = call(
        backward_kernel,
        frames,
        [
            rowed(LAT, 3 * D), framed(HEADS, LAT), rowed(LAT, D), rowed(LAT, D), rowed(LAT, D), rowed(LAT, D),
            rowed(LAT, FF), rowed(LAT, FF), framed(cap, LANES), rowed(LAT, LANES), framed(1, LAT),
            framed(token_rows_count, LANES), framed(8, LANES), framed(1, D), framed(16, LANES),
            fixed(LAT, D), fixed(8, D), fixed(D, D), fixed(D, 3 * D), fixed(D, FF), fixed(FF, D), fixed(D, LANES),
            fixed(LANES, D), fixed(1, FF), fixed(2, D), fixed(1, D), anywhere,
        ],
        [(kept(LANES, total_keys), shaped((LANES, total_keys))), (anywhere, shaped(flat_shape, BF))],
        (
            qkv, self_lse, mixed, g3, h2, h1, act_one, slope_one, kvf, cross_out, cross_lse, rank, counts,
            episode_rows, hot_lanes, latent, norms, w_so, w_qkv, up_one, down_one, w_q, w_o, dhid_two, dnorm_two,
            dout_two, flat,
        ),
        flops=2 * mlp_flops + 10 * attn_flops + 6 * score_flops,
        trans=rows_total * LAT * HEADS,
        scratch=[
            pltpu.VMEM((LAT, 3 * D), BF), pltpu.VMEM((slab, LANES), F32), pltpu.VMEM((slab, LANES), F32),
            pltpu.VMEM((3 * D * D // LANES, LANES), F32), pltpu.VMEM((D * D // LANES, LANES), F32),
            pltpu.VMEM((LAT * D // LANES, LANES), F32), pltpu.VMEM((D, LANES), F32), pltpu.VMEM((LANES, D), F32),
            pltpu.VMEM((16, D), F32), pltpu.VMEM((1, FF), F32), pltpu.VMEM((2, D), F32), pltpu.VMEM((2, D), F32),
            pltpu.VMEM((2, D), F32), pltpu.VMEM((1, D), F32), pltpu.VMEM((1, D), F32), pltpu.VMEM((1, D), F32),
            pltpu.VMEM((512, LANES), F32), pltpu.VMEM((2, slab, LANES), BF), pltpu.SemaphoreType.DMA((2,)),
        ],
        limit=60,
        aliases={26: 1},
    )
    grad_kv = lax.psum_scatter(dkv_t.T.astype(BF), "lat", scatter_dimension=0, tiled=True)
    grad_w_kv = t_mm(tok_normed, grad_kv)
    grad_tok_normed = mm_t(grad_kv, w_kv)
    unused, token_pull = jax.vjp(layer_norm, tokens[0].astype(F32), tok_norm[0], tok_norm[1])
    grad_tokens, grad_tok_gain, grad_tok_bias = token_pull(grad_tok_normed)
    token_grad = grad_tokens.astype(BF)[None]
    flat_at = flat_rows_of()
    tok_norm_grad = jnp.stack([grad_tok_gain, grad_tok_bias]).reshape(-1, LANES).astype(BF)
    flat = lax.dynamic_update_slice(flat, tok_norm_grad, (flat_at["tok_norm"], 0))
    flat = lax.dynamic_update_slice(flat, grad_w_kv.astype(BF), (flat_at["w_kv"], 0))
    local_flat = flat.reshape(-1)
    layout = param_layout()

    starts, ends, offset, bias_offset = [], [], 0, 0
    for name, shape in layout:
        if name == "hid_bias":
            bias_offset = offset
        starts.append(offset // LANES)
        offset += math.prod(shape)
        ends.append(offset // LANES)
    pad = [0] * (16 - len(layout))
    starts = jnp.broadcast_to(jnp.array(starts + pad, jnp.int32)[:, None], (16, LANES))
    ends = jnp.broadcast_to(jnp.array(ends + pad, jnp.int32)[:, None], (16, LANES))
    opt_rows = 784 if shard_rows % 784 == 0 else shard_rows
    opt_steps = shard_rows // opt_rows
    base = (lat_index * shard_rows).astype(jnp.int32).reshape(1)
    smem = pl.BlockSpec(memory_space=pltpu.SMEM)
    flat_rows = (shard_rows, LANES)
    bias_owner, bias_at = divmod(bias_offset, shard_len)
    if reach:
        summed, stats = reduce_all(local_flat, master_rows, starts, ends, bias_owner, bias_at // LANES)
    else:
        summed = lax.psum_scatter(local_flat, "lat", scatter_dimension=0, tiled=True)
        summed = lax.psum(summed, "kf").reshape(flat_rows)
        grad_sq, weight_sq = call(
            grad_stats_kernel,
            opt_steps,
            [smem, fixed(16, LANES), fixed(16, LANES), rowed(opt_rows, LANES), rowed(opt_rows, LANES)],
            [(kept(1, LANES), shaped((1, LANES))), (kept(16, LANES), shaped((16, LANES)))],
            (base, starts, ends, summed, master_rows),
        )
        bias_rows = summed[bias_at // LANES : bias_at // LANES + 2 * FF // LANES].astype(F32)
        bias_rows = jnp.where(lat_index == bias_owner, bias_rows, 0.0)
        stats = lax.psum(
            jnp.concatenate([grad_sq, jnp.zeros((7, LANES), F32), weight_sq, bias_rows]), "lat"
        )
    bias_grad = stats[24:STAT_ROWS].reshape(2, FF)
    grad_shard, lamb_update, new_one, new_two, update_sq = call(
        lamb_kernel,
        opt_steps,
        [smem, fixed(STAT_ROWS, LANES), fixed(16, LANES), fixed(16, LANES)] + [rowed(opt_rows, LANES)] * 4,
        [(rowed(opt_rows, LANES), shaped(flat_rows))] * 4 + [(kept(16, LANES), shaped((16, LANES)))],
        (
            base, stats, starts, ends, summed, master_rows,
            moment_one.reshape(flat_rows), moment_two.reshape(flat_rows),
        ),
    )
    if reach:
        vmem = pl.BlockSpec(memory_space=pltpu.VMEM)
        trust = pl.pallas_call(
            trust_kernel,
            out_shape=shaped((16, LANES)),
            in_specs=[vmem, vmem],
            out_specs=vmem,
            scratch_shapes=[
                pltpu.VMEM((8, 16, LANES), F32),
                pltpu.SemaphoreType.DMA((7,)),
                pltpu.SemaphoreType.DMA((7,)),
            ],
            compiler_params=pltpu.CompilerParams(collective_id=2, has_side_effects=True),
        )(update_sq, stats)[: len(layout), 0]
    else:
        update_sq = lax.psum(jnp.sum(update_sq, axis=1), "lat")
        weight_sq = jnp.sum(stats[8:24], axis=1)
        trust = (jnp.sqrt(weight_sq) / (jnp.sqrt(update_sq) + 1e-06))[: len(layout)]
    return (
        latents_out,
        token_grad,
        grad_shard.reshape(-1),
        lamb_update.reshape(-1),
        new_one.reshape(-1),
        new_two.reshape(-1),
        trust,
        bias_grad,
    )


def solution(mesh):
    return jax.shard_map(
        body,
        mesh=mesh,
        in_specs=(
            P("kf", "lat", None),
            P("kf", "lat"),
            P("kf", None),
            P("lat"),
            P("lat"),
            P("lat"),
            P("kf", None, "lat", None),
        ),
        out_specs=(
            P("kf", None, "lat", None),
            P("kf", "lat", None),
            P("lat"),
            P("lat"),
            P("lat"),
            P("lat"),
            P(),
            P(),
        ),
        check_vma=False,
    )
```

profile of v0, /device:TPU:0, one launch (start us, length us, event | category | flops | bytes accessed | tf_op | source)
XLA Modules:
  0.0 484.3 jit_solution(16118083371699146569)
XLA Ops:
  7.2 0.0 copy-start
  7.2 0.6 copy-done
  7.8 0.1 fusion.11
  7.9 0.1 iota_compare_fusion
  8.0 0.6 pad_convert_fusion.hot
  8.6 67.5 %shard_map.152 = (bf16[512,2048]{1,0:T(8,128)(2,1)}, bf16[2048,512]{1,0:T(8,128)(2,1)}, bf16[512,1536]{1,0:T(8,128)(2,1)}, bf16[512,512]{1,0:T(8,128)(2,1)}, bf1...) custom-call(f32[5488,128]{1,0:T(8,128)} %bitcast.38, ...), custom_call_target="tpu_custom_call" | custom-call | tf_op jit(solution)/shard_map/pallas_call | solution.py:719
  76.1 3.6 all-to-all-start
  79.7 0.0 reduce-scatter.2.cloned.1.call-start
  79.8 26.5 %all-to-all-done = bf16[32,64,512]{2,1,0:T(8,128)(2,1)S(1)} async-done(((bf16[32,64,512]{2,1,0:T(8,128)(2,1)}), bf16[32,64,512]{2,1,0:T(8,128)(2,1)S(1)}, u32[]{:S(2)}, u32[]{:S(2)}) %all-to-all-start) | async-done | bytes 2097184 | tf_op jit(solution)/shard_map/all_to_all | solution.py:1146
  106.3 1.5 copy.22
  107.7 128.7 %shard_map.153 = (f32[2048,512]{1,0:T(8,128)}, bf16[2048,1536]{1,0:T(8,128)(2,1)}, f32[4,8,512]{2,1,0:T(8,128)}, bf16[2048,512]{1,0:T(8,128)(2,1)}, bf16[2048,20...) custom-call(f32[2048,512]{1,0:T(8,128)} %get-tuple-element.54.h1, ...), custom_call_target="tpu_custom_call" | custom-call | flops 42949672960 | bytes 63789056 | tf_op jit(solution)/shard_map/pallas_call | solution.py:1046
  236.4 0.7 broadcast_in_dim.15.hot
  237.1 85.9 %shard_map.154 = (f32[128,4096]{1,0:T(8,128)}, bf16[43904,128]{1,0:T(8,128)(2,1)}) custom-call(bf16[2048,1536]{1,0:T(8,128)(2,1)} %get-tuple-element.66.qkv, f32[4,8,512]{2,1,0:T(8,128)} %get-tuple-element.67.lse, bf16[2048,512]{1,0:T(8,128)(2,1)} %get-tuple-element.68.mixed, f32[2048,512]{1,0:T(8,128)} %get-tuple-element.69.g3, ...), custom_call_target="tpu_custom_call", output_to_operand_aliasing={{1}: (26, {})} | custom-call | flops 40265318400 | bytes 70678528 | tf_op jit(solution)/shard_map/pallas_call | solution.py:1046
  323.1 0.0 copy-start.7
  323.1 0.0 copy-start.8
  323.1 2.8 convert_bitcast_fusion
  325.9 0.0 reduce-scatter.2.cloned.1.call-update
  326.0 0.0 copy-done.7
  326.0 0.1 convert_reduce_fusion
  326.1 0.2 fusion.5
  326.4 0.0 copy-done.8
  326.4 2.9 copy.23
  329.3 0.0 copy-start.11
  329.3 0.0 copy-start.2
  329.3 4.6 all-to-all-start.1
  334.0 0.0 copy-done.13
  334.0 35.3 %reduce-scatter.2.cloned.1.call-done = bf16[512,128]{0,1:T(8,128)(2,1)} async-done(((bf16[4096,128]{0,1:T(8,128)(2,1)}), bf16[512,128]{0,1:T(8,128)(2,1)}) %reduce-scatter.2.cloned.1.call-update) | async-done | bytes 131088 | tf_op jit(solution)/shard_map/reduce_scatter | solution.py:1220
  369.4 2.0 fusion.8
  371.4 0.6 constant_dynamic-update-slice_fusion
  372.0 1.8 fusion
  373.8 0.1 broadcast_in_dim.19.starts
  373.9 0.1 broadcast_in_dim.40.ends
  374.0 0.0 copy-done.2
  374.0 75.9 %shard_map.155 = (bf16[5488,128]{1,0:T(8,128)(2,1)S(1)}, f32[56,128]{1,0:T(8,128)S(1)}) custom-call(s32[16,128]{1,0:T(8,128)S(1)} %broadcast_in_dim.19.starts, s32[16,128]{1,0:T(8,128)S(1)} %broadcast_in_dim.40.ends, bf16[2,2,2,5488,128]{4,3,2,1,0:T(8,128)(2,1)} %bitcast.41, f32[5488,128]{1,0:T(8,128)S(1)} %bitcast.40), custom_call_target="tpu_custom_call" | custom-call | tf_op jit(solution)/shard_map/pallas_call | solution.py:1069
  449.9 0.0 copy-done.5
  449.9 0.0 copy-done.6
  449.9 0.0 copy-start.3
  449.9 1.1 copy-done.3
  451.1 0.6 copy-done.4
  451.7 12.6 %shard_map.156 = (f32[5488,128]{1,0:T(8,128)}, f32[5488,128]{1,0:T(8,128)}, f32[5488,128]{1,0:T(8,128)}, f32[5488,128]{1,0:T(8,128)}, f32[16,128]{1,0:T(8,128)}) custom-call(s32[1]{0:T(128)} %bitcast.15.base, f32[56,128]{1,0:T(8,128)} %copy-done.4, s32[16,128]{1,0:T(8,128)} %copy-done.5, s32[16,128]{1,0:T(8,128)} %copy-done.6, bf16[5488,128]{1,0:T(8,128)(2,1)} %copy-done.3, ...), custom_call_target="tpu_custom_call" | custom-call | bytes 21127172 | tf_op jit(solution)/shard_map/pallas_call | solution.py:1046
  464.3 6.2 %shard_map.157 = f32[16,128]{1,0:T(8,128)} custom-call(f32[16,128]{1,0:T(8,128)} %get-tuple-element.97.update_sq, f32[56,128]{1,0:T(8,128)} %copy-done.4), custom_call_target="tpu_custom_call" | custom-call | tf_op jit(solution)/shard_map/pallas_call | solution.py:1279
  470.5 0.6 reshape.109
  471.1 1.3 slice_reduce_fusion
  472.4 0.0 copy-start.1
  472.4 0.4 fusion.12
  472.8 0.8 fusion.9
  473.7 0.0 all-to-all-done.1
  473.7 3.4 copy.24
  (25 shorter events, 0.1 us)
Async XLA Ops:
  7.2 0.7 copy-start
  76.1 30.2 %all-to-all-start = ((bf16[32,64,512]{2,1,0:T(8,128)(2,1)}), bf16[32,64,512]{2,1,0:T(8,128)(2,1)S(1)}, u32[]{:S(2)}, u32[]{:S(2)}) async-start(bf16[32,64,512]{2,1,0:T(8,128)(2,1)} %bitcast.46), calls=%async_computation | async-start | bytes 4194304 | tf_op jit(solution)/shard_map/all_to_all | solution.py:1146
  79.7 289.7 %reduce-scatter.2.cloned.1.call-start = ((), (), s32[]{:S(2)}) async-start(), calls=%async_computation.3 | async-start | bytes 1179648 | tf_op jit(solution)/shard_map/reduce_scatter | solution.py:1220
  323.1 2.9 copy-start.7
  323.1 3.3 copy-start.8
  329.3 4.7 copy-start.13
  329.3 40.1 %copy-start.14 = (bf16[256,128]{1,0:T(8,128)(2,1)S(1)}, bf16[256,128]{1,0:T(8,128)(2,1)}, u32[]{:S(2)}) copy-start(bf16[256,128]{1,0:T(8,128)(2,1)} %get-tuple-element.87) | copy-start | bytes 196612
  329.3 42.7 %copy-start.10 = (bf16[512,256]{1,0:T(8,128)(2,1)S(1)}, bf16[512,256]{1,0:T(8,128)(2,1)}, u32[]{:S(2)}) copy-start(bf16[512,256]{1,0:T(8,128)(2,1)} %get-tuple-element.90) | copy-start | bytes 786436
  329.3 44.5 %copy-start.12 = (s32[16]{0:T(128)S(1)}, s32[16]{0:T(128)}, u32[]{:S(2)}) copy-start(s32[16]{0:T(128)} %constant.38.clone) | copy-start | bytes 196
  329.3 44.6 %copy-start.11 = (s32[16]{0:T(128)S(1)}, s32[16]{0:T(128)}, u32[]{:S(2)}) copy-start(s32[16]{0:T(128)} %constant.39.clone) | copy-start | bytes 196
  329.3 44.7 %copy-start.2 = (f32[702464]{0:T(1024)S(1)}, f32[702464]{0:T(1024)}, u32[]{:S(2)}) copy-start(f32[702464]{0:T(1024)} %param.12) | copy-start | bytes 8429572
  329.3 144.3 %all-to-all-start.1 = ((bf16[4,512,512]{2,0,1:T(4,128)(2,1)}), bf16[4,512,512]{2,0,1:T(4,128)(2,1)}, u32[]{:S(2)}, u32[]{:S(2)}) async-start(bf16[4,512,512]{2,0,1:T(4,128)(2,1)} %copy.23), calls=%async_computation.1 | async-start | bytes 4194304 | tf_op jit(solution)/shard_map/all_to_all | solution.py:1185
  373.9 76.0 %copy-start.5 = (s32[16,128]{1,0:T(8,128)}, s32[16,128]{1,0:T(8,128)S(1)}, u32[]{:S(2)}) copy-start(s32[16,128]{1,0:T(8,128)S(1)} %broadcast_in_dim.19.starts) | copy-start | bytes 24580
  374.0 75.9 %copy-start.6 = (s32[16,128]{1,0:T(8,128)}, s32[16,128]{1,0:T(8,128)S(1)}, u32[]{:S(2)}) copy-start(s32[16,128]{1,0:T(8,128)S(1)} %broadcast_in_dim.40.ends) | copy-start | bytes 24580
  449.9 1.1 copy-start.3
  451.1 0.6 copy-start.4
  451.7 20.8 %copy-start.9 = (f32[512,256]{1,0:T(8,128)S(1)}, f32[512,256]{1,0:T(8,128)}, u32[]{:S(2)}) copy-start(f32[512,256]{1,0:T(8,128)} %get-tuple-element.103) | copy-start | bytes 1572868
  472.4 4.7 copy-start.1
Sparse Core Ops, SparseCore 0:
  326.1 43.2 reduce-scatter.1
where the time goes:
time: 493 us; the launch traced here: 484 us
  Pallas kernels  377 us (76%)
  waiting for transfers between devices  61.9 us (13%)
  between operations  14.6 us (3%)
  local copies, waits for them, and re-layouts  13.8 us (3%)
  starting transfers between devices  8.29 us (2%)
  other arithmetic  5.15 us (1%)
    pallas_call x3, Pallas kernels, call(): pl.pallas_call(kernel, grid=(grid,), in_specs=in_specs, out_specs=list(ou...  227 us
    pallas_call x1, Pallas kernels, reduce_all(): pl.pallas_call(functools.partial(reduce_kernel, bias_owner, bias_row), ou...  75.9 us
    pallas_call x1, Pallas kernels, begin_all(): pl.pallas_call(functools.partial(begin_kernel, chunks), out_shape=[shaped...  67.5 us
    reduce_scatter x1, waiting for transfers between devices, body(): lax.psum_scatter(dkv_t.T.astype(BF), 'lat', scatter_dimension=0, tiled=True)  35.3 us
    all_to_all x1, waiting for transfers between devices, body(): lax.all_to_all(latent_grad[0], 'lat', split_axis=0, concat_axis=1, tiled=...  26.5 us
  transfers between devices with their start and end apart: 3, of which 2 were waited for; matrix products, arithmetic and copies ran while one was open for 2% of the time, Pallas kernels for 20%

commit v1 on v0

--- a/solution.py
+++ b/solution.py
@@ -100,15 +100,9 @@
 
 
 def gelu_pair(x):
-    size = jnp.abs(x)
-    t = pl.reciprocal(1.0 + (0.3275911 / math.sqrt(2.0)) * size, approx=True)
-    e = jnp.exp(x * x * -0.5)
-    poly = 0.5 * 1.061405429
-    for coef in (-1.453152027, 1.421413741, -0.284496736, 0.254829592):
-        poly = poly * t + 0.5 * coef
-    tail = poly * t * e
-    cdf = jnp.where(x >= 0.0, 1.0 - tail, tail)
-    return x * cdf, cdf + x * (e * (1.0 / math.sqrt(2.0 * math.pi)))
+    cdf = 0.5 + 0.5 * lax.erf(x * (1.0 / math.sqrt(2.0)))
+    density = jnp.exp(x * x * -0.5) * (1.0 / math.sqrt(2.0 * math.pi))
+    return x * cdf, cdf + x * density
 
 
 def accumulate(first, ref, value):
@@ -262,20 +256,22 @@
 
 class Reduction:
     lags = (0, 1, 3, 5, 7, 9, 11)
-
-    def __init__(self, place, grads, out, bufs, sems):
+    plane = 2
+
+    def __init__(self, place, shard, grads, out, bufs, sems):
         self.p = place
         self.grads = grads
         self.out = out
         self.own, self.rc, self.r1, self.r2, self.r3, self.r4, self.res = bufs
         self.own_sem, self.send, self.rc_sem, self.r1_sem, self.r2_sem, self.r3_sem, self.r4_sem, self.res_sem = sems
-        self.shard = grads.shape[3]
-        self.batches = pl.cdiv(self.shard, BATCH)
-        self.back = self.batches * BATCH - self.shard
+        self.shard = shard
+        self.full = pl.cdiv(shard, BATCH)
+        self.batches = self.full + self.plane
+        self.back = self.full * BATCH - shard
 
     @staticmethod
     def scratch(shard):
-        n = pl.cdiv(shard, BATCH)
+        n = pl.cdiv(shard, BATCH) + Reduction.plane
         bufs = [
             pltpu.VMEM((2, 2, 2, BATCH, LANES), BF),
             pltpu.VMEM((n, 2, 2, BATCH, LANES), BF),
@@ -290,7 +286,12 @@
         return bufs + sems
 
     def row(self, i):
-        return pl.multiple_of(i * BATCH - (i // (self.batches - 1)) * self.back, 16)
+        p, n, held = i - self.plane, self.full, flat_rows_of()["tok_norm"] // BATCH
+        late = p // (n - 4)
+        b = (1 - late) * lax.rem(p + held + 4, n) + late * (held + lax.rem(p - (n - 4) + 2, 4))
+        main = (i + n) // (n + self.plane)
+        row = (1 - main) * (self.shard + i * BATCH) + main * (b * BATCH - (b // (n - 1)) * self.back)
+        return pl.multiple_of(row, 16)
 
     def own_copy(self, i):
         slot = lax.rem(i, 2)
@@ -329,7 +330,7 @@
         ]
 
     def launch(self, stage, i):
-        @pl.when(i >= 4)
+        @pl.when(i >= (4 if stage < 3 else 4 + self.plane))
         def _():
             for copy in self.copies(stage, i - 4):
                 copy.wait_send()
@@ -368,14 +369,16 @@
         else:
             self.landed(5, i)
             self.out[pl.ds(self.row(i), BATCH), :] = self.res[i]
-        if stage < 6:
+        if stage == 3:
+            pl.when(i >= self.plane)(lambda: self.launch(stage, i))
+        elif stage < 6:
             self.launch(stage, i)
 
     def tick(self, t):
         for stage, lag in enumerate(self.lags):
             i = t - lag
 
-            @pl.when((i >= 0) & (i < self.batches))
+            @pl.when((i >= (0 if stage < 4 else self.plane)) & (i < self.batches))
             def _(stage=stage, i=i):
                 self.work(stage, i)
 
@@ -407,13 +410,44 @@
 STAT_ROWS = 56
 
 
-def reduce_kernel(bias_owner, bias_at, starts, ends, grads, master, summed, stats, *scratch):
+def token_backward(grad_kv, tokens, tok_normed, w_kv, tok_norm, token_grad, kv_grad, edge):
+    kv_grad[...] = t_mm(tok_normed[...], grad_kv).astype(BF)
+    grad = mm_t(grad_kv, w_kv[...])
+    xhat, rstd = norm_stats(tokens[...].astype(F32))
+    token_grad[...] = norm_back(grad, xhat, rstd, tok_norm[0:1, :]).astype(BF)
+    gain, bias = col_sum(grad * xhat), col_sum(grad)
+    parts = [half[:, j * LANES : (j + 1) * LANES] for half in (gain, bias) for j in range(DIN // LANES)]
+    keep = edge.shape[0] - len(parts)
+    edge[...] = jnp.concatenate([edge[...].astype(F32)[0:keep, :]] + parts, axis=0).astype(BF)
+
+
+def reduce_kernel(
+    bias_owner, bias_at, starts, ends, unused_flat, master, tokens, tok_normed, w_kv, tok_norm,
+    summed, stats, token_grad, grads, *scratch,
+):
     place = Place()
-    block, block_send, block_recv = scratch[:3]
-    red = Reduction(place, grads, summed, scratch[3:10], scratch[10:])
+    block, block_send, block_recv, edge, kv_grad, edge_sem = scratch[:6]
+    shard = master.shape[0]
+    red = Reduction(place, shard, grads, summed, scratch[6:13], scratch[13:])
     greet([place.lat_other(d) for d in range(1, 8)] + [place.z_other(d) for d in (1, 2, 3)])
-    lax.fori_loop(0, red.ticks(), lambda t, c: (red.tick(t), c)[1], 0)
-    shard = master.shape[0]
+    at = flat_rows_of()
+    edge_rows = grads.at[0, 0, 0, pl.ds(at["tok_norm"] // 16 * 16, 16), :]
+    fetch = pltpu.make_async_copy(edge_rows, edge, edge_sem.at[0])
+    fetch.start()
+    ready = red.lags[3] + red.plane
+    lax.fori_loop(0, ready, lambda t, c: (red.tick(t), c)[1], 0)
+    fetch.wait()
+    grad_kv = jnp.concatenate([red.r2[i, h] for i in range(red.plane) for h in range(2)], axis=0)
+    token_backward(grad_kv, tokens, tok_normed, w_kv, tok_norm, token_grad, kv_grad, edge)
+    writes = [
+        pltpu.make_async_copy(edge, edge_rows, edge_sem.at[0]),
+        pltpu.make_async_copy(kv_grad, grads.at[0, 0, 0, pl.ds(at["w_kv"], DIN), :], edge_sem.at[1]),
+    ]
+    for copy in writes:
+        copy.start()
+    for copy in writes:
+        copy.wait()
+    lax.fori_loop(ready, red.ticks(), lambda t, c: (red.tick(t), c)[1], 0)
     step = 784
     grad_sq = jnp.zeros((1, LANES), F32)
     weight_sq = jnp.zeros((16, LANES), F32)
@@ -580,7 +614,7 @@
     latent, norms, hid_bias, out_bias, w_q, w_o, w_kv, tok_norm, tok_normed, episode, rank, counts,
     kvf_out, co_out, lse_out, h1,
     whole, stage, all_ids, keys, m_up_one, m_down_one, m_qkv, m_so, m_up_two, m_down_two,
-    send, recv, key_send, key_recv, id_send, id_recv, out_sem,
+    episodes_held, send, recv, key_send, key_recv, id_send, id_recv, out_sem,
 ):
     place = Place()
     shard = master.shape[0]
@@ -659,32 +693,34 @@
     exchange.step(3)
     relayout(whole, 0, stage, latent, LAT, D)
 
-    tick = 12
     chunk = 8 * LANES
-    for f in range(frames):
-        start = latent[...].astype(F32) + episode_rows[f : f + 1, :]
-        episode[f] = episode_rows[f : f + 1, :]
-        kvf = jnp.zeros((cap, LANES), F32)
-        for j in range(n // 8):
-            sel = select_tokens(rank[f, 8 * j : 8 * j + 8, :], cap)
-            rows = keys[2 * j : 2 * j + 2].reshape(chunk, LANES)
-            kvf = kvf + mm(sel, rows)
-        kvf = kvf.astype(BF)
-        if tick < gather.ticks():
-            gather.tick(tick)
-            tick += 1
+    episodes_held[...] = episode_rows[0:8, :]
+
+    def attend(f, carry):
+        for tick in range(12, gather.ticks()):
+
+            @pl.when(f == (tick - 12) * frames // (gather.ticks() - 12))
+            def _(tick=tick):
+                gather.tick(tick)
+
+        row = episodes_held[pl.ds(f, 1), :]
+        start = latent[...].astype(F32) + row
+        episode[pl.ds(f, 1)] = row[None]
+
+        def pick(j, acc):
+            sel = select_tokens(rank[f, pl.ds(pl.multiple_of(8 * j, 8), 8), :], cap)
+            return acc + mm(sel, keys[pl.ds(2 * j, 2)].reshape(chunk, LANES))
+
+        kvf = lax.fori_loop(0, n // 8, pick, jnp.zeros((cap, LANES), F32)).astype(BF)
         co, lse = cross_attend(start, norms, w_q, kvf, counts[f, 0:1, 0:1])
-        rows = slice(f * LAT, (f + 1) * LAT)
+        rows = pl.ds(pl.multiple_of(f * LAT, LAT), LAT)
         h1[rows, :] = start + mm(co, w_o[...]) + out_bias[0:1, :]
         kvf_out[f] = kvf
         co_out[rows, :] = co
         lse_out[f] = lse
-        if tick < gather.ticks():
-            gather.tick(tick)
-            tick += 1
-    while tick < gather.ticks():
-        gather.tick(tick)
-        tick += 1
+        return carry
+
+    lax.fori_loop(0, frames, attend, 0)
 
     big = (
         (up_one, m_up_one, at["w_up"], D, FF),
@@ -747,6 +783,7 @@
         ]
         + [pltpu.VMEM(m, BF) for m in matrices]
         + [
+            pltpu.VMEM((8, D), F32),
             dma((7, len(chunks))), dma((7, len(chunks))), dma((8,)), dma((8,)), dma((7,)), dma((7,)), dma((6,)),
         ],
         compiler_params=pltpu.CompilerParams(
@@ -772,36 +809,47 @@
     return stage[0 : rows * wide, :]
 
 
-def feed_forward(rows, gain, bias, up_bias, down_bias, w_up, w_down, act_ref, slope_ref):
+def chunk_of(c, size=FCHUNK):
+    return pl.ds(pl.multiple_of(c * size, LANES), size)
+
+
+def feed_forward(rows, gain, bias, up_bias, down_bias, w_up, w_down, act_ref, slope_ref, normed_ref, total_ref):
     xhat, rstd = norm_stats(rows)
-    normed = (xhat * gain + bias).astype(BF)
-    total = rows + down_bias
-    for c in range(FF // FCHUNK):
-        at = slice(c * FCHUNK, (c + 1) * FCHUNK)
-        act, slope = gelu_pair(mm(normed, w_up[:, at]) + up_bias[:, at])
+    normed_ref[...] = (xhat * gain + bias).astype(BF)
+    total_ref[...] = rows + down_bias
+
+    def step(c, carry):
+        at = chunk_of(c)
+        act, slope = gelu_pair(mm(normed_ref[...], w_up[:, at]) + up_bias[:, at])
         act = act.astype(BF)
         act_ref[:, at] = act
         slope_ref[:, at] = slope.astype(BF)
-        total = total + mm(act, w_down[at, :])
-    return total, normed, xhat, rstd
-
-
-def feed_back(grad_low, grad_rows, normed, xhat, rstd, gain, act, slope, w_up, w_down, acc_up, acc_down, dhid, dnorm, dout):
-    grad_normed = jnp.zeros(grad_rows.shape, F32)
-    normed_t = normed.T
-    for c in range(FF // FCHUNK):
-        at = slice(c * FCHUNK, (c + 1) * FCHUNK)
-        dpre = (mm_t(grad_low, w_down[at, :]) * slope[:, at].astype(F32)).astype(BF)
+        total_ref[...] += mm(act, w_down[at, :])
+        return carry
+
+    lax.fori_loop(0, FF // FCHUNK, step, 0)
+
+
+def feed_back(grad_ref, normed_ref, xhat, rstd, gain, act, slope, w_up, w_down, acc_up, acc_down, dhid, dnorm, dout, work):
+    work[...] = jnp.zeros(work.shape, F32)
+
+    def step(c, carry):
+        at = chunk_of(c)
+        dpre = (mm_t(grad_ref[...], w_down[at, :]) * slope[:, at].astype(F32)).astype(BF)
         dhid[:, at] += col_sum(dpre.astype(F32))
-        grad_normed = grad_normed + mm_t(dpre, w_up[:, at])
-        part = mm(normed_t, dpre)
+        work[...] += mm_t(dpre, w_up[:, at])
+        part = t_mm(normed_ref[...], dpre)
         for j in range(FCHUNK // LANES):
             rows = pl.ds(c * (FCHUNK // LANES) + j, D, stride=FF // LANES)
             acc_up[rows, :] = acc_up[rows, :] + part[:, j * LANES : (j + 1) * LANES]
-        add_flat(acc_down, c * FCHUNK * (D // LANES), mm(act[:, at].T, grad_low))
+        add_flat(acc_down, c * FCHUNK * (D // LANES), t_mm(act[:, at], grad_ref[...]))
+        return carry
+
+    lax.fori_loop(0, FF // FCHUNK, step, 0)
+    grad_normed = work[...]
     dnorm[...] += jnp.concatenate([col_sum(grad_normed * xhat), col_sum(grad_normed)], axis=0)
-    dout[...] += col_sum(grad_low.astype(F32))
-    return grad_rows + norm_back(grad_normed, xhat, rstd, gain)
+    dout[...] += col_sum(grad_ref[...].astype(F32))
+    return norm_back(grad_normed, xhat, rstd, gain)
 
 
 def clear(first, refs):
@@ -811,82 +859,174 @@
             ref[...] = jnp.zeros_like(ref)
 
 
-def write_flat(flat, low, pieces, sems):
-    copies = []
+def flat_spans(row, count, shard, extra):
+    spans, done = [], 0
+    while done < count:
+        part = min(count - done, shard - (row + done) % shard)
+        spans.append((done, part, row + done + (row + done) // shard * extra))
+        done += part
+    return spans
+
+
+def write_flat(flat, low, pieces, sems, shard, extra):
+    pending = {}
     for j, (acc, row) in enumerate(pieces):
         count = acc.shape[0]
         slot = j % 2
-        if j >= 2:
-            copies[j - 2].wait()
+        for copy in pending.get(slot, []):
+            copy.wait()
         low[slot, 0:count, :] = acc[...].astype(BF)
-        copies.append(
-            pltpu.make_async_copy(low.at[slot, pl.ds(0, count), :], flat.at[pl.ds(row, count), :], sems.at[slot])
-        )
-        copies[-1].start()
-    for copy in copies[-2:]:
-        copy.wait()
+        pending[slot] = [
+            pltpu.make_async_copy(low.at[slot, pl.ds(off, part), :], flat.at[pl.ds(at, part), :], sems.at[slot, k])
+            for k, (off, part, at) in enumerate(flat_spans(row, count, shard, extra))
+        ]
+        for copy in pending[slot]:
+            copy.start()
+    for copies in pending.values():
+        for copy in copies:
+            copy.wait()
+
+
+class FrameExchange:
+    def __init__(self, place, source, grad, held, result, sems):
+        self.p, self.source, self.grad, self.held, self.result = place, source, grad, held, result
+        self.in_send, self.in_recv, self.out_send, self.out_recv, self.own_in, self.own_out = sems
+        self.frames, self.rows = grad.shape[0], source.shape[1]
+
+    @staticmethod
+    def scratch(frames):
+        dma = pltpu.SemaphoreType.DMA
+        return [dma((frames, 7))] * 4 + [dma((frames,))] * 2
+
+    def block(self, index):
+        return pl.ds(pl.multiple_of(index * self.rows, 16), self.rows)
+
+    def arriving(self, f, d):
+        target = self.p.lat_other(d)
+        src = self.source.at[target[1] * self.frames + f]
+        dst = self.grad.at[f, self.block(self.p.me), :]
+        return remote(src, dst, self.in_send.at[f, d - 1], self.in_recv.at[f, d - 1], target)
+
+    def own_arriving(self, f):
+        src = self.source.at[self.p.me * self.frames + f]
+        return pltpu.make_async_copy(src, self.grad.at[f, self.block(self.p.me), :], self.own_in.at[f])
+
+    def leaving(self, f, d):
+        target = self.p.lat_other(d)
+        src = self.held.at[f, self.block(target[1]), :]
+        dst = self.result.at[self.p.me * self.frames + f]
+        return remote(src, dst, self.out_send.at[f, d - 1], self.out_recv.at[f, d - 1], target)
+
+    def own_leaving(self, f):
+        dst = self.result.at[self.p.me * self.frames + f]
+        return pltpu.make_async_copy(self.held.at[f, self.block(self.p.me), :], dst, self.own_out.at[f])
+
+    def begin(self):
+        greet([self.p.lat_other(d) for d in range(1, 8)])
+        for f in range(self.frames):
+            self.own_arriving(f).start()
+            for d in range(1, 8):
+                self.arriving(f, d).start()
+
+    def await_frame(self, f):
+        self.own_arriving(f).wait()
+        for d in range(1, 8):
+            self.arriving(f, d).wait_recv()
+
+    def send_frame(self, f):
+        self.own_leaving(f).start()
+        for d in range(1, 8):
+            self.leaving(f, d).start()
+
+    def finish(self):
+        def step(f, carry):
+            self.own_leaving(f).wait()
+            for d in range(1, 8):
+                self.arriving(f, d).wait_send()
+                self.leaving(f, d).wait()
+            return carry
+
+        lax.fori_loop(0, self.frames, step, 0)
 
 
 def forward_kernel(
-    h1, grad, norms, hid_bias, out_bias, up_one, down_one, w_qkv, w_so, up_two, down_two,
+    reach, shard, extra, h1, grad, norms, hid_bias, out_bias, up_one, down_one, w_qkv, w_so, up_two, down_two,
     h2_out, qkv, lse_out, mixed_out, act_one, slope_one, latents, g3, dhid, dnorm, dout, flat,
-    act_two, slope_two, acc_up, acc_down, low, sems,
+    act_two, slope_two, acc_up, acc_down, low, normed, mixed_t, work, sems, *shared,
 ):
     step = pl.program_id(0)
+    if reach:
+        place = Place()
+        traffic = FrameExchange(place, grad, shared[0], shared[1], latents, shared[2:])
+        pl.when(step == 0)(traffic.begin)
+        grad = shared[0].at[step]
     clear(step == 0, (acc_up, acc_down, dhid, dnorm, dout))
-    h2, unused, unused, unused = feed_forward(
-        h1[...], norms[2:3, :], norms[3:4, :], hid_bias[0:1, :], out_bias[1:2, :], up_one, down_one, act_one, slope_one
+    feed_forward(
+        h1[...], norms[2:3, :], norms[3:4, :], hid_bias.at[0:1], out_bias[1:2, :], up_one, down_one, act_one,
+        slope_one, normed, h2_out,
     )
-    h2_out[...] = h2
-    xhat, unused = norm_stats(h2)
-    sa_in = (xhat * norms[4:5, :] + norms[5:6, :]).astype(BF)
-    for c in range(3):
-        at = slice(c * D, (c + 1) * D)
-        qkv[:, at] = mm(sa_in, w_qkv[:, at]).astype(BF)
-
+    xhat, unused = norm_stats(h2_out[...])
+    normed[...] = (xhat * norms[4:5, :] + norms[5:6, :]).astype(BF)
+
+    def project(c, carry):
+        at = chunk_of(c)
+        qkv[:, at] = mm(normed[...], w_qkv[:, at]).astype(BF)
+        return carry
+
+    lax.fori_loop(0, 3, project, 0)
     scale = jnp.asarray(0.125, BF)
-    mixed_rows = []
-    for pair in range(HEADS // 2):
-        base = pair * LANES
-        query_pair = qkv[:, base : base + LANES] * scale
-        key_pair = qkv[:, D + base : D + base + LANES]
-        value_t = qkv[:, 2 * D + base : 2 * D + base + LANES].T
+
+    def attend(pair, carry):
+        query_pair = qkv[:, chunk_of(pair, LANES)] * scale
+        key_pair = qkv[:, chunk_of(pair + D // LANES, LANES)]
+        value_t = qkv[:, chunk_of(pair + 2 * D // LANES, LANES)].T
         for half in range(2):
             scores = mm_t(key_pair, keep_half(query_pair, half))
             top = jnp.max(scores, axis=0, keepdims=True)
             terms = jnp.exp(scores - top)
             total = jnp.sum(terms, axis=0, keepdims=True)
             prob = (terms * (1.0 / total)).astype(BF)
-            head = 2 * pair + half
-            lse_out[0, head : head + 1, :] = top + jnp.log(total)
-            mixed_rows.append(mm(value_t[half * 64 : half * 64 + 64, :], prob))
-    mixed = jnp.concatenate(mixed_rows, axis=0).T.astype(BF)
+            lse_out[0, pl.ds(2 * pair + half, 1), :] = top + jnp.log(total)
+            at = pl.ds(pl.multiple_of(pair * LANES + half * HEAD_DIM, HEAD_DIM), HEAD_DIM)
+            mixed_t[at, :] = mm(value_t[half * HEAD_DIM : (half + 1) * HEAD_DIM, :], prob)
+        return carry
+
+    lax.fori_loop(0, HEADS // 2, attend, 0)
+    mixed = mixed_t[...].T.astype(BF)
     mixed_out[...] = mixed
-    h3 = h2 + mm(mixed, w_so[...]) + out_bias[2:3, :]
-
-    total, normed, xhat, rstd = feed_forward(
-        h3, norms[6:7, :], norms[7:8, :], hid_bias[1:2, :], out_bias[3:4, :], up_two, down_two, act_two, slope_two
+    h3 = h2_out[...] + mm(mixed, w_so[...]) + out_bias[2:3, :]
+    feed_forward(
+        h3, norms[6:7, :], norms[7:8, :], hid_bias.at[1:2], out_bias[3:4, :], up_two, down_two, act_two, slope_two,
+        normed, work,
     )
-    latents[...] = total.astype(BF)
-    grad_low = grad[...]
-    g3[...] = feed_back(
-        grad_low, grad_low.astype(F32), normed, xhat, rstd, norms[6:7, :], act_two, slope_two, up_two, down_two,
-        acc_up, acc_down, dhid, dnorm, dout,
+    if reach:
+        shared[1][step] = work[...].astype(BF)
+        traffic.send_frame(step)
+        traffic.await_frame(step)
+    else:
+        latents[...] = work[...].astype(BF)
+    xhat, rstd = norm_stats(h3)
+    g3[...] = grad[...].astype(F32) + feed_back(
+        grad, normed, xhat, rstd, norms[6:7, :], act_two, slope_two, up_two, down_two,
+        acc_up, acc_down, dhid, dnorm, dout, work,
     )
 
     @pl.when(step == pl.num_programs(0) - 1)
     def _():
         at = flat_rows_of()
         half = D * FF // LANES
-        write_flat(flat, low, [(acc_up, at["w_up"] + half), (acc_down, at["w_down"] + half)], sems)
+        write_flat(flat, low, [(acc_up, at["w_up"] + half), (acc_down, at["w_down"] + half)], sems, shard, extra)
+        if reach:
+            traffic.finish()
 
 
 def backward_kernel(
-    qkv, lse, mixed, g3, h2, h1, act_one, slope_one, kvf_in, co_in, cross_lse, rank, count, episode, hot,
+    shard, extra, kv_rows, qkv, lse, mixed, g3, h2, h1, act_one, slope_one, kvf_in, co_in, cross_lse, rank, count, episode, hot,
     latent, norms, w_so, w_qkv, up_one, down_one, w_q, w_o, dhid_two, dnorm_two, dout_two, flat_in,
-    dkv_t, flat,
+    flat,
     dqkv, acc_up, acc_down, acc_qkv, acc_so, acc_latent, acc_q, acc_o, acc_episode,
-    dhid, dnorm_sa, dnorm_one, dnorm_cross, dout_so, dout_one, dout_cross, stage, low, sems,
+    dhid, dnorm_sa, dnorm_one, dnorm_cross, dout_so, dout_one, dout_cross, stage, low, normed, grad_mixed, grad_low,
+    work, dkv_t, sems,
 ):
     step = pl.program_id(0)
     clear(
@@ -898,49 +1038,62 @@
     )
     scale = jnp.asarray(0.125, BF)
     grad_three = g3[...]
-    grad_low = grad_three.astype(BF)
-    dout_so[...] += col_sum(grad_low.astype(F32))
-    add_flat(acc_so, 0, t_mm(mixed[...], grad_low))
-    grad_mixed = mm_t(grad_low, w_so[...]).astype(BF)
-    for pair in range(HEADS // 2):
-        base = pair * LANES
-        query_pair = qkv[:, base : base + LANES] * scale
-        key_pair = qkv[:, D + base : D + base + LANES]
-        value_pair = qkv[:, 2 * D + base : 2 * D + base + LANES]
-        grad_pair = grad_mixed[:, base : base + LANES]
+    grad_low[...] = grad_three.astype(BF)
+    dout_so[...] += col_sum(grad_low[...].astype(F32))
+    add_flat(acc_so, 0, t_mm(mixed[...], grad_low[...]))
+    grad_mixed[...] = mm_t(grad_low[...], w_so[...]).astype(BF)
+
+    def attend(pair, carry):
+        query_at = chunk_of(pair, LANES)
+        key_at = chunk_of(pair + D // LANES, LANES)
+        value_at = chunk_of(pair + 2 * D // LANES, LANES)
+        query_pair = qkv[:, query_at] * scale
+        key_pair = qkv[:, key_at]
+        value_pair = qkv[:, value_at]
+        grad_pair = grad_mixed[:, query_at]
         key_t = key_pair.T
         query_t = []
         grad_key = jnp.zeros((LAT, LANES), F32)
         grad_value = jnp.zeros((LAT, LANES), F32)
         for half in range(2):
-            head = 2 * pair + half
             query = keep_half(query_pair, half)
             grad_head = keep_half(grad_pair, half)
-            prob = jnp.exp(mm_t(key_pair, query) - lse[0, head : head + 1, :])
+            prob = jnp.exp(mm_t(key_pair, query) - lse[0, pl.ds(2 * pair + half, 1), :])
             grad_value = grad_value + mm(prob.astype(BF), grad_head)
             weighted = prob * mm_t(value_pair, grad_head)
             grad_score = (weighted - prob * col_sum(weighted)).astype(BF)
             grad_key = grad_key + mm(grad_score, query)
-            query_t.append(mm(key_t[half * 64 : half * 64 + 64, :], grad_score))
-        dqkv[:, base : base + LANES] = (jnp.concatenate(query_t, axis=0).T * 0.125).astype(BF)
-        dqkv[:, D + base : D + base + LANES] = grad_key.astype(BF)
-        dqkv[:, 2 * D + base : 2 * D + base + LANES] = grad_value.astype(BF)
-    grad_in = mm_t(dqkv[...], w_qkv[...])
+            query_t.append(mm(key_t[half * HEAD_DIM : (half + 1) * HEAD_DIM, :], grad_score))
+        dqkv[:, query_at] = (jnp.concatenate(query_t, axis=0).T * 0.125).astype(BF)
+        dqkv[:, key_at] = grad_key.astype(BF)
+        dqkv[:, value_at] = grad_value.astype(BF)
+        return carry
+
+    lax.fori_loop(0, HEADS // 2, attend, 0)
     xhat, rstd = norm_stats(h2[...])
-    sa_t = (xhat * norms[4:5, :] + norms[5:6, :]).astype(BF).T
-    for c in range(3):
-        part = mm(sa_t, dqkv[:, c * D : (c + 1) * D])
+    normed[...] = (xhat * norms[4:5, :] + norms[5:6, :]).astype(BF)
+    work[...] = jnp.zeros(work.shape, F32)
+
+    def project(c, carry):
+        at = chunk_of(c)
+        work[...] += mm_t(dqkv[:, at], w_qkv[:, at])
+        part = t_mm(normed[...], dqkv[:, at])
         for j in range(D // LANES):
             rows = pl.ds(c * (D // LANES) + j, D, stride=3 * D // LANES)
             acc_qkv[rows, :] = acc_qkv[rows, :] + part[:, j * LANES : (j + 1) * LANES]
+        return carry
+
+    lax.fori_loop(0, 3, project, 0)
+    grad_in = work[...]
     dnorm_sa[...] += jnp.concatenate([col_sum(grad_in * xhat), col_sum(grad_in)], axis=0)
     grad_two = grad_three + norm_back(grad_in, xhat, rstd, norms[4:5, :])
 
     xhat, rstd = norm_stats(h1[...])
-    normed = (xhat * norms[2:3, :] + norms[3:4, :]).astype(BF)
-    grad_one = feed_back(
-        grad_two.astype(BF), grad_two, normed, xhat, rstd, norms[2:3, :], act_one, slope_one, up_one, down_one,
-        acc_up, acc_down, dhid, dnorm_one, dout_one,
+    normed[...] = (xhat * norms[2:3, :] + norms[3:4, :]).astype(BF)
+    grad_low[...] = grad_two.astype(BF)
+    grad_one = grad_two + feed_back(
+        grad_low, normed, xhat, rstd, norms[2:3, :], act_one, slope_one, up_one, down_one,
+        acc_up, acc_down, dhid, dnorm_one, dout_one, work,
     )
 
     cap = kvf_in.shape[1]
@@ -970,7 +1123,8 @@
 
     def scatter(j, carry):
         sel = select_tokens(rank[0, pl.ds(pl.multiple_of(j * 8, 8), 8), :], cap)
-        dkv_t[:, pl.ds(pl.multiple_of(j * chunk, chunk), chunk)] += mm(grad_kv_t, sel)
+        at = pl.ds(pl.multiple_of(j * chunk, chunk), chunk)
+        dkv_t[:, at] = added(dkv_t[:, at], mm(grad_kv_t, sel))
         return carry
 
     lax.fori_loop(0, dkv_t.shape[1] // chunk, scatter, 0)
@@ -984,7 +1138,7 @@
                 (acc_up, at["w_up"]), (acc_down, at["w_down"]), (acc_qkv, at["w_qkv"]), (acc_so, at["w_so"]),
                 (acc_latent, 0),
             ],
-            sems,
+            sems, shard, extra,
         )
         small = at["w_qkv"] - at["w_q"]
         first = at["w_q"] - at["episode"]
@@ -1005,18 +1159,31 @@
         out_rows = 4 * D // LANES
         low[1, hid.shape[0] : hid.shape[0] + out_rows, :] = to_flat(stage, outs).astype(BF)
         total = hid.shape[0] + out_rows
-        copies = [
-            pltpu.make_async_copy(
-                low.at[0, pl.ds(0, first + small), :], flat.at[pl.ds(at["episode"], first + small), :], sems.at[0]
-            ),
-            pltpu.make_async_copy(
-                low.at[1, pl.ds(0, total), :], flat.at[pl.ds(at["hid_bias"], total), :], sems.at[1]
-            ),
-        ]
+        copies = []
+        for slot, row, count in ((0, at["episode"], first + small), (1, at["hid_bias"], total)):
+            for k, (off, part, to) in enumerate(flat_spans(row, count, shard, extra)):
+                copies.append(
+                    pltpu.make_async_copy(
+                        low.at[slot, pl.ds(off, part), :], flat.at[pl.ds(to, part), :], sems.at[slot, k]
+                    )
+                )
         for copy in copies:
             copy.start()
         for copy in copies:
             copy.wait()
+        tokens = kv_rows[1]
+        for group in range(0, dkv_t.shape[1] // tokens, 16):
+            copies = []
+            for j in range(min(16, dkv_t.shape[1] // tokens - group)):
+                rows = pl.ds(j * tokens, tokens)
+                low[0, rows, :] = dkv_t[:, (group + j) * tokens : (group + j + 1) * tokens].T
+                to = kv_rows[0] + (group + j) * kv_rows[2]
+                copies.append(
+                    pltpu.make_async_copy(low.at[0, rows, :], flat.at[pl.ds(to, tokens), :], sems.at[0, j])
+                )
+                copies[-1].start()
+            for copy in copies:
+                copy.wait()
 
 
 def fixed(*shape):
@@ -1039,7 +1206,7 @@
     return jax.ShapeDtypeStruct(shape, dtype)
 
 
-def call(kernel, grid, in_specs, outs, args, flops=0, trans=0, scratch=(), limit=56, aliases=None):
+def call(kernel, grid, in_specs, outs, args, flops=0, trans=0, scratch=(), limit=56, aliases=None, collective=None):
     out_specs, out_shapes = zip(*outs)
     moved = sum(math.prod(a.shape) * a.dtype.itemsize for a in args)
     moved += sum(math.prod(s.shape) * s.dtype.itemsize for s in out_shapes)
@@ -1052,30 +1219,39 @@
         scratch_shapes=list(scratch),
         input_output_aliases=aliases or {},
         compiler_params=pltpu.CompilerParams(
-            dimension_semantics=("arbitrary",), vmem_limit_bytes=limit * MIB
+            dimension_semantics=("arbitrary",),
+            vmem_limit_bytes=limit * MIB,
+            collective_id=collective,
+            has_side_effects=collective is not None,
         ),
         cost_estimate=pl.CostEstimate(flops=flops, bytes_accessed=moved, transcendentals=trans),
     )(*args)
 
 
-def reduce_all(local_flat, master_rows, starts, ends, bias_owner, bias_row):
+def reduce_all(flat, master_rows, starts, ends, bias_owner, bias_row, tokens, tok_normed, w_kv, tok_norm):
     shard = master_rows.shape[0]
     vmem = pl.BlockSpec(memory_space=pltpu.VMEM)
-    block = [
-        pltpu.VMEM((8, STAT_ROWS, LANES), F32),
-        pltpu.SemaphoreType.DMA((7,)),
-        pltpu.SemaphoreType.DMA((7,)),
+    anywhere = pl.BlockSpec(memory_space=pl.ANY)
+    dma = pltpu.SemaphoreType.DMA
+    first = [
+        pltpu.VMEM((8, STAT_ROWS, LANES), F32), dma((7,)), dma((7,)), pltpu.VMEM((16, LANES), BF),
+        pltpu.VMEM((DIN, LANES), BF), dma((2,)),
     ]
+    grads = flat.reshape(2, 2, 2, -1, LANES)
     return pl.pallas_call(
         functools.partial(reduce_kernel, bias_owner, bias_row),
-        out_shape=[shaped((shard, LANES), BF), shaped((STAT_ROWS, LANES))],
-        in_specs=[vmem, vmem, pl.BlockSpec(memory_space=pl.ANY), vmem],
-        out_specs=[vmem, vmem],
-        scratch_shapes=block + Reduction.scratch(shard),
+        out_shape=[
+            shaped((shard, LANES), BF), shaped((STAT_ROWS, LANES)), shaped(tokens.shape, BF),
+            shaped(grads.shape, BF),
+        ],
+        in_specs=[vmem, vmem, anywhere] + [vmem] * 5,
+        out_specs=[vmem, vmem, vmem, anywhere],
+        scratch_shapes=first + Reduction.scratch(shard),
+        input_output_aliases={2: 3},
         compiler_params=pltpu.CompilerParams(
             collective_id=1, has_side_effects=True, vmem_limit_bytes=48 * MIB
         ),
-    )(starts, ends, local_flat.reshape(2, 2, 2, shard, LANES), master_rows)
+    )(starts, ends, grads, master_rows, tokens, tok_normed, w_kv, tok_norm)
 
 
 def body(tokens, frame_ids, episodes, master, moment_one, moment_two, latent_grad):
@@ -1104,7 +1280,6 @@
             latent, norms, hid_bias, out_bias, w_q, w_o, w_kv, tok_norm, tok_normed, episode_rows, rank, counts,
             kvf, cross_out, cross_lse, h1,
         ) = begin_all(master_rows, tokens[0], frame_ids.reshape(-1, LANES), hot, frames, cap)
-        latent_grad, h1 = lax.optimization_barrier((latent_grad, h1))
     else:
         weights = split_flat(lax.all_gather(master.astype(BF), "lat", axis=0, tiled=True))
         norms = weights["lat_norms"].astype(F32)
@@ -1143,20 +1318,33 @@
             flops=2 * score_flops + select_flops,
             trans=rows_total * cap,
         )
-    grad_rows_in = lax.all_to_all(
-        latent_grad[0], "lat", split_axis=0, concat_axis=1, tiled=True
-    ).reshape(rows_total, D)
-
     mlp_flops = 4 * rows_total * D * FF
     attn_flops = 4 * rows_total * LAT * D
-    flat_shape = (NPARAM // LANES, LANES)
     anywhere = pl.BlockSpec(memory_space=pl.ANY)
+    token_count = frame_ids.shape[1]
+    if reach:
+        flat_shard, extra = shard_rows, token_count
+        flat_shape = (lat_count * (shard_rows + extra), LANES)
+        kv_rows = (shard_rows, token_count, shard_rows + extra)
+        grad_in, grad_spec = latent_grad[0], anywhere
+        latents_spec = (anywhere, shaped(latent_grad.shape[1:], BF))
+        shared = [pltpu.VMEM((frames, LAT, D), BF)] * 2 + FrameExchange.scratch(frames)
+    else:
+        flat_shard, extra = NPARAM // LANES, 0
+        flat_shape = (flat_shard + total_keys, LANES)
+        kv_rows = (flat_shard, 512, 512)
+        grad_in = lax.all_to_all(
+            latent_grad[0], "lat", split_axis=0, concat_axis=1, tiled=True
+        ).reshape(rows_total, D)
+        grad_spec = rowed(LAT, D)
+        latents_spec = (rowed(LAT, D), shaped((rows_total, D), BF))
+        shared = []
     slab = D * FF // LANES
     h2, qkv, self_lse, mixed, act_one, slope_one, latents, g3, dhid_two, dnorm_two, dout_two, flat = call(
-        forward_kernel,
+        functools.partial(forward_kernel, reach, flat_shard, extra),
         frames,
         [
-            rowed(LAT, D), rowed(LAT, D), fixed(8, D), fixed(2, FF), fixed(4, D), fixed(D, FF), fixed(FF, D),
+            rowed(LAT, D), grad_spec, fixed(8, D), fixed(2, FF), fixed(4, D), fixed(D, FF), fixed(FF, D),
             fixed(D, 3 * D), fixed(D, D), fixed(D, FF), fixed(FF, D),
         ],
         [
@@ -1166,30 +1354,36 @@
             (rowed(LAT, D), shaped((rows_total, D), BF)),
             (rowed(LAT, FF), shaped((rows_total, FF), BF)),
             (rowed(LAT, FF), shaped((rows_total, FF), BF)),
-            (rowed(LAT, D), shaped((rows_total, D), BF)),
+            latents_spec,
             (rowed(LAT, D), shaped((rows_total, D))),
             (kept(1, FF), shaped((1, FF))),
             (kept(2, D), shaped((2, D))),
             (kept(1, D), shaped((1, D))),
             (anywhere, shaped(flat_shape, BF)),
         ],
-        (h1, grad_rows_in, norms, hid_bias, out_bias, up_one, down_one, w_qkv, w_so, up_two, down_two),
+        (h1, grad_in, norms, hid_bias, out_bias, up_one, down_one, w_qkv, w_so, up_two, down_two),
         flops=4 * mlp_flops + 4 * attn_flops,
         trans=4 * rows_total * FF,
         scratch=[
             pltpu.VMEM((LAT, FF), BF), pltpu.VMEM((LAT, FF), BF), pltpu.VMEM((slab, LANES), F32),
-            pltpu.VMEM((slab, LANES), F32), pltpu.VMEM((2, slab, LANES), BF), pltpu.SemaphoreType.DMA((2,)),
-        ],
-        limit=60,
+            pltpu.VMEM((slab, LANES), F32), pltpu.VMEM((2, slab, LANES), BF), pltpu.VMEM((LAT, D), BF),
+            pltpu.VMEM((D, LAT), F32), pltpu.VMEM((LAT, D), F32), pltpu.SemaphoreType.DMA((2, 16)),
+        ]
+        + shared,
+        limit=62,
+        collective=4 if reach else None,
     )
-    latents_out = lax.all_to_all(
-        latents.reshape(frames, LAT, D), "lat", split_axis=1, concat_axis=0, tiled=True
-    )[None]
+    if reach:
+        latents_out = latents[None]
+    else:
+        latents_out = lax.all_to_all(
+            latents.reshape(frames, LAT, D), "lat", split_axis=1, concat_axis=0, tiled=True
+        )[None]
     hot_lanes = jnp.broadcast_to(
         jnp.pad(episode_match.astype(F32), ((0, 0), (0, 16 - EPISODES)))[:, :, None], (frames, 16, LANES)
     )
-    dkv_t, flat = call(
-        backward_kernel,
+    (flat,) = call(
+        functools.partial(backward_kernel, flat_shard, extra, kv_rows),
         frames,
         [
             rowed(LAT, 3 * D), framed(HEADS, LAT), rowed(LAT, D), rowed(LAT, D), rowed(LAT, D), rowed(LAT, D),
@@ -1198,7 +1392,7 @@
             fixed(LAT, D), fixed(8, D), fixed(D, D), fixed(D, 3 * D), fixed(D, FF), fixed(FF, D), fixed(D, LANES),
             fixed(LANES, D), fixed(1, FF), fixed(2, D), fixed(1, D), anywhere,
         ],
-        [(kept(LANES, total_keys), shaped((LANES, total_keys))), (anywhere, shaped(flat_shape, BF))],
+        [(anywhere, shaped(flat_shape, BF))],
         (
             qkv, self_lse, mixed, g3, h2, h1, act_one, slope_one, kvf, cross_out, cross_lse, rank, counts,
             episode_rows, hot_lanes, latent, norms, w_so, w_qkv, up_one, down_one, w_q, w_o, dhid_two, dnorm_two,
@@ -1212,24 +1406,14 @@
             pltpu.VMEM((LAT * D // LANES, LANES), F32), pltpu.VMEM((D, LANES), F32), pltpu.VMEM((LANES, D), F32),
             pltpu.VMEM((16, D), F32), pltpu.VMEM((1, FF), F32), pltpu.VMEM((2, D), F32), pltpu.VMEM((2, D), F32),
             pltpu.VMEM((2, D), F32), pltpu.VMEM((1, D), F32), pltpu.VMEM((1, D), F32), pltpu.VMEM((1, D), F32),
-            pltpu.VMEM((512, LANES), F32), pltpu.VMEM((2, slab, LANES), BF), pltpu.SemaphoreType.DMA((2,)),
+            pltpu.VMEM((512, LANES), F32), pltpu.VMEM((2, slab, LANES), BF), pltpu.VMEM((LAT, D), BF),
+            pltpu.VMEM((LAT, D), BF), pltpu.VMEM((LAT, D), BF), pltpu.VMEM((LAT, D), F32),
+            pltpu.VMEM((LANES, total_keys), BF), pltpu.SemaphoreType.DMA((2, 16)),
         ],
         limit=60,
-        aliases={26: 1},
+        aliases={26: 0},
     )
-    grad_kv = lax.psum_scatter(dkv_t.T.astype(BF), "lat", scatter_dimension=0, tiled=True)
-    grad_w_kv = t_mm(tok_normed, grad_kv)
-    grad_tok_normed = mm_t(grad_kv, w_kv)
-    unused, token_pull = jax.vjp(layer_norm, tokens[0].astype(F32), tok_norm[0], tok_norm[1])
-    grad_tokens, grad_tok_gain, grad_tok_bias = token_pull(grad_tok_normed)
-    token_grad = grad_tokens.astype(BF)[None]
-    flat_at = flat_rows_of()
-    tok_norm_grad = jnp.stack([grad_tok_gain, grad_tok_bias]).reshape(-1, LANES).astype(BF)
-    flat = lax.dynamic_update_slice(flat, tok_norm_grad, (flat_at["tok_norm"], 0))
-    flat = lax.dynamic_update_slice(flat, grad_w_kv.astype(BF), (flat_at["w_kv"], 0))
-    local_flat = flat.reshape(-1)
     layout = param_layout()
-
     starts, ends, offset, bias_offset = [], [], 0, 0
     for name, shape in layout:
         if name == "hid_bias":
@@ -1247,8 +1431,22 @@
     flat_rows = (shard_rows, LANES)
     bias_owner, bias_at = divmod(bias_offset, shard_len)
     if reach:
-        summed, stats = reduce_all(local_flat, master_rows, starts, ends, bias_owner, bias_at // LANES)
+        summed, stats, token_grad, unused = reduce_all(
+            flat, master_rows, starts, ends, bias_owner, bias_at // LANES, tokens[0], tok_normed, w_kv, tok_norm
+        )
     else:
+        grad_kv = lax.psum_scatter(flat[flat_shard:], "lat", scatter_dimension=0, tiled=True)
+        flat = flat[:flat_shard]
+        grad_w_kv = t_mm(tok_normed, grad_kv)
+        grad_tok_normed = mm_t(grad_kv, w_kv)
+        unused, token_pull = jax.vjp(layer_norm, tokens[0].astype(F32), tok_norm[0], tok_norm[1])
+        grad_tokens, grad_tok_gain, grad_tok_bias = token_pull(grad_tok_normed)
+        token_grad = grad_tokens.astype(BF)
+        flat_at = flat_rows_of()
+        tok_norm_grad = jnp.stack([grad_tok_gain, grad_tok_bias]).reshape(-1, LANES).astype(BF)
+        flat = lax.dynamic_update_slice(flat, tok_norm_grad, (flat_at["tok_norm"], 0))
+        flat = lax.dynamic_update_slice(flat, grad_w_kv.astype(BF), (flat_at["w_kv"], 0))
+        local_flat = flat.reshape(-1)
         summed = lax.psum_scatter(local_flat, "lat", scatter_dimension=0, tiled=True)
         summed = lax.psum(summed, "kf").reshape(flat_rows)
         grad_sq, weight_sq = call(
@@ -1294,7 +1492,7 @@
         trust = (jnp.sqrt(weight_sq) / (jnp.sqrt(update_sq) + 1e-06))[: len(layout)]
     return (
         latents_out,
-        token_grad,
+        token_grad[None],
         grad_shard.reshape(-1),
         lamb_update.reshape(-1),
         new_one.reshape(-1),

time: 493 us -> 389 us (0.79); the launches traced: 484 us -> 389 us
  waiting for transfers between devices: 61.9 us -> 0 us
  between operations: 14.6 us -> 0.79 us
  starting transfers between devices: 8.29 us -> 0 us
  local copies, waits for them, and re-layouts: 13.8 us -> 7.26 us
    reduce_scatter x1 -> x0, waiting for transfers between devices: 35.3 us -> none  [body(): lax.psum_scatter(dkv_t.T.astype(BF), 'lat', scatter_dimension=0, tiled=True)]
    all_to_all x2 -> x0, waiting for transfers between devices: 26.5 us -> none  [the longest x1 26.5 us: body(): lax.all_to_all(latent_grad[0], 'lat', split_axis=0, concat_axis=1, tiled=...]
    all_to_all x2 -> x0, starting transfers between devices: 8.25 us -> none  [the longest x1 4.64 us: body(): lax.all_to_all(latents.reshape(frames, LAT, D), 'lat', split_axis=1, conc...]
  transfers between devices with their start and end apart: 3 -> 0, of which waited for: 2 -> 0; matrix products, arithmetic and copies ran while one was open for 2% -> 0% of each run, Pallas kernels for 20% -> 0%
where the time goes in v1:
time: 389 us
  Pallas kernels  380 us (98%)
  local copies, waits for them, and re-layouts  7.26 us (2%)
    pallas_call x3, Pallas kernels, call(): pl.pallas_call(kernel, grid=(grid,), in_specs=in_specs, out_specs=list(ou...  224 us
    pallas_call x1, Pallas kernels, reduce_all(): pl.pallas_call(functools.partial(reduce_kernel, bias_owner, bias_row), ou...  80.4 us
    pallas_call x1, Pallas kernels, begin_all(): pl.pallas_call(functools.partial(begin_kernel, chunks), out_shape=[shaped...  69.2 us

profile of v1, /device:TPU:0, one launch (start us, length us, event | category | flops | bytes accessed | tf_op | source)
XLA Modules:
  0.0 388.8 jit_solution(8024749568515675832)
XLA Ops:
  0.6 0.0 copy-start
  0.7 0.6 copy-done
  1.3 0.1 dynamic-slice_bitcast_fusion
  1.4 0.1 iota_compare_fusion
  1.4 0.6 pad_convert_fusion.hot
  2.0 69.2 %shard_map.152 = (bf16[512,2048]{1,0:T(8,128)(2,1)}, bf16[2048,512]{1,0:T(8,128)(2,1)}, bf16[512,1536]{1,0:T(8,128)(2,1)}, bf16[512,512]{1,0:T(8,128)(2,1)}, bf1...) custom-call(f32[5488,128]{1,0:T(8,128)} %bitcast.16, ...), custom_call_target="tpu_custom_call" | custom-call | tf_op jit(solution)/shard_map/pallas_call | solution.py:755
  71.3 109.4 %shard_map.153 = (f32[2048,512]{1,0:T(8,128)}, bf16[2048,1536]{1,0:T(8,128)(2,1)}, f32[4,8,512]{2,1,0:T(8,128)}, bf16[2048,512]{1,0:T(8,128)(2,1)}, bf16[2048,20...) custom-call(f32[2048,512]{1,0:T(8,128)} %get-tuple-element.50.h1, ...), custom_call_target="tpu_custom_call" | custom-call | flops 42949672960 | bytes 64837632 | tf_op jit(solution)/shard_map/pallas_call | solution.py:1213
  180.7 0.7 broadcast_in_dim.13.hot
  181.4 0.0 copy-start.14
  181.4 0.0 copy-start.13
  181.4 0.0 copy-start.2
  181.4 0.0 copy-start.4
  181.4 0.0 copy-start.5
  181.4 0.0 copy-start.10
  181.4 0.0 copy-start.11
  181.4 101.9 %shard_map.154 = bf16[48000,128]{1,0:T(8,128)(2,1)} custom-call(bf16[2048,1536]{1,0:T(8,128)(2,1)} %get-tuple-element.61.qkv, f32[4,8,512]{2,1,0:T(8,128)} %get-tuple-element.62.lse, bf16[2048,512]{1,0:T(8,128)(2,1)} %get-tuple-element.63.mixed, f32[2048,512]{1,0:T(8,128)} %get-tuple-element.64.g3, ...), custom_call_target="tpu_custom_call", output_to_operand_aliasing={{}: (26, {})} | custom-call | flops 40265318400 | bytes 70678528 | tf_op jit(solution)/shard_map/pallas_call | solution.py:1213
  283.3 0.0 copy-done.14
  283.3 0.1 broadcast_in_dim.11.starts
  283.4 0.0 copy-done.13
  283.4 0.0 copy-start.8
  283.4 0.1 broadcast_in_dim.12.ends
  283.5 0.0 copy-done.2
  283.5 0.0 copy-done.4
  283.5 0.0 copy-done.5
  283.5 0.0 copy-done.10
  283.5 0.0 copy-done.11
  283.5 0.0 copy-start.9
  283.5 80.4 %shard_map.155 = (bf16[5488,128]{1,0:T(8,128)(2,1)S(1)}, f32[56,128]{1,0:T(8,128)S(1)}, bf16[512,256]{1,0:T(8,128)(2,1)S(1)}, bf16[2,2,2,6000,128]{4,3,2,1,0:T(8,128)(2,1)}) custom-call(s32[16,128]{1,0:T(8,128)S(1)} %broadcast_in_dim.11.starts, s32[16,128]{1,0:T(8,128)S(1)} %broadcast_in_dim.12.ends, ...), custom_call_target="tpu_custom_call", output_to_operand_aliasing={{3}: (2, {})} | custom-call | tf_op jit(solution)/shard_map/pallas_call | solution.py:1241
  363.9 0.0 copy-done.8
  363.9 0.0 copy-done.9
  364.0 0.0 copy-start.3
  364.0 1.1 copy-done.3
  365.0 0.0 copy-start.6
  365.0 0.6 copy-done.6
  365.7 0.0 copy-start.7
  365.7 0.0 copy-start.12
  365.7 0.0 copy-start.1
  365.7 12.8 %shard_map.156 = (f32[5488,128]{1,0:T(8,128)}, f32[5488,128]{1,0:T(8,128)}, f32[5488,128]{1,0:T(8,128)}, f32[5488,128]{1,0:T(8,128)}, f32[16,128]{1,0:T(8,128)}) custom-call(s32[1]{0:T(128)} %bitcast.8.base, f32[56,128]{1,0:T(8,128)} %copy-done.6, s32[16,128]{1,0:T(8,128)} %copy-done.8, s32[16,128]{1,0:T(8,128)} %copy-done.9, bf16[5488,128]{1,0:T(8,128)(2,1)} %copy-done.3, ...), custom_call_target="tpu_custom_call" | custom-call | bytes 21127172 | tf_op jit(solution)/shard_map/pallas_call | solution.py:1213
  378.5 6.3 %shard_map.157 = f32[16,128]{1,0:T(8,128)} custom-call(f32[16,128]{1,0:T(8,128)} %get-tuple-element.91.update_sq, f32[56,128]{1,0:T(8,128)} %copy-done.6), custom_call_target="tpu_custom_call" | custom-call | tf_op jit(solution)/shard_map/pallas_call | solution.py:1477
  384.8 1.3 slice_reduce_fusion
  386.1 0.0 copy-done.7
  386.1 0.6 reshape.65
  386.7 0.0 copy-done.12
  386.7 1.3 copy.23
  388.1 0.7 copy.24
  388.8 0.0 copy-done.1
  (2 shorter events, 0.0 us)
Async XLA Ops:
  0.6 0.7 copy-start
  181.4 101.9 %copy-start.14 = (s32[16]{0:T(128)S(1)}, s32[16]{0:T(128)}, u32[]{:S(2)}) copy-start(s32[16]{0:T(128)} %constant.22.clone) | copy-start | bytes 196
  181.4 102.0 %copy-start.13 = (s32[16]{0:T(128)S(1)}, s32[16]{0:T(128)}, u32[]{:S(2)}) copy-start(s32[16]{0:T(128)} %constant.23.clone) | copy-start | bytes 196
  181.4 102.1 %copy-start.2 = (f32[702464]{0:T(1024)S(1)}, f32[702464]{0:T(1024)}, u32[]{:S(2)}) copy-start(f32[702464]{0:T(1024)} %param.12) | copy-start | bytes 8429572
  181.4 102.1 %copy-start.4 = (bf16[1,512,256]{2,1,0:T(8,128)(2,1)S(1)}, bf16[1,512,256]{2,1,0:T(8,128)(2,1)}, u32[]{:S(2)}) copy-start(bf16[1,512,256]{2,1,0:T(8,128)(2,1)} %param.9) | copy-start | bytes 786436
  181.4 102.1 %copy-start.5 = (bf16[512,256]{1,0:T(8,128)(2,1)S(1)}, bf16[512,256]{1,0:T(8,128)(2,1)}, u32[]{:S(2)}) copy-start(bf16[512,256]{1,0:T(8,128)(2,1)} %get-tuple-element.81.tok_normed) | copy-start | bytes 786436
  181.4 102.1 %copy-start.10 = (bf16[256,128]{1,0:T(8,128)(2,1)S(1)}, bf16[256,128]{1,0:T(8,128)(2,1)}, u32[]{:S(2)}) copy-start(bf16[256,128]{1,0:T(8,128)(2,1)} %get-tuple-element.82.w_kv) | copy-start | bytes 196612
  181.4 102.1 %copy-start.11 = (f32[2,256]{1,0:T(2,128)S(1)}, f32[2,256]{1,0:T(2,128)}, u32[]{:S(2)}) copy-start(f32[2,256]{1,0:T(2,128)} %get-tuple-element.83.tok_norm) | copy-start | bytes 6148
  283.4 80.5 %copy-start.8 = (s32[16,128]{1,0:T(8,128)}, s32[16,128]{1,0:T(8,128)S(1)}, u32[]{:S(2)}) copy-start(s32[16,128]{1,0:T(8,128)S(1)} %broadcast_in_dim.11.starts) | copy-start | bytes 24580
  283.5 80.4 %copy-start.9 = (s32[16,128]{1,0:T(8,128)}, s32[16,128]{1,0:T(8,128)S(1)}, u32[]{:S(2)}) copy-start(s32[16,128]{1,0:T(8,128)S(1)} %broadcast_in_dim.12.ends) | copy-start | bytes 24580
  364.0 1.1 copy-start.3
  365.0 0.6 copy-start.6
  365.7 20.5 %copy-start.7 = (f32[56,128]{1,0:T(8,128)S(1)}, f32[56,128]{1,0:T(8,128)}, u32[]{:S(2)}) copy-start(f32[56,128]{1,0:T(8,128)} %copy-done.6) | copy-start | bytes 86020
  365.7 21.1 %copy-start.12 = (bf16[32,64,512]{2,1,0:T(8,128)(2,1)S(1)}, bf16[32,64,512]{2,1,0:T(8,128)(2,1)}, u32[]{:S(2)}) copy-start(bf16[32,64,512]{2,1,0:T(8,128)(2,1)} %get-tuple-element.60) | copy-start | bytes 6291460
  365.7 23.1 %copy-start.1 = (s32[1,32]{1,0:T(1,128)S(1)}, s32[1,32]{1,0:T(1,128)}, u32[]{:S(2)}) copy-start(s32[1,32]{1,0:T(1,128)} %param.11) | copy-start | bytes 388

commit v2 on v1

--- a/solution.py
+++ b/solution.py
@@ -268,6 +268,8 @@
         self.full = pl.cdiv(shard, BATCH)
         self.batches = self.full + self.plane
         self.back = self.full * BATCH - shard
+        self.held = flat_rows_of()["tok_norm"] // BATCH
+        self.early = self.full - 1 - (self.held + 4)
 
     @staticmethod
     def scratch(shard):
@@ -285,13 +287,22 @@
         sems = [dma((2,)), dma((10, 4)), dma((n,)), dma((n, 2)), dma((n, 2)), dma((n,)), dma((n,)), dma((n, 3))]
         return bufs + sems
 
+    def from_on(self, i, first):
+        return (i + 64 - first) // 64
+
     def row(self, i):
-        p, n, held = i - self.plane, self.full, flat_rows_of()["tok_norm"] // BATCH
-        late = p // (n - 4)
-        b = (1 - late) * lax.rem(p + held + 4, n) + late * (held + lax.rem(p - (n - 4) + 2, 4))
-        main = (i + n) // (n + self.plane)
-        row = (1 - main) * (self.shard + i * BATCH) + main * (b * BATCH - (b // (n - 1)) * self.back)
+        n, held = self.full, self.held
+        on = functools.partial(self.from_on, i)
+        keys = on(self.early) - on(self.early + 2)
+        shift = held + 4 + on(self.early + 2) * (-2) + on(self.early + 3) * (-n)
+        shift = shift + on(self.early + 3 + held) * 2 + on(self.early + 5 + held) * (-4)
+        b = i + shift
+        row = keys * (self.shard + (i - self.early) * BATCH)
+        row = row + (1 - keys) * (b * BATCH - (b // (n - 1)) * self.back)
         return pl.multiple_of(row, 16)
+
+    def is_keys(self, i):
+        return (i >= self.early) & (i < self.early + self.plane)
 
     def own_copy(self, i):
         slot = lax.rem(i, 2)
@@ -330,9 +341,13 @@
         ]
 
     def launch(self, stage, i):
-        @pl.when(i >= (4 if stage < 3 else 4 + self.plane))
+        before = i - 4
+        if stage >= 3:
+            before = before - 4 * (self.from_on(before, self.early) - self.from_on(before, self.early + self.plane))
+
+        @pl.when(i >= 4)
         def _():
-            for copy in self.copies(stage, i - 4):
+            for copy in self.copies(stage, before):
                 copy.wait_send()
 
         for copy in self.copies(stage, i):
@@ -370,7 +385,7 @@
             self.landed(5, i)
             self.out[pl.ds(self.row(i), BATCH), :] = self.res[i]
         if stage == 3:
-            pl.when(i >= self.plane)(lambda: self.launch(stage, i))
+            pl.when(jnp.logical_not(self.is_keys(i)))(lambda: self.launch(stage, i))
         elif stage < 6:
             self.launch(stage, i)
 
@@ -378,7 +393,9 @@
         for stage, lag in enumerate(self.lags):
             i = t - lag
 
-            @pl.when((i >= (0 if stage < 4 else self.plane)) & (i < self.batches))
+            inside = (i >= 0) & (i < self.batches)
+
+            @pl.when(inside if stage < 4 else inside & jnp.logical_not(self.is_keys(i)))
             def _(stage=stage, i=i):
                 self.work(stage, i)
 
@@ -423,41 +440,84 @@
 
 def reduce_kernel(
     bias_owner, bias_at, starts, ends, unused_flat, master, tokens, tok_normed, w_kv, tok_norm,
+    g1, kvf, co, lse, rank, count, episode, hot, latent, norms, w_q, w_o,
+    dnorm_one, dnorm_sa, dnorm_two, dhid_one, dhid_two, dout_one, dout_so, dout_two,
     summed, stats, token_grad, grads, *scratch,
 ):
     place = Place()
-    block, block_send, block_recv, edge, kv_grad, edge_sem = scratch[:6]
-    shard = master.shape[0]
-    red = Reduction(place, shard, grads, summed, scratch[6:13], scratch[13:])
+    block, block_send, block_recv, edge, kv_grad, edge_sem, g1_held, g1_sem, kv_low, kv_sem = scratch[:10]
+    accs, (stage, low, latent_low), engine = scratch[10:17], scratch[17:20], scratch[20:]
+    acc_latent, acc_q, acc_o, acc_episode, dnorm, dout, dkv_t = accs
+    shard, frames = master.shape[0], kvf.shape[0]
+    red = Reduction(place, shard, grads, summed, engine[:7], engine[7:])
+    frame_copies = [pltpu.make_async_copy(g1.at[f], g1_held.at[f], g1_sem.at[f]) for f in range(frames)]
+    for copy in frame_copies:
+        copy.start()
     greet([place.lat_other(d) for d in range(1, 8)] + [place.z_other(d) for d in (1, 2, 3)])
+    for ref in accs:
+        ref[...] = jnp.zeros_like(ref)
+
+    def run(first, last):
+        lax.fori_loop(first, last, lambda t, c: (red.tick(t), c)[1], 0)
+
+    def frame(f, carry):
+        red.tick(2 * f)
+        pltpu.make_async_copy(g1.at[f], g1_held.at[f], g1_sem.at[f]).wait()
+        rows = pl.ds(pl.multiple_of(f * LAT, LAT), LAT)
+        cross_back_frame(
+            g1_held[f], kvf[f], co[rows, :], lse[f], rank.at[f], count[f, 0:1, 0:1], episode[f], hot[f, :, 0:1],
+            latent, norms, w_q, w_o, *accs, pause=lambda: red.tick(2 * f + 1),
+        )
+        return carry
+
+    lax.fori_loop(0, frames, frame, 0)
+    run(2 * frames, red.early)
     at = flat_rows_of()
-    edge_rows = grads.at[0, 0, 0, pl.ds(at["tok_norm"] // 16 * 16, 16), :]
-    fetch = pltpu.make_async_copy(edge_rows, edge, edge_sem.at[0])
-    fetch.start()
-    ready = red.lags[3] + red.plane
-    lax.fori_loop(0, ready, lambda t, c: (red.tick(t), c)[1], 0)
-    fetch.wait()
-    grad_kv = jnp.concatenate([red.r2[i, h] for i in range(red.plane) for h in range(2)], axis=0)
+    copies = []
+
+    def put(source, row):
+        owner, local = row if isinstance(row, tuple) else divmod(row, shard)
+        dst = grads.at[owner // 4, owner // 2 % 2, owner % 2, pl.ds(local, source.shape[0]), :]
+        copies.append(pltpu.make_async_copy(source, dst, kv_sem.at[len(copies)]))
+        copies[-1].start()
+
+    write_small(
+        put, stage, low, latent_low, acc_latent, acc_q, acc_o, acc_episode,
+        stacked(dnorm, dnorm_one, dnorm_sa, dnorm_two), stacked(dhid_one, dhid_two),
+        stacked(dout, dout_one, dout_so, dout_two),
+    )
+    edge_row = at["tok_norm"] // 16 * 16
+    edge[...] = low[0, edge_row - at["episode"] : edge_row - at["episode"] + 16, :]
+    count_kv = tokens.shape[0]
+    for j in range(8):
+        kv_low[j] = dkv_t[:, j * count_kv : (j + 1) * count_kv].T
+        put(kv_low.at[j], (j, shard))
+    for copy in copies:
+        copy.wait()
+    ready = red.early + red.lags[3] + red.plane
+    run(red.early, ready)
+    grad_kv = jnp.concatenate([red.r2[red.early + i, h] for i in range(red.plane) for h in range(2)], axis=0)
     token_backward(grad_kv, tokens, tok_normed, w_kv, tok_norm, token_grad, kv_grad, edge)
     writes = [
-        pltpu.make_async_copy(edge, edge_rows, edge_sem.at[0]),
+        pltpu.make_async_copy(edge, grads.at[0, 0, 0, pl.ds(edge_row, 16), :], edge_sem.at[0]),
         pltpu.make_async_copy(kv_grad, grads.at[0, 0, 0, pl.ds(at["w_kv"], DIN), :], edge_sem.at[1]),
     ]
     for copy in writes:
         copy.start()
+    run(ready, ready + 2)
     for copy in writes:
         copy.wait()
-    lax.fori_loop(ready, red.ticks(), lambda t, c: (red.tick(t), c)[1], 0)
     step = 784
-    grad_sq = jnp.zeros((1, LANES), F32)
     weight_sq = jnp.zeros((16, LANES), F32)
     for j in range(shard // step):
-        at = slice(j * step, (j + 1) * step)
-        part = summed[at, :].astype(F32)
+        hot_rows = segment_hot(starts, ends, place.me * shard + j * step, step)
+        part = master[j * step : (j + 1) * step, :]
+        weight_sq = weight_sq + segment_sums(hot_rows, part * part)
+    run(ready + 2, red.ticks())
+    grad_sq = jnp.zeros((1, LANES), F32)
+    for j in range(shard // step):
+        part = summed[j * step : (j + 1) * step, :].astype(F32)
         grad_sq = grad_sq + col_sum(part * part)
-        hot = segment_hot(starts, ends, place.me * shard + j * step, step)
-        part = master[at, :]
-        weight_sq = weight_sq + segment_sums(hot, part * part)
     bias = summed[bias_at : bias_at + 2 * FF // LANES, :].astype(F32)
     bias = jnp.where(place.me == bias_owner, bias, 0.0)
     head = jnp.concatenate([grad_sq, jnp.zeros((7, LANES), F32), weight_sq, bias], axis=0)
@@ -795,13 +855,6 @@
 FCHUNK = 512
 
 
-def add_flat(acc, row, part):
-    wide = part.shape[1] // LANES
-    for j in range(wide):
-        at = pl.ds(row + j, part.shape[0], stride=wide)
-        acc[at, :] = acc[at, :] + part[:, j * LANES : (j + 1) * LANES]
-
-
 def to_flat(stage, matrix):
     rows, wide = matrix.shape[0], matrix.shape[1] // LANES
     for j in range(wide):
@@ -818,34 +871,24 @@
     normed_ref[...] = (xhat * gain + bias).astype(BF)
     total_ref[...] = rows + down_bias
 
-    def step(c, carry):
-        at = chunk_of(c)
+    for c in range(FF // FCHUNK):
+        at = slice(c * FCHUNK, (c + 1) * FCHUNK)
         act, slope = gelu_pair(mm(normed_ref[...], w_up[:, at]) + up_bias[:, at])
         act = act.astype(BF)
         act_ref[:, at] = act
         slope_ref[:, at] = slope.astype(BF)
         total_ref[...] += mm(act, w_down[at, :])
-        return carry
-
-    lax.fori_loop(0, FF // FCHUNK, step, 0)
 
 
 def feed_back(grad_ref, normed_ref, xhat, rstd, gain, act, slope, w_up, w_down, acc_up, acc_down, dhid, dnorm, dout, work):
     work[...] = jnp.zeros(work.shape, F32)
-
-    def step(c, carry):
-        at = chunk_of(c)
+    for c in range(FF // FCHUNK):
+        at = slice(c * FCHUNK, (c + 1) * FCHUNK)
         dpre = (mm_t(grad_ref[...], w_down[at, :]) * slope[:, at].astype(F32)).astype(BF)
         dhid[:, at] += col_sum(dpre.astype(F32))
         work[...] += mm_t(dpre, w_up[:, at])
-        part = t_mm(normed_ref[...], dpre)
-        for j in range(FCHUNK // LANES):
-            rows = pl.ds(c * (FCHUNK // LANES) + j, D, stride=FF // LANES)
-            acc_up[rows, :] = acc_up[rows, :] + part[:, j * LANES : (j + 1) * LANES]
-        add_flat(acc_down, c * FCHUNK * (D // LANES), t_mm(act[:, at], grad_ref[...]))
-        return carry
-
-    lax.fori_loop(0, FF // FCHUNK, step, 0)
+        acc_up[:, at] += t_mm(normed_ref[...], dpre)
+        acc_down[at, :] += t_mm(act[:, at], grad_ref[...])
     grad_normed = work[...]
     dnorm[...] += jnp.concatenate([col_sum(grad_normed * xhat), col_sum(grad_normed)], axis=0)
     dout[...] += col_sum(grad_ref[...].astype(F32))
@@ -868,14 +911,29 @@
     return spans
 
 
-def write_flat(flat, low, pieces, sems, shard, extra):
+def flatten(acc, stage, low, slot):
+    wide = acc.shape[1] // LANES
+    block = min(acc.shape[0], 2048 // wide // 128 * 128)
+    span = block * wide
+
+    def step(i, carry):
+        part = acc[pl.ds(pl.multiple_of(i * block, block), block), :]
+        for j in range(wide):
+            stage[pl.ds(j, block, stride=wide), :] = part[:, j * LANES : (j + 1) * LANES]
+        low[slot, pl.ds(pl.multiple_of(i * span, span), span), :] = stage[0:span, :].astype(BF)
+        return carry
+
+    lax.fori_loop(0, acc.shape[0] // block, step, 0)
+
+
+def write_flat(flat, stage, low, pieces, sems, shard, extra):
     pending = {}
     for j, (acc, row) in enumerate(pieces):
-        count = acc.shape[0]
+        count = acc.shape[0] * acc.shape[1] // LANES
         slot = j % 2
         for copy in pending.get(slot, []):
             copy.wait()
-        low[slot, 0:count, :] = acc[...].astype(BF)
+        flatten(acc, stage, low, slot)
         pending[slot] = [
             pltpu.make_async_copy(low.at[slot, pl.ds(off, part), :], flat.at[pl.ds(at, part), :], sems.at[slot, k])
             for k, (off, part, at) in enumerate(flat_spans(row, count, shard, extra))
@@ -952,7 +1010,7 @@
 def forward_kernel(
     reach, shard, extra, h1, grad, norms, hid_bias, out_bias, up_one, down_one, w_qkv, w_so, up_two, down_two,
     h2_out, qkv, lse_out, mixed_out, act_one, slope_one, latents, g3, dhid, dnorm, dout, flat,
-    act_two, slope_two, acc_up, acc_down, low, normed, mixed_t, work, sems, *shared,
+    act_two, slope_two, acc_up, acc_down, stage, low, normed, mixed_t, work, sems, *shared,
 ):
     step = pl.program_id(0)
     if reach:
@@ -976,6 +1034,8 @@
     lax.fori_loop(0, 3, project, 0)
     scale = jnp.asarray(0.125, BF)
 
+    ones = jnp.ones((16, LAT), BF)
+
     def attend(pair, carry):
         query_pair = qkv[:, chunk_of(pair, LANES)] * scale
         key_pair = qkv[:, chunk_of(pair + D // LANES, LANES)]
@@ -983,12 +1043,13 @@
         for half in range(2):
             scores = mm_t(key_pair, keep_half(query_pair, half))
             top = jnp.max(scores, axis=0, keepdims=True)
-            terms = jnp.exp(scores - top)
-            total = jnp.sum(terms, axis=0, keepdims=True)
-            prob = (terms * (1.0 / total)).astype(BF)
+            terms = jnp.exp(scores - top).astype(BF)
+            values = jnp.concatenate([value_t[half * HEAD_DIM : (half + 1) * HEAD_DIM, :], ones], axis=0)
+            product = mm(values, terms)
+            total = product[HEAD_DIM : HEAD_DIM + 1, :]
             lse_out[0, pl.ds(2 * pair + half, 1), :] = top + jnp.log(total)
             at = pl.ds(pl.multiple_of(pair * LANES + half * HEAD_DIM, HEAD_DIM), HEAD_DIM)
-            mixed_t[at, :] = mm(value_t[half * HEAD_DIM : (half + 1) * HEAD_DIM, :], prob)
+            mixed_t[at, :] = product[0:HEAD_DIM, :] * (1.0 / total)
         return carry
 
     lax.fori_loop(0, HEADS // 2, attend, 0)
@@ -1015,32 +1076,26 @@
     def _():
         at = flat_rows_of()
         half = D * FF // LANES
-        write_flat(flat, low, [(acc_up, at["w_up"] + half), (acc_down, at["w_down"] + half)], sems, shard, extra)
+        write_flat(flat, stage, low, [(acc_up, at["w_up"] + half), (acc_down, at["w_down"] + half)], sems, shard, extra)
         if reach:
             traffic.finish()
 
 
 def backward_kernel(
-    shard, extra, kv_rows, qkv, lse, mixed, g3, h2, h1, act_one, slope_one, kvf_in, co_in, cross_lse, rank, count, episode, hot,
-    latent, norms, w_so, w_qkv, up_one, down_one, w_q, w_o, dhid_two, dnorm_two, dout_two, flat_in,
-    flat,
-    dqkv, acc_up, acc_down, acc_qkv, acc_so, acc_latent, acc_q, acc_o, acc_episode,
-    dhid, dnorm_sa, dnorm_one, dnorm_cross, dout_so, dout_one, dout_cross, stage, low, normed, grad_mixed, grad_low,
-    work, dkv_t, sems,
+    shard, extra, qkv, lse, mixed, g3, h2, h1, act_one, slope_one, norms, w_so, w_qkv, up_one, down_one, flat_in,
+    g1, dhid, dnorm_sa, dnorm_one, dout_so, dout_one, flat,
+    dqkv, acc_up, acc_down, acc_qkv, acc_so, stage, low, normed, grad_mixed, grad_low, work, sems,
 ):
     step = pl.program_id(0)
     clear(
         step == 0,
-        (
-            acc_up, acc_down, acc_qkv, acc_so, acc_latent, acc_q, acc_o, acc_episode, dhid, dnorm_sa, dnorm_one,
-            dnorm_cross, dout_so, dout_one, dout_cross, dkv_t,
-        ),
+        (acc_up, acc_down, acc_qkv, acc_so, dhid, dnorm_sa, dnorm_one, dout_so, dout_one),
     )
     scale = jnp.asarray(0.125, BF)
     grad_three = g3[...]
     grad_low[...] = grad_three.astype(BF)
     dout_so[...] += col_sum(grad_low[...].astype(F32))
-    add_flat(acc_so, 0, t_mm(mixed[...], grad_low[...]))
+    acc_so[...] += t_mm(mixed[...], grad_low[...])
     grad_mixed[...] = mm_t(grad_low[...], w_so[...]).astype(BF)
 
     def attend(pair, carry):
@@ -1074,16 +1129,10 @@
     normed[...] = (xhat * norms[4:5, :] + norms[5:6, :]).astype(BF)
     work[...] = jnp.zeros(work.shape, F32)
 
-    def project(c, carry):
-        at = chunk_of(c)
+    for c in range(3):
+        at = slice(c * D, (c + 1) * D)
         work[...] += mm_t(dqkv[:, at], w_qkv[:, at])
-        part = t_mm(normed[...], dqkv[:, at])
-        for j in range(D // LANES):
-            rows = pl.ds(c * (D // LANES) + j, D, stride=3 * D // LANES)
-            acc_qkv[rows, :] = acc_qkv[rows, :] + part[:, j * LANES : (j + 1) * LANES]
-        return carry
-
-    lax.fori_loop(0, 3, project, 0)
+        acc_qkv[:, at] += t_mm(normed[...], dqkv[:, at])
     grad_in = work[...]
     dnorm_sa[...] += jnp.concatenate([col_sum(grad_in * xhat), col_sum(grad_in)], axis=0)
     grad_two = grad_three + norm_back(grad_in, xhat, rstd, norms[4:5, :])
@@ -1096,94 +1145,131 @@
         acc_up, acc_down, dhid, dnorm_one, dout_one, work,
     )
 
-    cap = kvf_in.shape[1]
-    start = latent[...].astype(F32) + episode[0]
+    g1[...] = grad_one
+
+    @pl.when(step == pl.num_programs(0) - 1)
+    def _():
+        at = flat_rows_of()
+        write_flat(
+            flat, stage, low,
+            [(acc_up, at["w_up"]), (acc_down, at["w_down"]), (acc_qkv, at["w_qkv"]), (acc_so, at["w_so"])],
+            sems, shard, extra,
+        )
+
+
+def cross_back_frame(
+    grad_one, kvf, co, lse, rank_ref, count, episode_row, hot_column, latent, norms, w_q, w_o,
+    acc_latent, acc_q, acc_o, acc_episode, dnorm, dout, dkv_t, pause=lambda: None,
+):
+    cap = kvf.shape[0]
+    start = latent[...].astype(F32) + episode_row
     xhat, rstd = norm_stats(start)
     query_in = (xhat * norms[0:1, :] + norms[1:2, :]).astype(BF)
-    queries = mm(query_in, w_q[...]).astype(BF) * scale
-    kvf = kvf_in[0]
+    queries = mm(query_in, w_q[...]).astype(BF) * jnp.asarray(0.125, BF)
     branch = grad_one.astype(BF)
     grad_co = mm_t(branch, w_o[...]).astype(BF)
-    acc_o[...] += t_mm(co_in[...], branch)
-    dout_cross[...] += col_sum(branch.astype(F32))
-    scores = cross_scores(kvf, queries, count[0, 0:1, 0:1])
-    prob = jnp.exp(scores - cross_lse[0])
+    acc_o[...] += t_mm(co, branch)
+    dout[...] += col_sum(branch.astype(F32))
+    scores = cross_scores(kvf, queries, count)
+    prob = jnp.exp(scores - lse)
     weighted = prob * mm_t(kvf, grad_co)
     grad_score = (weighted - prob * col_sum(weighted)).astype(BF)
     grad_kv = (mm(grad_score, queries) + mm(prob.astype(BF), grad_co)).astype(BF)
     grad_query = (t_mm(kvf, grad_score).T * 0.125).astype(BF)
+    pause()
     acc_q[...] += t_mm(query_in, grad_query)
     grad_in = mm_t(grad_query, w_q[...])
     grad_start = grad_one + norm_back(grad_in, xhat, rstd, norms[0:1, :])
-    dnorm_cross[...] += jnp.concatenate([col_sum(grad_in * xhat), col_sum(grad_in)], axis=0)
-    add_flat(acc_latent, 0, grad_start)
-    acc_episode[...] += hot[0, :, 0:1] * col_sum(grad_start)
+    dnorm[...] += jnp.concatenate([col_sum(grad_in * xhat), col_sum(grad_in)], axis=0)
+    acc_latent[...] += grad_start
+    acc_episode[...] += hot_column * col_sum(grad_start)
     grad_kv_t = grad_kv.T
     chunk = 8 * LANES
 
     def scatter(j, carry):
-        sel = select_tokens(rank[0, pl.ds(pl.multiple_of(j * 8, 8), 8), :], cap)
+        sel = select_tokens(rank_ref[pl.ds(pl.multiple_of(j * 8, 8), 8), :], cap)
         at = pl.ds(pl.multiple_of(j * chunk, chunk), chunk)
         dkv_t[:, at] = added(dkv_t[:, at], mm(grad_kv_t, sel))
         return carry
 
     lax.fori_loop(0, dkv_t.shape[1] // chunk, scatter, 0)
 
+
+def write_small(put, stage, low, latent_low, acc_latent, acc_q, acc_o, acc_episode, norm_grads, hid_grads, out_grads):
+    at = flat_rows_of()
+    flatten(acc_latent, stage, latent_low, 0)
+    put(latent_low.at[0], 0)
+    head = at["lat_norms"] - at["episode"]
+    used = EPISODES * (D // LANES)
+    rows = [to_flat(stage, acc_episode[...])[0:used, :], jnp.zeros((head - used, LANES), F32)]
+    rows = jnp.concatenate(rows + [to_flat(stage, norm_grads)], axis=0)
+    top = rows.shape[0]
+    low[0, 0:top, :] = rows.astype(BF)
+    put(low.at[0, pl.ds(0, top), :], at["episode"])
+    stage[0:D, :] = acc_q[...]
+    even = stage[pl.ds(0, D // 2, stride=2), :]
+    odd = pltpu.roll(stage[pl.ds(1, D // 2, stride=2), :], CH, 1)
+    low[0, top : top + D // 2, :] = jnp.where(lane_half(even.shape, 0), even, odd).astype(BF)
+    both = D // 2 + CH * D // LANES
+    low[0, top + D // 2 : top + both, :] = to_flat(stage, acc_o[CH : 2 * CH, :]).astype(BF)
+    put(low.at[0, pl.ds(top, both), :], at["w_q"])
+    hid = to_flat(stage, hid_grads)
+    last = top + both
+    low[0, last : last + hid.shape[0], :] = hid.astype(BF)
+    end = hid.shape[0] + 4 * D // LANES
+    low[0, last + hid.shape[0] : last + end, :] = to_flat(stage, out_grads).astype(BF)
+    put(low.at[0, pl.ds(last, end), :], at["hid_bias"])
+
+
+def cross_accumulators(total_keys):
+    shapes = [(LAT, D), (D, LANES), (LANES, D), (16, D), (2, D), (1, D)]
+    return [pltpu.VMEM(shape, F32) for shape in shapes] + [pltpu.VMEM((LANES, total_keys), BF)]
+
+
+def small_buffers():
+    return [pltpu.VMEM((2048, LANES), F32), pltpu.VMEM((1, 640, LANES), BF), pltpu.VMEM((1, 2048, LANES), BF)]
+
+
+def stacked(*parts):
+    return jnp.concatenate([part[...] for part in parts], axis=0)
+
+
+def cross_bwd_kernel(
+    kv_rows, g1, kvf, co, lse, rank, count, episode, hot, latent, norms, w_q, w_o,
+    dnorm_one, dnorm_sa, dnorm_two, dhid_one, dhid_two, dout_one, dout_so, dout_two, flat_in, flat,
+    acc_latent, acc_q, acc_o, acc_episode, dnorm, dout, dkv_t, stage, low, latent_low, kv_low, sems,
+):
+    step = pl.program_id(0)
+    accs = (acc_latent, acc_q, acc_o, acc_episode, dnorm, dout, dkv_t)
+    clear(step == 0, accs)
+    cross_back_frame(
+        g1[...], kvf[0], co[...], lse[0], rank.at[0], count[0, 0:1, 0:1], episode[0], hot[0, :, 0:1],
+        latent, norms, w_q, w_o, *accs,
+    )
+
     @pl.when(step == pl.num_programs(0) - 1)
     def _():
-        at = flat_rows_of()
-        write_flat(
-            flat, low,
-            [
-                (acc_up, at["w_up"]), (acc_down, at["w_down"]), (acc_qkv, at["w_qkv"]), (acc_so, at["w_so"]),
-                (acc_latent, 0),
-            ],
-            sems, shard, extra,
+        copies = []
+
+        def put(source, row):
+            copies.append(
+                pltpu.make_async_copy(source, flat.at[pl.ds(row, source.shape[0]), :], sems.at[len(copies)])
+            )
+            copies[-1].start()
+
+        write_small(
+            put, stage, low, latent_low, acc_latent, acc_q, acc_o, acc_episode,
+            stacked(dnorm, dnorm_one, dnorm_sa, dnorm_two), stacked(dhid_one, dhid_two),
+            stacked(dout, dout_one, dout_so, dout_two),
         )
-        small = at["w_qkv"] - at["w_q"]
-        first = at["w_q"] - at["episode"]
-        head = at["lat_norms"] - at["episode"]
-        low[0, 0:first, :] = jnp.zeros((first, LANES), BF)
-        norm_grads = jnp.concatenate([dnorm_cross[...], dnorm_one[...], dnorm_sa[...], dnorm_two[...]], axis=0)
-        rows = jnp.concatenate([to_flat(stage, acc_episode[...])[0 : EPISODES * (D // LANES), :], jnp.zeros((head - EPISODES * (D // LANES), LANES), F32)], axis=0)
-        rows = jnp.concatenate([rows, to_flat(stage, norm_grads)], axis=0)
-        low[0, 0 : rows.shape[0], :] = rows.astype(BF)
-        stage[0:D, :] = acc_q[...]
-        even = stage[pl.ds(0, D // 2, stride=2), :]
-        odd = pltpu.roll(stage[pl.ds(1, D // 2, stride=2), :], CH, 1)
-        low[0, first : first + D // 2, :] = jnp.where(lane_half(even.shape, 0), even, odd).astype(BF)
-        low[0, first + D // 2 : first + small, :] = to_flat(stage, acc_o[CH : 2 * CH, :]).astype(BF)
-        hid = to_flat(stage, jnp.concatenate([dhid[...], dhid_two[...]], axis=0))
-        low[1, 0 : hid.shape[0], :] = hid.astype(BF)
-        outs = jnp.concatenate([dout_cross[...], dout_one[...], dout_so[...], dout_two[...]], axis=0)
-        out_rows = 4 * D // LANES
-        low[1, hid.shape[0] : hid.shape[0] + out_rows, :] = to_flat(stage, outs).astype(BF)
-        total = hid.shape[0] + out_rows
-        copies = []
-        for slot, row, count in ((0, at["episode"], first + small), (1, at["hid_bias"], total)):
-            for k, (off, part, to) in enumerate(flat_spans(row, count, shard, extra)):
-                copies.append(
-                    pltpu.make_async_copy(
-                        low.at[slot, pl.ds(off, part), :], flat.at[pl.ds(to, part), :], sems.at[slot, k]
-                    )
-                )
-        for copy in copies:
-            copy.start()
         for copy in copies:
             copy.wait()
         tokens = kv_rows[1]
-        for group in range(0, dkv_t.shape[1] // tokens, 16):
-            copies = []
-            for j in range(min(16, dkv_t.shape[1] // tokens - group)):
-                rows = pl.ds(j * tokens, tokens)
-                low[0, rows, :] = dkv_t[:, (group + j) * tokens : (group + j + 1) * tokens].T
-                to = kv_rows[0] + (group + j) * kv_rows[2]
-                copies.append(
-                    pltpu.make_async_copy(low.at[0, rows, :], flat.at[pl.ds(to, tokens), :], sems.at[0, j])
-                )
-                copies[-1].start()
-            for copy in copies:
-                copy.wait()
+        for j in range(dkv_t.shape[1] // tokens):
+            kv_low[...] = dkv_t[:, j * tokens : (j + 1) * tokens].T
+            copy = pltpu.make_async_copy(kv_low, flat.at[pl.ds(kv_rows[0] + j * tokens, tokens), :], sems.at[0])
+            copy.start()
+            copy.wait()
 
 
 def fixed(*shape):
@@ -1228,14 +1314,15 @@
     )(*args)
 
 
-def reduce_all(flat, master_rows, starts, ends, bias_owner, bias_row, tokens, tok_normed, w_kv, tok_norm):
+def reduce_all(flat, master_rows, starts, ends, bias_owner, bias_row, tokens, tok_normed, w_kv, tok_norm, g1, cross):
     shard = master_rows.shape[0]
     vmem = pl.BlockSpec(memory_space=pltpu.VMEM)
     anywhere = pl.BlockSpec(memory_space=pl.ANY)
     dma = pltpu.SemaphoreType.DMA
     first = [
         pltpu.VMEM((8, STAT_ROWS, LANES), F32), dma((7,)), dma((7,)), pltpu.VMEM((16, LANES), BF),
-        pltpu.VMEM((DIN, LANES), BF), dma((2,)),
+        pltpu.VMEM((DIN, LANES), BF), dma((2,)), pltpu.VMEM(g1.shape, F32), dma((g1.shape[0],)),
+        pltpu.VMEM((8, tokens.shape[0], LANES), BF), dma((16,)),
     ]
     grads = flat.reshape(2, 2, 2, -1, LANES)
     return pl.pallas_call(
@@ -1244,14 +1331,17 @@
             shaped((shard, LANES), BF), shaped((STAT_ROWS, LANES)), shaped(tokens.shape, BF),
             shaped(grads.shape, BF),
         ],
-        in_specs=[vmem, vmem, anywhere] + [vmem] * 5,
+        in_specs=[vmem, vmem, anywhere] + [vmem] * 5 + [anywhere] + [vmem] * len(cross),
         out_specs=[vmem, vmem, vmem, anywhere],
-        scratch_shapes=first + Reduction.scratch(shard),
+        scratch_shapes=first
+        + cross_accumulators(8 * tokens.shape[0])
+        + small_buffers()
+        + Reduction.scratch(shard),
         input_output_aliases={2: 3},
         compiler_params=pltpu.CompilerParams(
-            collective_id=1, has_side_effects=True, vmem_limit_bytes=48 * MIB
+            collective_id=1, has_side_effects=True, vmem_limit_bytes=56 * MIB
         ),
-    )(starts, ends, grads, master_rows, tokens, tok_normed, w_kv, tok_norm)
+    )(starts, ends, grads, master_rows, tokens, tok_normed, w_kv, tok_norm, g1, *cross)
 
 
 def body(tokens, frame_ids, episodes, master, moment_one, moment_two, latent_grad):
@@ -1365,8 +1455,8 @@
         flops=4 * mlp_flops + 4 * attn_flops,
         trans=4 * rows_total * FF,
         scratch=[
-            pltpu.VMEM((LAT, FF), BF), pltpu.VMEM((LAT, FF), BF), pltpu.VMEM((slab, LANES), F32),
-            pltpu.VMEM((slab, LANES), F32), pltpu.VMEM((2, slab, LANES), BF), pltpu.VMEM((LAT, D), BF),
+            pltpu.VMEM((LAT, FF), BF), pltpu.VMEM((LAT, FF), BF), pltpu.VMEM((D, FF), F32), pltpu.VMEM((FF, D), F32),
+            pltpu.VMEM((2048, LANES), F32), pltpu.VMEM((2, slab, LANES), BF), pltpu.VMEM((LAT, D), BF),
             pltpu.VMEM((D, LAT), F32), pltpu.VMEM((LAT, D), F32), pltpu.SemaphoreType.DMA((2, 16)),
         ]
         + shared,
@@ -1382,36 +1472,41 @@
     hot_lanes = jnp.broadcast_to(
         jnp.pad(episode_match.astype(F32), ((0, 0), (0, 16 - EPISODES)))[:, :, None], (frames, 16, LANES)
     )
-    (flat,) = call(
-        functools.partial(backward_kernel, flat_shard, extra, kv_rows),
+    g1, dhid_one, dnorm_sa, dnorm_one, dout_so, dout_one, flat = call(
+        functools.partial(backward_kernel, flat_shard, extra),
         frames,
         [
             rowed(LAT, 3 * D), framed(HEADS, LAT), rowed(LAT, D), rowed(LAT, D), rowed(LAT, D), rowed(LAT, D),
-            rowed(LAT, FF), rowed(LAT, FF), framed(cap, LANES), rowed(LAT, LANES), framed(1, LAT),
-            framed(token_rows_count, LANES), framed(8, LANES), framed(1, D), framed(16, LANES),
-            fixed(LAT, D), fixed(8, D), fixed(D, D), fixed(D, 3 * D), fixed(D, FF), fixed(FF, D), fixed(D, LANES),
-            fixed(LANES, D), fixed(1, FF), fixed(2, D), fixed(1, D), anywhere,
+            rowed(LAT, FF), rowed(LAT, FF), fixed(8, D), fixed(D, D), fixed(D, 3 * D), fixed(D, FF), fixed(FF, D),
+            anywhere,
         ],
-        [(anywhere, shaped(flat_shape, BF))],
+        [
+            (rowed(LAT, D), shaped((rows_total, D))),
+            (kept(1, FF), shaped((1, FF))),
+            (kept(2, D), shaped((2, D))),
+            (kept(2, D), shaped((2, D))),
+            (kept(1, D), shaped((1, D))),
+            (kept(1, D), shaped((1, D))),
+            (anywhere, shaped(flat_shape, BF)),
+        ],
         (
-            qkv, self_lse, mixed, g3, h2, h1, act_one, slope_one, kvf, cross_out, cross_lse, rank, counts,
-            episode_rows, hot_lanes, latent, norms, w_so, w_qkv, up_one, down_one, w_q, w_o, dhid_two, dnorm_two,
-            dout_two, flat,
+            qkv, self_lse, mixed, g3, h2, h1, act_one, slope_one, norms, w_so, w_qkv, up_one, down_one, flat,
         ),
-        flops=2 * mlp_flops + 10 * attn_flops + 6 * score_flops,
+        flops=2 * mlp_flops + 10 * attn_flops,
         trans=rows_total * LAT * HEADS,
         scratch=[
-            pltpu.VMEM((LAT, 3 * D), BF), pltpu.VMEM((slab, LANES), F32), pltpu.VMEM((slab, LANES), F32),
-            pltpu.VMEM((3 * D * D // LANES, LANES), F32), pltpu.VMEM((D * D // LANES, LANES), F32),
-            pltpu.VMEM((LAT * D // LANES, LANES), F32), pltpu.VMEM((D, LANES), F32), pltpu.VMEM((LANES, D), F32),
-            pltpu.VMEM((16, D), F32), pltpu.VMEM((1, FF), F32), pltpu.VMEM((2, D), F32), pltpu.VMEM((2, D), F32),
-            pltpu.VMEM((2, D), F32), pltpu.VMEM((1, D), F32), pltpu.VMEM((1, D), F32), pltpu.VMEM((1, D), F32),
-            pltpu.VMEM((512, LANES), F32), pltpu.VMEM((2, slab, LANES), BF), pltpu.VMEM((LAT, D), BF),
+            pltpu.VMEM((LAT, 3 * D), BF), pltpu.VMEM((D, FF), F32), pltpu.VMEM((FF, D), F32),
+            pltpu.VMEM((D, 3 * D), F32), pltpu.VMEM((D, D), F32),
+            pltpu.VMEM((2048, LANES), F32), pltpu.VMEM((2, slab, LANES), BF), pltpu.VMEM((LAT, D), BF),
             pltpu.VMEM((LAT, D), BF), pltpu.VMEM((LAT, D), BF), pltpu.VMEM((LAT, D), F32),
-            pltpu.VMEM((LANES, total_keys), BF), pltpu.SemaphoreType.DMA((2, 16)),
+            pltpu.SemaphoreType.DMA((2, 16)),
         ],
         limit=60,
-        aliases={26: 0},
+        aliases={13: 6},
+    )
+    cross = (
+        kvf, cross_out, cross_lse, rank, counts, episode_rows, hot_lanes, latent, norms, w_q, w_o,
+        dnorm_one, dnorm_sa, dnorm_two, dhid_one, dhid_two, dout_one, dout_so, dout_two,
     )
     layout = param_layout()
     starts, ends, offset, bias_offset = [], [], 0, 0
@@ -1424,7 +1519,7 @@
     pad = [0] * (16 - len(layout))
     starts = jnp.broadcast_to(jnp.array(starts + pad, jnp.int32)[:, None], (16, LANES))
     ends = jnp.broadcast_to(jnp.array(ends + pad, jnp.int32)[:, None], (16, LANES))
-    opt_rows = 784 if shard_rows % 784 == 0 else shard_rows
+    opt_rows = shard_rows // 2 if shard_rows % 16 == 0 else shard_rows
     opt_steps = shard_rows // opt_rows
     base = (lat_index * shard_rows).astype(jnp.int32).reshape(1)
     smem = pl.BlockSpec(memory_space=pltpu.SMEM)
@@ -1432,9 +1527,29 @@
     bias_owner, bias_at = divmod(bias_offset, shard_len)
     if reach:
         summed, stats, token_grad, unused = reduce_all(
-            flat, master_rows, starts, ends, bias_owner, bias_at // LANES, tokens[0], tok_normed, w_kv, tok_norm
+            flat, master_rows, starts, ends, bias_owner, bias_at // LANES, tokens[0], tok_normed, w_kv, tok_norm,
+            g1.reshape(frames, LAT, D), cross,
         )
     else:
+        (flat,) = call(
+            functools.partial(cross_bwd_kernel, kv_rows),
+            frames,
+            [
+                rowed(LAT, D), framed(cap, LANES), rowed(LAT, LANES), framed(1, LAT), framed(token_rows_count, LANES),
+                framed(8, LANES), framed(1, D), framed(16, LANES), fixed(LAT, D), fixed(8, D), fixed(D, LANES),
+                fixed(LANES, D),
+            ]
+            + [fixed(*part.shape) for part in cross[11:]]
+            + [anywhere],
+            [(anywhere, shaped(flat_shape, BF))],
+            (g1,) + cross + (flat,),
+            flops=6 * score_flops,
+            trans=rows_total * cap,
+            scratch=cross_accumulators(total_keys)
+            + small_buffers()
+            + [pltpu.VMEM((kv_rows[1], LANES), BF), pltpu.SemaphoreType.DMA((8,))],
+            aliases={20: 0},
+        )
         grad_kv = lax.psum_scatter(flat[flat_shard:], "lat", scatter_dimension=0, tiled=True)
         flat = flat[:flat_shard]
         grad_w_kv = t_mm(tok_normed, grad_kv)

time: 389 us -> 347 us (0.89); the launches traced: 389 us -> 343 us
  Pallas kernels: 380 us -> 334 us
    pallas_call x3, Pallas kernels: 224 us -> 172 us  [call(): pl.pallas_call(kernel, grid=(grid,), in_specs=in_specs, out_specs=list(ou...]
    pallas_call x1, Pallas kernels: 80.4 us -> 86.1 us  [reduce_all(): pl.pallas_call(functools.partial(reduce_kernel, bias_owner, bias_row), ou...]
where the time goes in v2:
time: 347 us; the launch traced here: 343 us
  Pallas kernels  334 us (96%)
  local copies, waits for them, and re-layouts  6.75 us (2%)
    pallas_call x3, Pallas kernels, call(): pl.pallas_call(kernel, grid=(grid,), in_specs=in_specs, out_specs=list(ou...  172 us
    pallas_call x1, Pallas kernels, reduce_all(): pl.pallas_call(functools.partial(reduce_kernel, bias_owner, bias_row), ou...  86.1 us
    pallas_call x1, Pallas kernels, begin_all(): pl.pallas_call(functools.partial(begin_kernel, chunks), out_shape=[shaped...  69.4 us

profile of v2, /device:TPU:0, one launch (start us, length us, event | category | flops | bytes accessed | tf_op | source)
XLA Modules:
  0.0 342.5 jit_solution(3710340530244402387)
XLA Ops:
  0.6 0.0 copy-start
  0.7 0.6 copy-done
  1.3 0.1 dynamic-slice_bitcast_fusion
  1.4 0.1 iota_compare_fusion
  1.4 0.6 pad_convert_fusion.hot
  2.0 69.4 %shard_map.152 = (bf16[512,2048]{1,0:T(8,128)(2,1)}, bf16[2048,512]{1,0:T(8,128)(2,1)}, bf16[512,1536]{1,0:T(8,128)(2,1)}, bf16[512,512]{1,0:T(8,128)(2,1)}, bf1...) custom-call(f32[5488,128]{1,0:T(8,128)} %bitcast.17, ...), custom_call_target="tpu_custom_call" | custom-call | tf_op jit(solution)/shard_map/pallas_call | solution.py:815
  71.4 90.5 %shard_map.153 = (f32[2048,512]{1,0:T(8,128)}, bf16[2048,1536]{1,0:T(8,128)(2,1)}, f32[4,8,512]{2,1,0:T(8,128)}, bf16[2048,512]{1,0:T(8,128)(2,1)}, bf16[2048,20...) custom-call(f32[2048,512]{1,0:T(8,128)} %get-tuple-element.57.h1, ...), custom_call_target="tpu_custom_call" | custom-call | flops 42949672960 | bytes 64837632 | tf_op jit(solution)/shard_map/pallas_call | solution.py:1299
  161.9 0.0 copy-start.6
  161.9 0.0 copy-start.5
  161.9 72.3 %shard_map.154 = (f32[2048,512]{1,0:T(8,128)}, f32[1,2048]{1,0:T(1,128)}, f32[2,512]{1,0:T(2,128)}, f32[2,512]{1,0:T(2,128)}, f32[1,512]{1,0:T(1,128)}, /*index=5*/f32[1,512]{1,0:T(1,128)}, bf16[48000,128]{1,0:T(8,128)(2,1)}) custom-call(bf16[2048,1536]{1,0:T(8,128)(2,1)} %get-tuple-element.68.qkv, ...), custom_call_target="tpu_custom_call", output_to_operand_aliasing={{6}: (13, {})} | custom-call | flops 38654705664 | bytes 72912896 | tf_op jit(solution)/shard_map/pallas_call | solution.py:1299
  234.2 0.7 broadcast_in_dim.13.hot
  234.9 0.0 copy-done.6
  234.9 0.7 broadcast_in_dim.11.starts
  235.6 0.0 copy-done.5
  235.6 0.7 broadcast_in_dim.12.ends
  236.3 86.1 %shard_map.155 = (bf16[5488,128]{1,0:T(8,128)(2,1)}, f32[56,128]{1,0:T(8,128)}, bf16[512,256]{1,0:T(8,128)(2,1)}, bf16[2,2,2,6000,128]{4,3,2,1,0:T(8,128)(2,1)}) custom-call(s32[16,128]{1,0:T(8,128)} %broadcast_in_dim.11.starts, s32[16,128]{1,0:T(8,128)} %broadcast_in_dim.12.ends, ...), custom_call_target="tpu_custom_call", output_to_operand_aliasing={{3}: (2, {})} | custom-call | tf_op jit(solution)/shard_map/pallas_call | solution.py:1328
  322.3 0.0 copy-start.4
  322.4 0.0 copy-start.2
  322.4 0.0 copy-start.1
  322.4 9.5 %shard_map.156 = (f32[5488,128]{1,0:T(8,128)}, f32[5488,128]{1,0:T(8,128)}, f32[5488,128]{1,0:T(8,128)}, f32[5488,128]{1,0:T(8,128)}, f32[16,128]{1,0:T(8,128)}) custom-call(s32[1]{0:T(128)} %bitcast.9.base, f32[56,128]{1,0:T(8,128)} %get-tuple-element.99.stats, s32[16,128]{1,0:T(8,128)} %broadcast_in_dim.11.starts, s32[16,128]{1,0:T(8,128)} %broadcast_in_dim.12.ends, ...), custom_call_target="tpu_custom_call" | custom-call | bytes 21127172 | tf_op jit(solution)/shard_map/pallas_call | solution.py:1299
  331.9 0.0 copy-start.3
  331.9 6.2 %shard_map.157 = f32[16,128]{1,0:T(8,128)} custom-call(f32[16,128]{1,0:T(8,128)} %get-tuple-element.105.update_sq, f32[56,128]{1,0:T(8,128)} %get-tuple-element.99.stats), custom_call_target="tpu_custom_call" | custom-call | tf_op jit(solution)/shard_map/pallas_call | solution.py:1592
  338.1 1.3 slice_reduce_fusion
  339.4 0.0 copy-done.4
  339.5 0.6 reshape.69
  340.1 0.0 copy-done.2
  340.1 1.3 copy.23
  341.4 0.0 copy-done.3
  341.4 0.7 copy.24
  342.1 0.0 copy-done.1
  (2 shorter events, 0.0 us)
Async XLA Ops:
  0.6 0.7 copy-start
  161.9 73.0 %copy-start.6 = (s32[16]{0:T(128)S(1)}, s32[16]{0:T(128)}, u32[]{:S(2)}) copy-start(s32[16]{0:T(128)} %constant.22.clone) | copy-start | bytes 196
  161.9 73.7 %copy-start.5 = (s32[16]{0:T(128)S(1)}, s32[16]{0:T(128)}, u32[]{:S(2)}) copy-start(s32[16]{0:T(128)} %constant.23.clone) | copy-start | bytes 196
  322.3 17.1 %copy-start.4 = (f32[56,128]{1,0:T(8,128)S(1)}, f32[56,128]{1,0:T(8,128)}, u32[]{:S(2)}) copy-start(f32[56,128]{1,0:T(8,128)} %get-tuple-element.99.stats) | copy-start | bytes 86020
  322.4 17.7 %copy-start.2 = (bf16[32,64,512]{2,1,0:T(8,128)(2,1)S(1)}, bf16[32,64,512]{2,1,0:T(8,128)(2,1)}, u32[]{:S(2)}) copy-start(bf16[32,64,512]{2,1,0:T(8,128)(2,1)} %get-tuple-element.67) | copy-start | bytes 6291460
  322.4 19.7 %copy-start.1 = (s32[1,32]{1,0:T(1,128)S(1)}, s32[1,32]{1,0:T(1,128)}, u32[]{:S(2)}) copy-start(s32[1,32]{1,0:T(1,128)} %param.11) | copy-start | bytes 388
  331.9 9.5 %copy-start.3 = (bf16[512,256]{1,0:T(8,128)(2,1)S(1)}, bf16[512,256]{1,0:T(8,128)(2,1)}, u32[]{:S(2)}) copy-start(bf16[512,256]{1,0:T(8,128)(2,1)} %get-tuple-element.98) | copy-start | bytes 786436

commit v3 on v2

--- a/solution.py
+++ b/solution.py
@@ -3,6 +3,7 @@
 
 import jax
 import jax.numpy as jnp
+import numpy as np
 from jax import lax
 from jax.experimental import pallas as pl
 from jax.experimental.pallas import tpu as pltpu
@@ -584,26 +585,23 @@
         ref = self.whole.at[pl.ds(pl.multiple_of(block * self.shard + row, 16), count), :]
         return remote(ref, ref, self.send.at[kind, k], self.recv.at[kind, k], target)
 
-    def tick(self, t):
-        n = len(self.chunks)
-        if t < n:
-            self.copy(0, t).start()
-            self.copy(1, t).start()
-        if 0 <= t - 2 < n:
-            self.copy(0, t - 2).wait_recv()
-            for kind in (2, 3, 4):
-                self.copy(kind, t - 2).start()
-        if 0 <= t - 4 < n:
-            self.copy(2, t - 4).wait_recv()
-            self.copy(5, t - 4).start()
-            self.copy(3, t - 4).wait_recv()
-            self.copy(6, t - 4).start()
-        if 0 <= t - 5 < n:
-            for kind in (1, 4, 5, 6):
-                self.copy(kind, t - 5).wait_recv()
-
-    def ticks(self):
-        return len(self.chunks) + 5
+    def play(self, *events):
+        for event in events:
+            kind, k = event[0], int(event[1:])
+            if kind == "a":
+                self.copy(0, k).start()
+                self.copy(1, k).start()
+            elif kind == "b":
+                self.copy(0, k).wait_recv()
+                for way in (2, 3, 4):
+                    self.copy(way, k).start()
+            elif kind == "c":
+                for arrived, onward in ((2, 5), (3, 6)):
+                    self.copy(arrived, k).wait_recv()
+                    self.copy(onward, k).start()
+            else:
+                for way in (1, 4, 5, 6):
+                    self.copy(way, k).wait_recv()
 
     def finish(self):
         for k in range(len(self.chunks)):
@@ -674,7 +672,7 @@
     latent, norms, hid_bias, out_bias, w_q, w_o, w_kv, tok_norm, tok_normed, episode, rank, counts,
     kvf_out, co_out, lse_out, h1,
     whole, stage, all_ids, keys, m_up_one, m_down_one, m_qkv, m_so, m_up_two, m_down_two,
-    episodes_held, send, recv, key_send, key_recv, id_send, id_recv, out_sem,
+    episodes_held, h1_held, h1_sem, send, recv, key_send, key_recv, id_send, id_recv, out_sem,
 ):
     place = Place()
     shard = master.shape[0]
@@ -693,8 +691,7 @@
     own_at = place.me * shard
     for row, count in chunks:
         whole[pl.ds(pl.multiple_of(own_at + row, 16), count), :] = master[row : row + count, :].astype(BF)
-    for t in range(4):
-        gather.tick(t)
+    gather.play("a0", "a1", "a2", "a3", "a4")
 
     for copy in id_copies:
         copy.wait_recv()
@@ -716,8 +713,7 @@
         rank[f] = jnp.where(hit, place_in, -1)
         total = jnp.sum(row_total[:, 0:1], axis=0, keepdims=True).astype(jnp.int32)
         counts[f] = jnp.broadcast_to(total, (8, LANES))
-    for t in range(4, 7):
-        gather.tick(t)
+    gather.play("b0", "b1", "a5", "b2", "c0", "c1", "a6", "d0", "d1")
 
     pair = whole[at["tok_norm"] // 16 * 16 : at["lat_norms"], :].astype(F32)
     pair = pair[at["tok_norm"] % 16 : at["tok_norm"] % 16 + 4, :]
@@ -734,35 +730,36 @@
     tok_normed[...] = normed
     keys[pl.ds(place.me, 1)] = mm(normed, w_kv[...]).astype(BF)[None]
     exchange.step(0)
+    gather.play("a7", "a8", "b3", "c2")
     norms[...] = small_matrix(whole, at["lat_norms"], stage, 8, D)
     hid_bias[...] = small_matrix(whole, at["hid_bias"], stage, 2, FF)
     out_bias[...] = small_matrix(whole, at["out_bias"], stage, 4, D)
     episode_rows = mm(hot[...], small_matrix(whole, at["episode"], stage, 16, D).astype(BF))
-    gather.tick(7)
+    gather.play("b4", "c3", "d2", "b5", "c4", "d3", "b6")
     exchange.step(1)
+    gather.play("a9", "a10", "c5", "d4", "c6", "d5")
     packed = whole[at["w_q"] : at["w_q"] + D // 2, :].astype(F32)
     stage[pl.ds(0, D // 2, stride=2), :] = packed
     stage[pl.ds(1, D // 2, stride=2), :] = pltpu.roll(packed, CH, 1)
     w_q[...] = keep_half(stage[0:D, :], 0).astype(BF)
     w_o[0:CH, :] = jnp.zeros((CH, D), BF)
     w_o[CH : 2 * CH, :] = small_matrix(whole, at["w_o"], stage, CH, D).astype(BF)
-    gather.tick(8)
     exchange.step(2)
-    for t in range(9, 12):
-        gather.tick(t)
+    gather.play("a11", "b7", "d6")
     exchange.step(3)
     relayout(whole, 0, stage, latent, LAT, D)
 
     chunk = 8 * LANES
     episodes_held[...] = episode_rows[0:8, :]
+    before = [("b8",), ("b9", "d7"), ("b10", "d8"), ("b11", "d9")]
+    midway = [("c7",), ("c8",), ("c9",), ("c10",)]
+
+    def play(frame, parts):
+        for step, events in enumerate(parts):
+            pl.when(frame == step)(functools.partial(gather.play, *events))
 
     def attend(f, carry):
-        for tick in range(12, gather.ticks()):
-
-            @pl.when(f == (tick - 12) * frames // (gather.ticks() - 12))
-            def _(tick=tick):
-                gather.tick(tick)
-
+        play(f, before)
         row = episodes_held[pl.ds(f, 1), :]
         start = latent[...].astype(F32) + row
         episode[pl.ds(f, 1)] = row[None]
@@ -772,15 +769,18 @@
             return acc + mm(sel, keys[pl.ds(2 * j, 2)].reshape(chunk, LANES))
 
         kvf = lax.fori_loop(0, n // 8, pick, jnp.zeros((cap, LANES), F32)).astype(BF)
+        play(f, midway)
         co, lse = cross_attend(start, norms, w_q, kvf, counts[f, 0:1, 0:1])
         rows = pl.ds(pl.multiple_of(f * LAT, LAT), LAT)
-        h1[rows, :] = start + mm(co, w_o[...]) + out_bias[0:1, :]
+        h1_held[f] = start + mm(co, w_o[...]) + out_bias[0:1, :]
+        pltpu.make_async_copy(h1_held.at[f], h1.at[rows, :], h1_sem.at[f]).start()
         kvf_out[f] = kvf
         co_out[rows, :] = co
         lse_out[f] = lse
         return carry
 
     lax.fori_loop(0, frames, attend, 0)
+    gather.play("c11", "d10", "d11")
 
     big = (
         (up_one, m_up_one, at["w_up"], D, FF),
@@ -797,6 +797,8 @@
         outs[-1].start()
     for copy in outs:
         copy.wait()
+    for f in range(frames):
+        pltpu.make_async_copy(h1_held.at[f], h1.at[f * LAT : (f + 1) * LAT, :], h1_sem.at[f]).wait()
     for copy in id_copies:
         copy.wait_send()
     exchange.finish()
@@ -834,7 +836,7 @@
             shaped((frames * LAT, D)),
         ],
         in_specs=[vmem] * 4,
-        out_specs=[anywhere] * 6 + [vmem] * 16,
+        out_specs=[anywhere] * 6 + [vmem] * 15 + [anywhere],
         scratch_shapes=[
             pltpu.VMEM((8 * shard, LANES), BF),
             pltpu.VMEM((2048, LANES), F32),
@@ -844,6 +846,8 @@
         + [pltpu.VMEM(m, BF) for m in matrices]
         + [
             pltpu.VMEM((8, D), F32),
+            pltpu.VMEM((frames, LAT, D), F32),
+            dma((frames,)),
             dma((7, len(chunks))), dma((7, len(chunks))), dma((8,)), dma((8,)), dma((7,)), dma((7,)), dma((6,)),
         ],
         compiler_params=pltpu.CompilerParams(
@@ -871,8 +875,8 @@
     normed_ref[...] = (xhat * gain + bias).astype(BF)
     total_ref[...] = rows + down_bias
 
-    for c in range(FF // FCHUNK):
-        at = slice(c * FCHUNK, (c + 1) * FCHUNK)
+    for c in range(2):
+        at = slice(c * FF // 2, (c + 1) * FF // 2)
         act, slope = gelu_pair(mm(normed_ref[...], w_up[:, at]) + up_bias[:, at])
         act = act.astype(BF)
         act_ref[:, at] = act
@@ -1007,12 +1011,39 @@
         lax.fori_loop(0, self.frames, step, 0)
 
 
+class Late:
+    def __init__(self, step, sources, refs, sems):
+        self.first = step == 0
+        self.copies = [
+            pltpu.make_async_copy(src, ref, sems.at[k]) for k, (src, ref) in enumerate(zip(sources, refs))
+        ]
+
+        @pl.when(self.first)
+        def _():
+            for copy in self.copies:
+                copy.start()
+
+    def need(self, *which):
+        @pl.when(self.first)
+        def _():
+            for k in which:
+                self.copies[k].wait()
+
+
 def forward_kernel(
-    reach, shard, extra, h1, grad, norms, hid_bias, out_bias, up_one, down_one, w_qkv, w_so, up_two, down_two,
+    reach, shard, extra, h1, grad, norms, hid_bias, out_bias, up_one, down_one, *rest,
+):
+    forward_body(reach, shard, extra, h1, grad, norms, hid_bias, out_bias, up_one, down_one, rest[:4], *rest[4:])
+
+
+def forward_body(
+    reach, shard, extra, h1, grad, norms, hid_bias, out_bias, up_one, down_one, late_sources,
     h2_out, qkv, lse_out, mixed_out, act_one, slope_one, latents, g3, dhid, dnorm, dout, flat,
-    act_two, slope_two, acc_up, acc_down, stage, low, normed, mixed_t, work, sems, *shared,
+    act_two, slope_two, acc_up, acc_down, stage, low, normed, mixed_t, work, sems,
+    w_qkv, w_so, up_two, down_two, late_sems, *shared,
 ):
     step = pl.program_id(0)
+    late = Late(step, late_sources, (w_qkv, w_so, up_two, down_two), late_sems)
     if reach:
         place = Place()
         traffic = FrameExchange(place, grad, shared[0], shared[1], latents, shared[2:])
@@ -1026,6 +1057,8 @@
     xhat, unused = norm_stats(h2_out[...])
     normed[...] = (xhat * norms[4:5, :] + norms[5:6, :]).astype(BF)
 
+    late.need(0)
+
     def project(c, carry):
         at = chunk_of(c)
         qkv[:, at] = mm(normed[...], w_qkv[:, at]).astype(BF)
@@ -1036,10 +1069,11 @@
 
     ones = jnp.ones((16, LAT), BF)
 
-    def attend(pair, carry):
-        query_pair = qkv[:, chunk_of(pair, LANES)] * scale
-        key_pair = qkv[:, chunk_of(pair + D // LANES, LANES)]
-        value_t = qkv[:, chunk_of(pair + 2 * D // LANES, LANES)].T
+    for pair in range(HEADS // 2):
+        base = pair * LANES
+        query_pair = qkv[:, base : base + LANES] * scale
+        key_pair = qkv[:, D + base : D + base + LANES]
+        value_t = qkv[:, 2 * D + base : 2 * D + base + LANES].T
         for half in range(2):
             scores = mm_t(key_pair, keep_half(query_pair, half))
             top = jnp.max(scores, axis=0, keepdims=True)
@@ -1047,12 +1081,10 @@
             values = jnp.concatenate([value_t[half * HEAD_DIM : (half + 1) * HEAD_DIM, :], ones], axis=0)
             product = mm(values, terms)
             total = product[HEAD_DIM : HEAD_DIM + 1, :]
-            lse_out[0, pl.ds(2 * pair + half, 1), :] = top + jnp.log(total)
-            at = pl.ds(pl.multiple_of(pair * LANES + half * HEAD_DIM, HEAD_DIM), HEAD_DIM)
-            mixed_t[at, :] = product[0:HEAD_DIM, :] * (1.0 / total)
-        return carry
-
-    lax.fori_loop(0, HEADS // 2, attend, 0)
+            head = 2 * pair + half
+            lse_out[0, head : head + 1, :] = top + jnp.log(total)
+            mixed_t[head * HEAD_DIM : (head + 1) * HEAD_DIM, :] = product[0:HEAD_DIM, :] * (1.0 / total)
+    late.need(1, 2, 3)
     mixed = mixed_t[...].T.astype(BF)
     mixed_out[...] = mixed
     h3 = h2_out[...] + mm(mixed, w_so[...]) + out_bias[2:3, :]
@@ -1082,11 +1114,13 @@
 
 
 def backward_kernel(
-    shard, extra, qkv, lse, mixed, g3, h2, h1, act_one, slope_one, norms, w_so, w_qkv, up_one, down_one, flat_in,
+    shard, extra, qkv, lse, mixed, g3, h2, h1, act_one, slope_one, norms, w_so, src_qkv, src_up, src_down, flat_in,
     g1, dhid, dnorm_sa, dnorm_one, dout_so, dout_one, flat,
     dqkv, acc_up, acc_down, acc_qkv, acc_so, stage, low, normed, grad_mixed, grad_low, work, sems,
+    w_qkv, up_one, down_one, late_sems,
 ):
     step = pl.program_id(0)
+    late = Late(step, (src_qkv, src_up, src_down), (w_qkv, up_one, down_one), late_sems)
     clear(
         step == 0,
         (acc_up, acc_down, acc_qkv, acc_so, dhid, dnorm_sa, dnorm_one, dout_so, dout_one),
@@ -1125,6 +1159,7 @@
         return carry
 
     lax.fori_loop(0, HEADS // 2, attend, 0)
+    late.need(0, 1, 2)
     xhat, rstd = norm_stats(h2[...])
     normed[...] = (xhat * norms[4:5, :] + norms[5:6, :]).astype(BF)
     work[...] = jnp.zeros(work.shape, F32)
@@ -1435,8 +1470,8 @@
         frames,
         [
             rowed(LAT, D), grad_spec, fixed(8, D), fixed(2, FF), fixed(4, D), fixed(D, FF), fixed(FF, D),
-            fixed(D, 3 * D), fixed(D, D), fixed(D, FF), fixed(FF, D),
-        ],
+        ]
+        + [anywhere] * 4,
         [
             (rowed(LAT, D), shaped((rows_total, D))),
             (rowed(LAT, 3 * D), shaped((rows_total, 3 * D), BF)),
@@ -1458,6 +1493,8 @@
             pltpu.VMEM((LAT, FF), BF), pltpu.VMEM((LAT, FF), BF), pltpu.VMEM((D, FF), F32), pltpu.VMEM((FF, D), F32),
             pltpu.VMEM((2048, LANES), F32), pltpu.VMEM((2, slab, LANES), BF), pltpu.VMEM((LAT, D), BF),
             pltpu.VMEM((D, LAT), F32), pltpu.VMEM((LAT, D), F32), pltpu.SemaphoreType.DMA((2, 16)),
+            pltpu.VMEM((D, 3 * D), BF), pltpu.VMEM((D, D), BF), pltpu.VMEM((D, FF), BF), pltpu.VMEM((FF, D), BF),
+            pltpu.SemaphoreType.DMA((4,)),
         ]
         + shared,
         limit=62,
@@ -1477,9 +1514,9 @@
         frames,
         [
             rowed(LAT, 3 * D), framed(HEADS, LAT), rowed(LAT, D), rowed(LAT, D), rowed(LAT, D), rowed(LAT, D),
-            rowed(LAT, FF), rowed(LAT, FF), fixed(8, D), fixed(D, D), fixed(D, 3 * D), fixed(D, FF), fixed(FF, D),
-            anywhere,
-        ],
+            rowed(LAT, FF), rowed(LAT, FF), fixed(8, D), fixed(D, D),
+        ]
+        + [anywhere] * 4,
         [
             (rowed(LAT, D), shaped((rows_total, D))),
             (kept(1, FF), shaped((1, FF))),
@@ -1500,6 +1537,8 @@
             pltpu.VMEM((2048, LANES), F32), pltpu.VMEM((2, slab, LANES), BF), pltpu.VMEM((LAT, D), BF),
             pltpu.VMEM((LAT, D), BF), pltpu.VMEM((LAT, D), BF), pltpu.VMEM((LAT, D), F32),
             pltpu.SemaphoreType.DMA((2, 16)),
+            pltpu.VMEM((D, 3 * D), BF), pltpu.VMEM((D, FF), BF), pltpu.VMEM((FF, D), BF),
+            pltpu.SemaphoreType.DMA((3,)),
         ],
         limit=60,
         aliases={13: 6},
@@ -1517,8 +1556,7 @@
         offset += math.prod(shape)
         ends.append(offset // LANES)
     pad = [0] * (16 - len(layout))
-    starts = jnp.broadcast_to(jnp.array(starts + pad, jnp.int32)[:, None], (16, LANES))
-    ends = jnp.broadcast_to(jnp.array(ends + pad, jnp.int32)[:, None], (16, LANES))
+    starts, ends = (np.tile(np.array(v + pad, np.int32)[:, None], (1, LANES)) for v in (starts, ends))
     opt_rows = shard_rows // 2 if shard_rows % 16 == 0 else shard_rows
     opt_steps = shard_rows // opt_rows
     base = (lat_index * shard_rows).astype(jnp.int32).reshape(1)

time: 347 us -> 334 us (0.963)
  Pallas kernels: 334 us -> 322 us
    pallas_call x3, Pallas kernels: 172 us -> 165 us  [call(): pl.pallas_call(kernel, grid=(grid,), in_specs=in_specs, out_specs=list(ou...]
    pallas_call x1, Pallas kernels: 69.4 us -> 65 us  [begin_all(): pl.pallas_call(functools.partial(begin_kernel, chunks), out_shape=[shaped...]
where the time goes in v3:
time: 334 us; the launch traced here: 329 us
  Pallas kernels  322 us (96%)
  local copies, waits for them, and re-layouts  5.4 us (2%)
    pallas_call x3, Pallas kernels, call(): pl.pallas_call(kernel, grid=(grid,), in_specs=in_specs, out_specs=list(ou...  165 us
    pallas_call x1, Pallas kernels, reduce_all(): pl.pallas_call(functools.partial(reduce_kernel, bias_owner, bias_row), ou...  85.7 us
    pallas_call x1, Pallas kernels, begin_all(): pl.pallas_call(functools.partial(begin_kernel, chunks), out_shape=[shaped...  65 us

profile of v3, /device:TPU:0, one launch (start us, length us, event | category | flops | bytes accessed | tf_op | source)
XLA Modules:
  0.0 329.2 jit_solution(2003521499175907287)
XLA Ops:
  0.6 0.0 copy-start
  0.7 0.6 copy-done
  1.3 0.1 dynamic-slice_bitcast_fusion
  1.4 0.1 iota_compare_fusion
  1.4 0.6 pad_convert_fusion.hot
  2.0 65.0 %shard_map.152 = (bf16[512,2048]{1,0:T(8,128)(2,1)}, bf16[2048,512]{1,0:T(8,128)(2,1)}, bf16[512,1536]{1,0:T(8,128)(2,1)}, bf16[512,512]{1,0:T(8,128)(2,1)}, bf1...) custom-call(f32[5488,128]{1,0:T(8,128)} %bitcast.17, ...), custom_call_target="tpu_custom_call" | custom-call | tf_op jit(solution)/shard_map/pallas_call | solution.py:817
  67.1 85.2 %shard_map.153 = (f32[2048,512]{1,0:T(8,128)}, bf16[2048,1536]{1,0:T(8,128)(2,1)}, f32[4,8,512]{2,1,0:T(8,128)}, bf16[2048,512]{1,0:T(8,128)(2,1)}, bf16[2048,20...) custom-call(f32[2048,512]{1,0:T(8,128)} %get-tuple-element.57.h1, ...), custom_call_target="tpu_custom_call" | custom-call | flops 42949672960 | bytes 64837632 | tf_op jit(solution)/shard_map/pallas_call | solution.py:1334
  152.2 70.5 %shard_map.154 = (f32[2048,512]{1,0:T(8,128)}, f32[1,2048]{1,0:T(1,128)}, f32[2,512]{1,0:T(2,128)}, f32[2,512]{1,0:T(2,128)}, f32[1,512]{1,0:T(1,128)}, /*index=5*/f32[1,512]{1,0:T(1,128)}, bf16[48000,128]{1,0:T(8,128)(2,1)}) custom-call(bf16[2048,1536]{1,0:T(8,128)(2,1)} %get-tuple-element.68.qkv, ...), custom_call_target="tpu_custom_call", output_to_operand_aliasing={{6}: (13, {})} | custom-call | flops 38654705664 | bytes 72912896 | tf_op jit(solution)/shard_map/pallas_call | solution.py:1334
  222.8 0.7 broadcast_in_dim.7.hot
  223.5 85.7 %shard_map.155 = (bf16[5488,128]{1,0:T(8,128)(2,1)}, f32[56,128]{1,0:T(8,128)}, bf16[512,256]{1,0:T(8,128)(2,1)}, bf16[2,2,2,6000,128]{4,3,2,1,0:T(8,128)(2,1)}) custom-call(s32[16,128]{1,0:T(8,128)} %constant.22.clone.starts, s32[16,128]{1,0:T(8,128)} %constant.23.clone.ends, ...), custom_call_target="tpu_custom_call", output_to_operand_aliasing={{3}: (2, {})} | custom-call | tf_op jit(solution)/shard_map/pallas_call | solution.py:1363
  309.2 0.0 copy-start.4
  309.2 0.0 copy-start.2
  309.2 0.0 copy-start.1
  309.2 9.6 %shard_map.156 = (f32[5488,128]{1,0:T(8,128)}, f32[5488,128]{1,0:T(8,128)}, f32[5488,128]{1,0:T(8,128)}, f32[5488,128]{1,0:T(8,128)}, f32[16,128]{1,0:T(8,128)}) custom-call(s32[1]{0:T(128)} %bitcast.9.base, f32[56,128]{1,0:T(8,128)} %get-tuple-element.99.stats, s32[16,128]{1,0:T(8,128)} %constant.22.clone.starts, s32[16,128]{1,0:T(8,128)} %constant.23.clone.ends, ...), custom_call_target="tpu_custom_call" | custom-call | bytes 21127172 | tf_op jit(solution)/shard_map/pallas_call | solution.py:1334
  318.9 0.0 copy-start.3
  318.9 6.2 %shard_map.157 = f32[16,128]{1,0:T(8,128)} custom-call(f32[16,128]{1,0:T(8,128)} %get-tuple-element.105.update_sq, f32[56,128]{1,0:T(8,128)} %get-tuple-element.99.stats), custom_call_target="tpu_custom_call" | custom-call | tf_op jit(solution)/shard_map/pallas_call | solution.py:1630
  325.1 1.3 slice_reduce_fusion
  326.4 0.0 copy-done.4
  326.4 0.6 reshape.67
  327.0 0.0 copy-done.2
  327.0 1.3 copy.23
  328.3 0.0 copy-done.3
  328.3 0.7 copy.24
  329.0 0.0 copy-done.1
  (2 shorter events, 0.0 us)
Async XLA Ops:
  0.6 0.7 copy-start
  309.2 17.2 %copy-start.4 = (f32[56,128]{1,0:T(8,128)S(1)}, f32[56,128]{1,0:T(8,128)}, u32[]{:S(2)}) copy-start(f32[56,128]{1,0:T(8,128)} %get-tuple-element.99.stats) | copy-start | bytes 86020
  309.2 17.8 %copy-start.2 = (bf16[32,64,512]{2,1,0:T(8,128)(2,1)S(1)}, bf16[32,64,512]{2,1,0:T(8,128)(2,1)}, u32[]{:S(2)}) copy-start(bf16[32,64,512]{2,1,0:T(8,128)(2,1)} %get-tuple-element.67) | copy-start | bytes 6291460
  309.2 19.8 %copy-start.1 = (s32[1,32]{1,0:T(1,128)S(1)}, s32[1,32]{1,0:T(1,128)}, u32[]{:S(2)}) copy-start(s32[1,32]{1,0:T(1,128)} %param.11) | copy-start | bytes 388
  318.9 9.5 %copy-start.3 = (bf16[512,256]{1,0:T(8,128)(2,1)S(1)}, bf16[512,256]{1,0:T(8,128)(2,1)}, u32[]{:S(2)}) copy-start(bf16[512,256]{1,0:T(8,128)(2,1)} %get-tuple-element.98) | copy-start | bytes 786436

commit v4 on v3

--- a/solution.py
+++ b/solution.py
@@ -16,6 +16,7 @@
 HEADS = 8
 HEAD_DIM = 64
 FF = 2048
+FRAMES = 32
 EPISODES = 11
 NPARAM = 5619712
 LANES = 128
@@ -181,16 +182,7 @@
     return mm(hot, high) + mm(hot, low)
 
 
-def grad_stats_kernel(base, starts, ends, summed, master, grad_sq, weight_sq):
-    i = pl.program_id(0)
-    rows = master.shape[0]
-    hot = segment_hot(starts, ends, base[0] + i * rows, rows)
-    grad = summed[...].astype(F32)
-    accumulate(i == 0, grad_sq, col_sum(grad * grad))
-    accumulate(i == 0, weight_sq, segment_sums(hot, master[...] * master[...]))
-
-
-def lamb_kernel(base, stats, starts, ends, summed, master, one, two, grad_out, update_out, one_out, two_out, update_sq):
+def lamb_kernel(base, stats, starts, ends, summed, master, one, two, grad_out, update_out, one_out, two_out, norms_sq, bias):
     i = pl.program_id(0)
     rows = master.shape[0]
     hot = segment_hot(starts, ends, base[0] + i * rows, rows)
@@ -207,7 +199,10 @@
     second_hat = new_two * (1.0 / (1.0 - beta_two**lamb_step))
     update = first_hat / (jnp.sqrt(second_hat) + adam_eps) + decay_rate * master[...]
     update_out[...] = update
-    accumulate(i == 0, update_sq, segment_sums(hot, update * update))
+    accumulate(i == 0, norms_sq, segment_sums(hot, jnp.concatenate([update * update, master[...] * master[...]], axis=1)))
+    for j in range(2 * FF // LANES):
+        r, c = divmod(j, FF // LANES)
+        bias[r : r + 1, c * LANES : (c + 1) * LANES] = stats[8 + j : 9 + j, :]
 
 
 BATCH = 256
@@ -248,7 +243,10 @@
     barrier = pltpu.get_barrier_semaphore()
     for device in devices:
         pl.semaphore_signal(barrier, inc=1, device_id=device, device_id_type=MESH)
-    pl.semaphore_wait(barrier, len(devices))
+
+
+def met(devices):
+    pl.semaphore_wait(pltpu.get_barrier_semaphore(), len(devices))
 
 
 def added(left, right):
@@ -425,7 +423,7 @@
         copy.wait()
 
 
-STAT_ROWS = 56
+STAT_ROWS = 40
 
 
 def token_backward(grad_kv, tokens, tok_normed, w_kv, tok_norm, token_grad, kv_grad, edge):
@@ -440,7 +438,7 @@
 
 
 def reduce_kernel(
-    bias_owner, bias_at, starts, ends, unused_flat, master, tokens, tok_normed, w_kv, tok_norm,
+    shard, bias_owner, bias_at, unused_flat, tokens, tok_normed, w_kv, tok_norm,
     g1, kvf, co, lse, rank, count, episode, hot, latent, norms, w_q, w_o,
     dnorm_one, dnorm_sa, dnorm_two, dhid_one, dhid_two, dout_one, dout_so, dout_two,
     summed, stats, token_grad, grads, *scratch,
@@ -449,14 +447,16 @@
     block, block_send, block_recv, edge, kv_grad, edge_sem, g1_held, g1_sem, kv_low, kv_sem = scratch[:10]
     accs, (stage, low, latent_low), engine = scratch[10:17], scratch[17:20], scratch[20:]
     acc_latent, acc_q, acc_o, acc_episode, dnorm, dout, dkv_t = accs
-    shard, frames = master.shape[0], kvf.shape[0]
+    frames = kvf.shape[0]
     red = Reduction(place, shard, grads, summed, engine[:7], engine[7:])
     frame_copies = [pltpu.make_async_copy(g1.at[f], g1_held.at[f], g1_sem.at[f]) for f in range(frames)]
     for copy in frame_copies:
         copy.start()
-    greet([place.lat_other(d) for d in range(1, 8)] + [place.z_other(d) for d in (1, 2, 3)])
+    partners = [place.lat_other(d) for d in range(1, 8)] + [place.z_other(d) for d in (1, 2, 3)]
+    greet(partners)
     for ref in accs:
         ref[...] = jnp.zeros_like(ref)
+    met(partners)
 
     def run(first, last):
         lax.fori_loop(first, last, lambda t, c: (red.tick(t), c)[1], 0)
@@ -508,20 +508,15 @@
     run(ready, ready + 2)
     for copy in writes:
         copy.wait()
-    step = 784
-    weight_sq = jnp.zeros((16, LANES), F32)
-    for j in range(shard // step):
-        hot_rows = segment_hot(starts, ends, place.me * shard + j * step, step)
-        part = master[j * step : (j + 1) * step, :]
-        weight_sq = weight_sq + segment_sums(hot_rows, part * part)
     run(ready + 2, red.ticks())
     grad_sq = jnp.zeros((1, LANES), F32)
+    step = 784
     for j in range(shard // step):
         part = summed[j * step : (j + 1) * step, :].astype(F32)
         grad_sq = grad_sq + col_sum(part * part)
     bias = summed[bias_at : bias_at + 2 * FF // LANES, :].astype(F32)
     bias = jnp.where(place.me == bias_owner, bias, 0.0)
-    head = jnp.concatenate([grad_sq, jnp.zeros((7, LANES), F32), weight_sq, bias], axis=0)
+    head = jnp.concatenate([grad_sq, jnp.zeros((7, LANES), F32), bias], axis=0)
     block[pl.ds(place.me, 1)] = head[None]
     share_all(place, block, block_send, block_recv)
     total = block[0]
@@ -531,17 +526,20 @@
     red.finish()
 
 
-def trust_kernel(update_sq, stats, trust, block, send, recv):
+def trust_kernel(norms_sq, trust, block, send, recv):
     place = Place()
-    greet([place.lat_other(d) for d in range(1, 8)])
-    block[pl.ds(place.me, 1)] = update_sq[...][None]
+    partners = [place.lat_other(d) for d in range(1, 8)]
+    greet(partners)
+    block[pl.ds(place.me, 1)] = norms_sq[...][None]
+    met(partners)
     share_all(place, block, send, recv)
     total = block[0]
     for s in range(1, 8):
         total = total + block[s]
-    update_norm = jnp.sqrt(jnp.sum(total, axis=1, keepdims=True))
-    weight_norm = jnp.sqrt(jnp.sum(stats[8:24, :], axis=1, keepdims=True))
-    trust[...] = jnp.broadcast_to(weight_norm / (update_norm + 1e-06), (16, LANES))
+    update_sq = jnp.sum(total[:, 0:LANES].T, axis=0, keepdims=True)
+    weight_sq = jnp.sum(total[:, LANES : 2 * LANES].T, axis=0, keepdims=True)
+    ratio = jnp.sqrt(weight_sq) / (jnp.sqrt(update_sq) + 1e-06)
+    trust[...] = ratio[:, 0 : trust.shape[1]]
 
 
 def relayout(whole, row, stage, dst, rows, cols):
@@ -667,10 +665,10 @@
 
 
 def begin_kernel(
-    chunks, master, tokens, ids, hot,
+    chunks, master, tokens, ids, episodes,
     up_one, down_one, qkv_w, so_w, up_two, down_two,
     latent, norms, hid_bias, out_bias, w_q, w_o, w_kv, tok_norm, tok_normed, episode, rank, counts,
-    kvf_out, co_out, lse_out, h1,
+    kvf_out, co_out, lse_out, hot_lanes, h1,
     whole, stage, all_ids, keys, m_up_one, m_down_one, m_qkv, m_so, m_up_two, m_down_two,
     episodes_held, h1_held, h1_sem, send, recv, key_send, key_recv, id_send, id_recv, out_sem,
 ):
@@ -680,17 +678,19 @@
     gather = Gather(place, whole, shard, chunks, send, recv)
     exchange = KeyExchange(place, keys, key_send, key_recv)
     at = flat_rows_of()
-    greet([place.lat_other(d) for d in range(1, 8)] + [place.z_near])
+    partners = [place.lat_other(d) for d in range(1, 8)] + [place.z_near]
+    greet(partners)
     all_ids[pl.ds(place.me, 1)] = ids[...][None]
     id_copies = [
         remote(all_ids.at[place.me], all_ids.at[place.me], id_send.at[d - 1], id_recv.at[d - 1], place.lat_other(d))
         for d in range(1, 8)
     ]
-    for copy in id_copies:
-        copy.start()
     own_at = place.me * shard
     for row, count in chunks:
         whole[pl.ds(pl.multiple_of(own_at + row, 16), count), :] = master[row : row + count, :].astype(BF)
+    met(partners)
+    for copy in id_copies:
+        copy.start()
     gather.play("a0", "a1", "a2", "a3", "a4")
 
     for copy in id_copies:
@@ -734,7 +734,14 @@
     norms[...] = small_matrix(whole, at["lat_norms"], stage, 8, D)
     hid_bias[...] = small_matrix(whole, at["hid_bias"], stage, 2, FF)
     out_bias[...] = small_matrix(whole, at["out_bias"], stage, 4, D)
-    episode_rows = mm(hot[...], small_matrix(whole, at["episode"], stage, 16, D).astype(BF))
+    mine = lax.broadcasted_iota(jnp.int32, (16, FRAMES), 0) + place.me * frames
+    mine = mine == lax.broadcasted_iota(jnp.int32, (16, FRAMES), 1)
+    own = jnp.sum(jnp.where(mine, episodes[...].astype(F32), 0.0), axis=1, keepdims=True)
+    hot = jnp.where(lax.broadcasted_iota(jnp.int32, (16, 16), 1).astype(F32) == own, 1.0, 0.0).astype(BF)
+    for f in range(frames):
+        row = lax.broadcasted_iota(jnp.int32, (16, LANES), 0).astype(F32)
+        hot_lanes[f] = jnp.where(row == own[f : f + 1, 0:1], 1.0, 0.0)
+    episode_rows = mm(hot, small_matrix(whole, at["episode"], stage, 16, D).astype(BF))
     gather.play("b4", "c3", "d2", "b5", "c4", "d3", "b6")
     exchange.step(1)
     gather.play("a9", "a10", "c5", "d4", "c6", "d5")
@@ -805,7 +812,7 @@
     gather.finish()
 
 
-def begin_all(master_rows, token_rows, ids, hot, frames, cap):
+def begin_all(master_rows, token_rows, ids, episodes, frames, cap):
     shard = master_rows.shape[0]
     tokens = token_rows.shape[0]
     total = 8 * tokens
@@ -833,10 +840,11 @@
             shaped((frames, cap, LANES), BF),
             shaped((frames * LAT, LANES), BF),
             shaped((frames, 1, LAT)),
+            shaped((frames, 16, LANES)),
             shaped((frames * LAT, D)),
         ],
         in_specs=[vmem] * 4,
-        out_specs=[anywhere] * 6 + [vmem] * 15 + [anywhere],
+        out_specs=[anywhere] * 6 + [vmem] * 16 + [anywhere],
         scratch_shapes=[
             pltpu.VMEM((8 * shard, LANES), BF),
             pltpu.VMEM((2048, LANES), F32),
@@ -853,7 +861,7 @@
         compiler_params=pltpu.CompilerParams(
             collective_id=3, has_side_effects=True, vmem_limit_bytes=56 * MIB
         ),
-    )(master_rows, token_rows, ids, hot)
+    )(master_rows, token_rows, ids, episodes)
 
 
 FCHUNK = 512
@@ -983,8 +991,11 @@
         dst = self.result.at[self.p.me * self.frames + f]
         return pltpu.make_async_copy(self.held.at[f, self.block(self.p.me), :], dst, self.own_out.at[f])
 
+    def partners(self):
+        return [self.p.lat_other(d) for d in range(1, 8)]
+
     def begin(self):
-        greet([self.p.lat_other(d) for d in range(1, 8)])
+        met(self.partners())
         for f in range(self.frames):
             self.own_arriving(f).start()
             for d in range(1, 8):
@@ -1047,7 +1058,7 @@
     if reach:
         place = Place()
         traffic = FrameExchange(place, grad, shared[0], shared[1], latents, shared[2:])
-        pl.when(step == 0)(traffic.begin)
+        pl.when(step == 0)(lambda: greet(traffic.partners()))
         grad = shared[0].at[step]
     clear(step == 0, (acc_up, acc_down, dhid, dnorm, dout))
     feed_forward(
@@ -1058,6 +1069,8 @@
     normed[...] = (xhat * norms[4:5, :] + norms[5:6, :]).astype(BF)
 
     late.need(0)
+    if reach:
+        pl.when(step == 0)(traffic.begin)
 
     def project(c, carry):
         at = chunk_of(c)
@@ -1349,8 +1362,7 @@
     )(*args)
 
 
-def reduce_all(flat, master_rows, starts, ends, bias_owner, bias_row, tokens, tok_normed, w_kv, tok_norm, g1, cross):
-    shard = master_rows.shape[0]
+def reduce_all(flat, shard, bias_owner, bias_row, tokens, tok_normed, w_kv, tok_norm, g1, cross):
     vmem = pl.BlockSpec(memory_space=pltpu.VMEM)
     anywhere = pl.BlockSpec(memory_space=pl.ANY)
     dma = pltpu.SemaphoreType.DMA
@@ -1361,22 +1373,22 @@
     ]
     grads = flat.reshape(2, 2, 2, -1, LANES)
     return pl.pallas_call(
-        functools.partial(reduce_kernel, bias_owner, bias_row),
+        functools.partial(reduce_kernel, shard, bias_owner, bias_row),
         out_shape=[
             shaped((shard, LANES), BF), shaped((STAT_ROWS, LANES)), shaped(tokens.shape, BF),
             shaped(grads.shape, BF),
         ],
-        in_specs=[vmem, vmem, anywhere] + [vmem] * 5 + [anywhere] + [vmem] * len(cross),
+        in_specs=[anywhere] + [vmem] * 4 + [anywhere] + [vmem] * len(cross),
         out_specs=[vmem, vmem, vmem, anywhere],
         scratch_shapes=first
         + cross_accumulators(8 * tokens.shape[0])
         + small_buffers()
         + Reduction.scratch(shard),
-        input_output_aliases={2: 3},
+        input_output_aliases={0: 3},
         compiler_params=pltpu.CompilerParams(
             collective_id=1, has_side_effects=True, vmem_limit_bytes=56 * MIB
         ),
-    )(starts, ends, grads, master_rows, tokens, tok_normed, w_kv, tok_norm, g1, *cross)
+    )(grads, tokens, tok_normed, w_kv, tok_norm, g1, *cross)
 
 
 def body(tokens, frame_ids, episodes, master, moment_one, moment_two, latent_grad):
@@ -1393,19 +1405,20 @@
     reach = lat_count == 8 and lax.axis_size("kf") == 4
     shard_rows = shard_len // LANES
     master_rows = master.reshape(shard_rows, LANES)
-    episode_index = jnp.arange(EPISODES, dtype=jnp.int32)
-    own_episodes = lax.dynamic_slice_in_dim(episodes[0], lat_index * frames, frames, 0)
-    episode_match = own_episodes[:, None] == episode_index[None, :]
     score_flops = rows_total * cap * LANES * 2
     select_flops = frames * cap * total_keys * LANES * 2
     if reach:
-        hot = jnp.pad(episode_match.astype(BF), ((0, 16 - frames), (0, 16 - EPISODES)))
         (
             up_one, down_one, w_qkv, w_so, up_two, down_two,
             latent, norms, hid_bias, out_bias, w_q, w_o, w_kv, tok_norm, tok_normed, episode_rows, rank, counts,
-            kvf, cross_out, cross_lse, h1,
-        ) = begin_all(master_rows, tokens[0], frame_ids.reshape(-1, LANES), hot, frames, cap)
+            kvf, cross_out, cross_lse, hot_lanes, h1,
+        ) = begin_all(master_rows, tokens[0], frame_ids.reshape(-1, LANES), episodes, frames, cap)
     else:
+        own_episodes = lax.dynamic_slice_in_dim(episodes[0], lat_index * frames, frames, 0)
+        episode_match = own_episodes[:, None] == jnp.arange(EPISODES, dtype=jnp.int32)[None, :]
+        hot_lanes = jnp.broadcast_to(
+            jnp.pad(episode_match.astype(F32), ((0, 0), (0, 16 - EPISODES)))[:, :, None], (frames, 16, LANES)
+        )
         weights = split_flat(lax.all_gather(master.astype(BF), "lat", axis=0, tiled=True))
         norms = weights["lat_norms"].astype(F32)
         out_bias = weights["out_bias"].astype(F32)
@@ -1506,9 +1519,6 @@
         latents_out = lax.all_to_all(
             latents.reshape(frames, LAT, D), "lat", split_axis=1, concat_axis=0, tiled=True
         )[None]
-    hot_lanes = jnp.broadcast_to(
-        jnp.pad(episode_match.astype(F32), ((0, 0), (0, 16 - EPISODES)))[:, :, None], (frames, 16, LANES)
-    )
     g1, dhid_one, dnorm_sa, dnorm_one, dout_so, dout_one, flat = call(
         functools.partial(backward_kernel, flat_shard, extra),
         frames,
@@ -1565,7 +1575,7 @@
     bias_owner, bias_at = divmod(bias_offset, shard_len)
     if reach:
         summed, stats, token_grad, unused = reduce_all(
-            flat, master_rows, starts, ends, bias_owner, bias_at // LANES, tokens[0], tok_normed, w_kv, tok_norm,
+            flat, shard_rows, bias_owner, bias_at // LANES, tokens[0], tok_normed, w_kv, tok_norm,
             g1.reshape(frames, LAT, D), cross,
         )
     else:
@@ -1602,24 +1612,16 @@
         local_flat = flat.reshape(-1)
         summed = lax.psum_scatter(local_flat, "lat", scatter_dimension=0, tiled=True)
         summed = lax.psum(summed, "kf").reshape(flat_rows)
-        grad_sq, weight_sq = call(
-            grad_stats_kernel,
-            opt_steps,
-            [smem, fixed(16, LANES), fixed(16, LANES), rowed(opt_rows, LANES), rowed(opt_rows, LANES)],
-            [(kept(1, LANES), shaped((1, LANES))), (kept(16, LANES), shaped((16, LANES)))],
-            (base, starts, ends, summed, master_rows),
-        )
         bias_rows = summed[bias_at // LANES : bias_at // LANES + 2 * FF // LANES].astype(F32)
         bias_rows = jnp.where(lat_index == bias_owner, bias_rows, 0.0)
-        stats = lax.psum(
-            jnp.concatenate([grad_sq, jnp.zeros((7, LANES), F32), weight_sq, bias_rows]), "lat"
-        )
-    bias_grad = stats[24:STAT_ROWS].reshape(2, FF)
-    grad_shard, lamb_update, new_one, new_two, update_sq = call(
+        grad_sq = jnp.sum(jnp.square(summed.astype(F32)), axis=0, keepdims=True)
+        stats = lax.psum(jnp.concatenate([grad_sq, jnp.zeros((7, LANES), F32), bias_rows]), "lat")
+    grad_shard, lamb_update, new_one, new_two, norms_sq, bias_grad = call(
         lamb_kernel,
         opt_steps,
         [smem, fixed(STAT_ROWS, LANES), fixed(16, LANES), fixed(16, LANES)] + [rowed(opt_rows, LANES)] * 4,
-        [(rowed(opt_rows, LANES), shaped(flat_rows))] * 4 + [(kept(16, LANES), shaped((16, LANES)))],
+        [(rowed(opt_rows, LANES), shaped(flat_rows))] * 4
+        + [(kept(16, 2 * LANES), shaped((16, 2 * LANES))), (kept(2, FF), shaped((2, FF)))],
         (
             base, stats, starts, ends, summed, master_rows,
             moment_one.reshape(flat_rows), moment_two.reshape(flat_rows),
@@ -1629,20 +1631,19 @@
         vmem = pl.BlockSpec(memory_space=pltpu.VMEM)
         trust = pl.pallas_call(
             trust_kernel,
-            out_shape=shaped((16, LANES)),
-            in_specs=[vmem, vmem],
+            out_shape=shaped((1, len(layout))),
+            in_specs=[vmem],
             out_specs=vmem,
             scratch_shapes=[
-                pltpu.VMEM((8, 16, LANES), F32),
+                pltpu.VMEM((8, 16, 2 * LANES), F32),
                 pltpu.SemaphoreType.DMA((7,)),
                 pltpu.SemaphoreType.DMA((7,)),
             ],
             compiler_params=pltpu.CompilerParams(collective_id=2, has_side_effects=True),
-        )(update_sq, stats)[: len(layout), 0]
+        )(norms_sq).reshape(-1)
     else:
-        update_sq = lax.psum(jnp.sum(update_sq, axis=1), "lat")
-        weight_sq = jnp.sum(stats[8:24], axis=1)
-        trust = (jnp.sqrt(weight_sq) / (jnp.sqrt(update_sq) + 1e-06))[: len(layout)]
+        sums = lax.psum(jnp.sum(norms_sq.reshape(16, 2, LANES), axis=2), "lat")[: len(layout)]
+        trust = jnp.sqrt(sums[:, 1]) / (jnp.sqrt(sums[:, 0]) + 1e-06)
     return (
         latents_out,
         token_grad[None],

time: 334 us -> 326 us (0.976)
  Pallas kernels: 322 us -> 318 us
    pallas_call x3, Pallas kernels: 165 us -> 162 us  [call(): pl.pallas_call(kernel, grid=(grid,), in_specs=in_specs, out_specs=list(ou...]
where the time goes in v4:
time: 326 us; the launch traced here: 321 us
  Pallas kernels  318 us (98%)
    pallas_call x3, Pallas kernels, call(): pl.pallas_call(kernel, grid=(grid,), in_specs=in_specs, out_specs=list(ou...  162 us
    pallas_call x1, Pallas kernels, reduce_all(): pl.pallas_call(functools.partial(reduce_kernel, shard, bias_owner, bias_r...  84.8 us
    pallas_call x1, Pallas kernels, begin_all(): pl.pallas_call(functools.partial(begin_kernel, chunks), out_shape=[shaped...  65 us

profile of v4, /device:TPU:0, one launch (start us, length us, event | category | flops | bytes accessed | tf_op | source)
XLA Modules:
  0.0 321.5 jit_solution(1083733396239748483)
XLA Ops:
  0.6 65.0 %shard_map.152 = (bf16[512,2048]{1,0:T(8,128)(2,1)}, bf16[2048,512]{1,0:T(8,128)(2,1)}, bf16[512,1536]{1,0:T(8,128)(2,1)}, bf16[512,512]{1,0:T(8,128)(2,1)}, bf1...) custom-call(f32[5488,128]{1,0:T(8,128)} %bitcast.17, ...), custom_call_target="tpu_custom_call" | custom-call | tf_op jit(solution)/shard_map/pallas_call | solution.py:824
  65.6 82.6 %shard_map.153 = (f32[2048,512]{1,0:T(8,128)}, bf16[2048,1536]{1,0:T(8,128)(2,1)}, f32[4,8,512]{2,1,0:T(8,128)}, bf16[2048,512]{1,0:T(8,128)(2,1)}, bf16[2048,20...) custom-call(f32[2048,512]{1,0:T(8,128)} %get-tuple-element.59.h1, ...), custom_call_target="tpu_custom_call" | custom-call | flops 42949672960 | bytes 64837632 | tf_op jit(solution)/shard_map/pallas_call | solution.py:1347
  148.2 70.4 %shard_map.154 = (f32[2048,512]{1,0:T(8,128)}, f32[1,2048]{1,0:T(1,128)}, f32[2,512]{1,0:T(2,128)}, f32[2,512]{1,0:T(2,128)}, f32[1,512]{1,0:T(1,128)}, /*index=5*/f32[1,512]{1,0:T(1,128)}, bf16[48000,128]{1,0:T(8,128)(2,1)}) custom-call(bf16[2048,1536]{1,0:T(8,128)(2,1)} %get-tuple-element.70.qkv, ...), custom_call_target="tpu_custom_call", output_to_operand_aliasing={{6}: (13, {})} | custom-call | flops 38654705664 | bytes 72912896 | tf_op jit(solution)/shard_map/pallas_call | solution.py:1347
  218.6 84.8 %shard_map.155 = (bf16[5488,128]{1,0:T(8,128)(2,1)}, f32[40,128]{1,0:T(8,128)}, bf16[512,256]{1,0:T(8,128)(2,1)}, bf16[2,2,2,6000,128]{4,3,2,1,0:T(8,128)(2,1)}) custom-call(bf16[2,2,2,6000,128]{4,3,2,1,0:T(8,128)(2,1)} %bitcast.16, bf16[512,256]{1,0:T(8,128)(2,1)} %bitcast.24, ...), custom_call_target="tpu_custom_call", output_to_operand_aliasing={{3}: (0, {})} | custom-call | tf_op jit(solution)/shard_map/pallas_call | solution.py:1375
  303.4 0.0 copy-start
  303.4 8.7 %shard_map.156 = (f32[5488,128]{1,0:T(8,128)}, f32[5488,128]{1,0:T(8,128)}, f32[5488,128]{1,0:T(8,128)}, f32[5488,128]{1,0:T(8,128)}, f32[16,256]{1,0:T(8,128)}, /*index=5*/f32[2,2048]{1,0:T(2,128)}) custom-call(s32[1]{0:T(128)} %bitcast.8.base, f32[40,128]{1,0:T(8,128)} %get-tuple-element.102.stats, s32[16,128]{1,0:T(8,128)} %constant.10.clone.starts, ...), custom_call_target="tpu_custom_call" | custom-call | bytes 21143556 | tf_op jit(solution)/shard_map/pallas_call | solution.py:1347
  312.1 0.0 copy-start.1
  312.1 6.4 %shard_map.157 = f32[1,13]{1,0:T(1,128)} custom-call(f32[16,256]{1,0:T(8,128)} %get-tuple-element.108.norms_sq), custom_call_target="tpu_custom_call" | custom-call | tf_op jit(solution)/shard_map/pallas_call | solution.py:1632
  318.5 0.0 copy-start.2
  318.5 0.0 copy-done
  318.5 1.3 copy.24
  319.8 0.0 copy-done.1
  319.8 0.7 copy.25
  320.5 0.0 copy-done.2
  320.5 0.5 copy.26
Async XLA Ops:
  303.4 15.1 %copy-start = (bf16[32,64,512]{2,1,0:T(8,128)(2,1)S(1)}, bf16[32,64,512]{2,1,0:T(8,128)(2,1)}, u32[]{:S(2)}) copy-start(bf16[32,64,512]{2,1,0:T(8,128)(2,1)} %get-tuple-element.69) | copy-start | bytes 6291460
  312.1 7.7 %copy-start.1 = (bf16[512,256]{1,0:T(8,128)(2,1)S(1)}, bf16[512,256]{1,0:T(8,128)(2,1)}, u32[]{:S(2)}) copy-start(bf16[512,256]{1,0:T(8,128)(2,1)} %get-tuple-element.101) | copy-start | bytes 786436
  318.5 2.0 copy-start.2

commit v5 on v4

--- a/solution.py
+++ b/solution.py
@@ -119,11 +119,15 @@
 
 def lane_half(shape, half):
     lane = lax.broadcasted_iota(jnp.int32, shape, 1)
-    return (lane >= half * 64) & (lane < half * 64 + 64)
+    return (lane >= half * HEAD_DIM) & (lane < (half + 1) * HEAD_DIM)
 
 
 def keep_half(values, half):
     return jnp.where(lane_half(values.shape, half), values, jnp.zeros_like(values))
+
+
+def by_head(values):
+    return jnp.concatenate([keep_half(values, h) for h in range(values.shape[1] // HEAD_DIM)], axis=0)
 
 
 def select_tokens(rank_rows, cap):
@@ -182,8 +186,12 @@
     return mm(hot, high) + mm(hot, low)
 
 
-def lamb_kernel(base, stats, starts, ends, summed, master, one, two, grad_out, update_out, one_out, two_out, norms_sq, bias):
+def lamb_kernel(
+    base, stats, starts, ends, summed, master, one, two, token_in,
+    grad_out, update_out, one_out, two_out, norms_sq, bias, token_out,
+):
     i = pl.program_id(0)
+    token_out[...] = token_in[...]
     rows = master.shape[0]
     hot = segment_hot(starts, ends, base[0] + i * rows, rows)
     total_sq = jnp.sum(stats[0:1, :], axis=1, keepdims=True)
@@ -874,10 +882,6 @@
     return stage[0 : rows * wide, :]
 
 
-def chunk_of(c, size=FCHUNK):
-    return pl.ds(pl.multiple_of(c * size, LANES), size)
-
-
 def feed_forward(rows, gain, bias, up_bias, down_bias, w_up, w_down, act_ref, slope_ref, normed_ref, total_ref):
     xhat, rstd = norm_stats(rows)
     normed_ref[...] = (xhat * gain + bias).astype(BF)
@@ -1022,6 +1026,50 @@
         lax.fori_loop(0, self.frames, step, 0)
 
 
+class Flow:
+    def __init__(self, step, steps, array, slots, sems):
+        self.step, self.steps, self.array, self.slots, self.sems = step, steps, array, slots, sems
+        self.rows = slots.shape[1]
+
+    def here(self):
+        return self.slots.at[lax.rem(self.step, 2)]
+
+    def ends(self, step):
+        slot = lax.rem(step, 2)
+        rows = pl.ds(pl.multiple_of(step * self.rows, self.rows), self.rows)
+        return self.array.at[rows, :], self.slots.at[slot], self.sems.at[slot]
+
+    def load(self, step):
+        outside, inside, sem = self.ends(step)
+        return pltpu.make_async_copy(outside, inside, sem)
+
+    def store(self, step):
+        outside, inside, sem = self.ends(step)
+        return pltpu.make_async_copy(inside, outside, sem)
+
+    def fetch_ahead(self):
+        pl.when(self.step == 0)(lambda: self.load(self.step).start())
+        pl.when(self.step + 1 < self.steps)(lambda: self.load(self.step + 1).start())
+
+    def arrived(self):
+        self.load(self.step).wait()
+
+    def free(self):
+        pl.when(self.step >= 2)(lambda: self.store(self.step - 2).wait())
+
+    def send(self):
+        self.store(self.step).start()
+
+    def drain(self):
+        if self.steps > 1:
+            self.store(self.step - 1).wait()
+        self.store(self.step).wait()
+
+
+def flow_slots(shape, dtype):
+    return [pltpu.VMEM((2,) + shape, dtype), pltpu.SemaphoreType.DMA((2,))]
+
+
 class Late:
     def __init__(self, step, sources, refs, sems):
         self.first = step == 0
@@ -1042,19 +1090,30 @@
 
 
 def forward_kernel(
-    reach, shard, extra, h1, grad, norms, hid_bias, out_bias, up_one, down_one, *rest,
+    reach, shard, extra, steps, h1, grad, norms, hid_bias, out_bias, up_one, down_one, *rest,
 ):
-    forward_body(reach, shard, extra, h1, grad, norms, hid_bias, out_bias, up_one, down_one, rest[:4], *rest[4:])
+    forward_body(reach, shard, extra, steps, h1, grad, norms, hid_bias, out_bias, up_one, down_one, rest[:4], *rest[4:])
 
 
 def forward_body(
-    reach, shard, extra, h1, grad, norms, hid_bias, out_bias, up_one, down_one, late_sources,
-    h2_out, qkv, lse_out, mixed_out, act_one, slope_one, latents, g3, dhid, dnorm, dout, flat,
+    reach, shard, extra, steps, h1, grad, norms, hid_bias, out_bias, up_one, down_one, late_sources,
+    h2_all, qkv_all, lse_out, mixed_all, act_all, slope_all, latents, g3, dhid, dnorm, dout, flat,
     act_two, slope_two, acc_up, acc_down, stage, low, normed, mixed_t, work, sems,
-    w_qkv, w_so, up_two, down_two, late_sems, *shared,
+    w_qkv, w_so, up_two, down_two, late_sems,
+    h2_slots, h2_sems, qkv_slots, qkv_sems, mixed_slots, mixed_sems, act_slots, act_sems, slope_slots, slope_sems, *shared,
 ):
     step = pl.program_id(0)
     late = Late(step, late_sources, (w_qkv, w_so, up_two, down_two), late_sems)
+    flows = [
+        Flow(step, steps, *parts)
+        for parts in (
+            (h2_all, h2_slots, h2_sems), (qkv_all, qkv_slots, qkv_sems), (mixed_all, mixed_slots, mixed_sems),
+            (act_all, act_slots, act_sems), (slope_all, slope_slots, slope_sems),
+        )
+    ]
+    for flow in flows:
+        flow.free()
+    h2_out, qkv, mixed_out, act_one, slope_one = (flow.here() for flow in flows)
     if reach:
         place = Place()
         traffic = FrameExchange(place, grad, shared[0], shared[1], latents, shared[2:])
@@ -1072,34 +1131,31 @@
     if reach:
         pl.when(step == 0)(traffic.begin)
 
-    def project(c, carry):
-        at = chunk_of(c)
-        qkv[:, at] = mm(normed[...], w_qkv[:, at]).astype(BF)
-        return carry
-
-    lax.fori_loop(0, 3, project, 0)
+    qkv[...] = mm(normed[...], w_qkv[...]).astype(BF)
+    for k in (0, 1, 3, 4):
+        flows[k].send()
     scale = jnp.asarray(0.125, BF)
-
     ones = jnp.ones((16, LAT), BF)
-
-    for pair in range(HEADS // 2):
-        base = pair * LANES
-        query_pair = qkv[:, base : base + LANES] * scale
-        key_pair = qkv[:, D + base : D + base + LANES]
-        value_t = qkv[:, 2 * D + base : 2 * D + base + LANES].T
-        for half in range(2):
-            scores = mm_t(key_pair, keep_half(query_pair, half))
-            top = jnp.max(scores, axis=0, keepdims=True)
-            terms = jnp.exp(scores - top).astype(BF)
-            values = jnp.concatenate([value_t[half * HEAD_DIM : (half + 1) * HEAD_DIM, :], ones], axis=0)
-            product = mm(values, terms)
+    group = 4
+    width = group * HEAD_DIM
+    for base in range(0, D, width):
+        queries = by_head(qkv[:, base : base + width] * scale)
+        value_t = qkv[:, 2 * D + base : 2 * D + base + width].T
+        scores = mm_t(qkv[:, D + base : D + base + width], queries)
+        top = jnp.max(scores, axis=0, keepdims=True)
+        terms = jnp.exp(scores - top).astype(BF)
+        for j in range(group):
+            at = slice(j * LAT, (j + 1) * LAT)
+            values = jnp.concatenate([value_t[j * HEAD_DIM : (j + 1) * HEAD_DIM, :], ones], axis=0)
+            product = mm(values, terms[:, at])
             total = product[HEAD_DIM : HEAD_DIM + 1, :]
-            head = 2 * pair + half
-            lse_out[0, head : head + 1, :] = top + jnp.log(total)
+            head = base // HEAD_DIM + j
+            lse_out[0, head : head + 1, :] = top[:, at] + jnp.log(total)
             mixed_t[head * HEAD_DIM : (head + 1) * HEAD_DIM, :] = product[0:HEAD_DIM, :] * (1.0 / total)
     late.need(1, 2, 3)
     mixed = mixed_t[...].T.astype(BF)
     mixed_out[...] = mixed
+    flows[2].send()
     h3 = h2_out[...] + mm(mixed, w_so[...]) + out_bias[2:3, :]
     feed_forward(
         h3, norms[6:7, :], norms[7:8, :], hid_bias.at[1:2], out_bias[3:4, :], up_two, down_two, act_two, slope_two,
@@ -1124,16 +1180,39 @@
         write_flat(flat, stage, low, [(acc_up, at["w_up"] + half), (acc_down, at["w_down"] + half)], sems, shard, extra)
         if reach:
             traffic.finish()
+        for flow in flows:
+            flow.drain()
 
 
 def backward_kernel(
-    shard, extra, qkv, lse, mixed, g3, h2, h1, act_one, slope_one, norms, w_so, src_qkv, src_up, src_down, flat_in,
-    g1, dhid, dnorm_sa, dnorm_one, dout_so, dout_one, flat,
+    shard, extra, steps, qkv, lse, mixed, g3, h2_all, h1_all, act_all, slope_all, norms, w_so, src_qkv, src_up, src_down,
+    latents_in, flat_in,
+    g1, dhid, dnorm_sa, dnorm_one, dout_so, dout_one, latents_out, flat,
     dqkv, acc_up, acc_down, acc_qkv, acc_so, stage, low, normed, grad_mixed, grad_low, work, sems,
     w_qkv, up_one, down_one, late_sems,
+    h2_slots, h2_sems, h1_slots, h1_sems, act_slots, act_sems, slope_slots, slope_sems, latents_held, pass_sem,
 ):
     step = pl.program_id(0)
     late = Late(step, (src_qkv, src_up, src_down), (w_qkv, up_one, down_one), late_sems)
+    flows = [
+        Flow(step, steps, *parts)
+        for parts in (
+            (h2_all, h2_slots, h2_sems), (h1_all, h1_slots, h1_sems), (act_all, act_slots, act_sems),
+            (slope_all, slope_slots, slope_sems),
+        )
+    ]
+    for flow in flows:
+        flow.fetch_ahead()
+    h2, h1, act_one, slope_one = (flow.here() for flow in flows)
+    latents_load = pltpu.make_async_copy(latents_in, latents_held, pass_sem.at[0])
+    latents_store = pltpu.make_async_copy(latents_held, latents_out, pass_sem.at[1])
+    pl.when(step == 0)(lambda: latents_load.start())
+
+    @pl.when(step == min(1, steps - 1))
+    def _():
+        latents_load.wait()
+        latents_store.start()
+
     clear(
         step == 0,
         (acc_up, acc_down, acc_qkv, acc_so, dhid, dnorm_sa, dnorm_one, dout_so, dout_one),
@@ -1145,43 +1224,32 @@
     acc_so[...] += t_mm(mixed[...], grad_low[...])
     grad_mixed[...] = mm_t(grad_low[...], w_so[...]).astype(BF)
 
-    def attend(pair, carry):
-        query_at = chunk_of(pair, LANES)
-        key_at = chunk_of(pair + D // LANES, LANES)
-        value_at = chunk_of(pair + 2 * D // LANES, LANES)
-        query_pair = qkv[:, query_at] * scale
-        key_pair = qkv[:, key_at]
-        value_pair = qkv[:, value_at]
-        grad_pair = grad_mixed[:, query_at]
-        key_t = key_pair.T
-        query_t = []
-        grad_key = jnp.zeros((LAT, LANES), F32)
-        grad_value = jnp.zeros((LAT, LANES), F32)
-        for half in range(2):
-            query = keep_half(query_pair, half)
-            grad_head = keep_half(grad_pair, half)
-            prob = jnp.exp(mm_t(key_pair, query) - lse[0, pl.ds(2 * pair + half, 1), :])
-            grad_value = grad_value + mm(prob.astype(BF), grad_head)
-            weighted = prob * mm_t(value_pair, grad_head)
-            grad_score = (weighted - prob * col_sum(weighted)).astype(BF)
-            grad_key = grad_key + mm(grad_score, query)
-            query_t.append(mm(key_t[half * HEAD_DIM : (half + 1) * HEAD_DIM, :], grad_score))
+    for base in range(0, D, LANES):
+        query_at = slice(base, base + LANES)
+        key_at = slice(D + base, D + base + LANES)
+        value_at = slice(2 * D + base, 2 * D + base + LANES)
+        head = base // HEAD_DIM
+        queries = by_head(qkv[:, query_at] * scale)
+        grads = by_head(grad_mixed[:, query_at])
+        keys = qkv[:, key_at]
+        key_t = keys.T
+        log_total = jnp.concatenate([lse[0, head : head + 1, :], lse[0, head + 1 : head + 2, :]], axis=1)
+        prob = jnp.exp(mm_t(keys, queries) - log_total)
+        dqkv[:, value_at] = mm(prob.astype(BF), grads).astype(BF)
+        weighted = prob * mm_t(qkv[:, value_at], grads)
+        grad_score = (weighted - prob * col_sum(weighted)).astype(BF)
+        dqkv[:, key_at] = mm(grad_score, queries).astype(BF)
+        query_t = [
+            mm(key_t[j * HEAD_DIM : (j + 1) * HEAD_DIM, :], grad_score[:, j * LAT : (j + 1) * LAT]) for j in range(2)
+        ]
         dqkv[:, query_at] = (jnp.concatenate(query_t, axis=0).T * 0.125).astype(BF)
-        dqkv[:, key_at] = grad_key.astype(BF)
-        dqkv[:, value_at] = grad_value.astype(BF)
-        return carry
-
-    lax.fori_loop(0, HEADS // 2, attend, 0)
     late.need(0, 1, 2)
+    for flow in flows:
+        flow.arrived()
     xhat, rstd = norm_stats(h2[...])
     normed[...] = (xhat * norms[4:5, :] + norms[5:6, :]).astype(BF)
-    work[...] = jnp.zeros(work.shape, F32)
-
-    for c in range(3):
-        at = slice(c * D, (c + 1) * D)
-        work[...] += mm_t(dqkv[:, at], w_qkv[:, at])
-        acc_qkv[:, at] += t_mm(normed[...], dqkv[:, at])
-    grad_in = work[...]
+    grad_in = mm_t(dqkv[...], w_qkv[...])
+    acc_qkv[...] += t_mm(normed[...], dqkv[...])
     dnorm_sa[...] += jnp.concatenate([col_sum(grad_in * xhat), col_sum(grad_in)], axis=0)
     grad_two = grad_three + norm_back(grad_in, xhat, rstd, norms[4:5, :])
 
@@ -1203,6 +1271,7 @@
             [(acc_up, at["w_up"]), (acc_down, at["w_down"]), (acc_qkv, at["w_qkv"]), (acc_so, at["w_so"])],
             sems, shard, extra,
         )
+        latents_store.wait()
 
 
 def cross_back_frame(
@@ -1479,19 +1548,19 @@
         shared = []
     slab = D * FF // LANES
     h2, qkv, self_lse, mixed, act_one, slope_one, latents, g3, dhid_two, dnorm_two, dout_two, flat = call(
-        functools.partial(forward_kernel, reach, flat_shard, extra),
+        functools.partial(forward_kernel, reach, flat_shard, extra, frames),
         frames,
         [
             rowed(LAT, D), grad_spec, fixed(8, D), fixed(2, FF), fixed(4, D), fixed(D, FF), fixed(FF, D),
         ]
         + [anywhere] * 4,
         [
-            (rowed(LAT, D), shaped((rows_total, D))),
-            (rowed(LAT, 3 * D), shaped((rows_total, 3 * D), BF)),
+            (anywhere, shaped((rows_total, D))),
+            (anywhere, shaped((rows_total, 3 * D), BF)),
             (framed(HEADS, LAT), shaped((frames, HEADS, LAT))),
-            (rowed(LAT, D), shaped((rows_total, D), BF)),
-            (rowed(LAT, FF), shaped((rows_total, FF), BF)),
-            (rowed(LAT, FF), shaped((rows_total, FF), BF)),
+            (anywhere, shaped((rows_total, D), BF)),
+            (anywhere, shaped((rows_total, FF), BF)),
+            (anywhere, shaped((rows_total, FF), BF)),
             latents_spec,
             (rowed(LAT, D), shaped((rows_total, D))),
             (kept(1, FF), shaped((1, FF))),
@@ -1509,24 +1578,23 @@
             pltpu.VMEM((D, 3 * D), BF), pltpu.VMEM((D, D), BF), pltpu.VMEM((D, FF), BF), pltpu.VMEM((FF, D), BF),
             pltpu.SemaphoreType.DMA((4,)),
         ]
+        + flow_slots((LAT, D), F32)
+        + flow_slots((LAT, 3 * D), BF)
+        + flow_slots((LAT, D), BF)
+        + flow_slots((LAT, FF), BF)
+        + flow_slots((LAT, FF), BF)
         + shared,
         limit=62,
         collective=4 if reach else None,
     )
-    if reach:
-        latents_out = latents[None]
-    else:
-        latents_out = lax.all_to_all(
-            latents.reshape(frames, LAT, D), "lat", split_axis=1, concat_axis=0, tiled=True
-        )[None]
-    g1, dhid_one, dnorm_sa, dnorm_one, dout_so, dout_one, flat = call(
-        functools.partial(backward_kernel, flat_shard, extra),
+    g1, dhid_one, dnorm_sa, dnorm_one, dout_so, dout_one, latents, flat = call(
+        functools.partial(backward_kernel, flat_shard, extra, frames),
         frames,
         [
-            rowed(LAT, 3 * D), framed(HEADS, LAT), rowed(LAT, D), rowed(LAT, D), rowed(LAT, D), rowed(LAT, D),
-            rowed(LAT, FF), rowed(LAT, FF), fixed(8, D), fixed(D, D),
+            rowed(LAT, 3 * D), framed(HEADS, LAT), rowed(LAT, D), rowed(LAT, D), anywhere, anywhere, anywhere, anywhere,
+            fixed(8, D), fixed(D, D),
         ]
-        + [anywhere] * 4,
+        + [anywhere] * 5,
         [
             (rowed(LAT, D), shaped((rows_total, D))),
             (kept(1, FF), shaped((1, FF))),
@@ -1534,10 +1602,11 @@
             (kept(2, D), shaped((2, D))),
             (kept(1, D), shaped((1, D))),
             (kept(1, D), shaped((1, D))),
+            (anywhere, shaped(latents.shape, BF)),
             (anywhere, shaped(flat_shape, BF)),
         ],
         (
-            qkv, self_lse, mixed, g3, h2, h1, act_one, slope_one, norms, w_so, w_qkv, up_one, down_one, flat,
+            qkv, self_lse, mixed, g3, h2, h1, act_one, slope_one, norms, w_so, w_qkv, up_one, down_one, latents, flat,
         ),
         flops=2 * mlp_flops + 10 * attn_flops,
         trans=rows_total * LAT * HEADS,
@@ -1549,10 +1618,21 @@
             pltpu.SemaphoreType.DMA((2, 16)),
             pltpu.VMEM((D, 3 * D), BF), pltpu.VMEM((D, FF), BF), pltpu.VMEM((FF, D), BF),
             pltpu.SemaphoreType.DMA((3,)),
-        ],
+        ]
+        + flow_slots((LAT, D), F32)
+        + flow_slots((LAT, D), F32)
+        + flow_slots((LAT, FF), BF)
+        + flow_slots((LAT, FF), BF)
+        + [pltpu.VMEM(latents.shape, BF), pltpu.SemaphoreType.DMA((2,))],
         limit=60,
-        aliases={13: 6},
+        aliases={14: 7},
     )
+    if reach:
+        latents_out = latents[None]
+    else:
+        latents_out = lax.all_to_all(
+            latents.reshape(frames, LAT, D), "lat", split_axis=1, concat_axis=0, tiled=True
+        )[None]
     cross = (
         kvf, cross_out, cross_lse, rank, counts, episode_rows, hot_lanes, latent, norms, w_q, w_o,
         dnorm_one, dnorm_sa, dnorm_two, dhid_one, dhid_two, dout_one, dout_so, dout_two,
@@ -1616,15 +1696,16 @@
         bias_rows = jnp.where(lat_index == bias_owner, bias_rows, 0.0)
         grad_sq = jnp.sum(jnp.square(summed.astype(F32)), axis=0, keepdims=True)
         stats = lax.psum(jnp.concatenate([grad_sq, jnp.zeros((7, LANES), F32), bias_rows]), "lat")
-    grad_shard, lamb_update, new_one, new_two, norms_sq, bias_grad = call(
+    grad_shard, lamb_update, new_one, new_two, norms_sq, bias_grad, token_grad = call(
         lamb_kernel,
         opt_steps,
-        [smem, fixed(STAT_ROWS, LANES), fixed(16, LANES), fixed(16, LANES)] + [rowed(opt_rows, LANES)] * 4,
+        [smem, fixed(STAT_ROWS, LANES), fixed(16, LANES), fixed(16, LANES)] + [rowed(opt_rows, LANES)] * 4 + [fixed(*token_grad.shape)],
         [(rowed(opt_rows, LANES), shaped(flat_rows))] * 4
-        + [(kept(16, 2 * LANES), shaped((16, 2 * LANES))), (kept(2, FF), shaped((2, FF)))],
+        + [(kept(16, 2 * LANES), shaped((16, 2 * LANES))), (kept(2, FF), shaped((2, FF)))]
+        + [(kept(*token_grad.shape), shaped(token_grad.shape, BF))],
         (
             base, stats, starts, ends, summed, master_rows,
-            moment_one.reshape(flat_rows), moment_two.reshape(flat_rows),
+            moment_one.reshape(flat_rows), moment_two.reshape(flat_rows), token_grad,
         ),
     )
     if reach:

time: 326 us -> 307 us (0.942)
  Pallas kernels: 318 us -> 301 us
    pallas_call x3, Pallas kernels: 162 us -> 145 us  [call(): pl.pallas_call(kernel, grid=(grid,), in_specs=in_specs, out_specs=list(ou...]
where the time goes in v5:
time: 307 us; the launch traced here: 303 us
  Pallas kernels  301 us (98%)
    pallas_call x3, Pallas kernels, call(): pl.pallas_call(kernel, grid=(grid,), in_specs=in_specs, out_specs=list(ou...  145 us
    pallas_call x1, Pallas kernels, reduce_all(): pl.pallas_call(functools.partial(reduce_kernel, shard, bias_owner, bias_r...  85.1 us
    pallas_call x1, Pallas kernels, begin_all(): pl.pallas_call(functools.partial(begin_kernel, chunks), out_shape=[shaped...  65 us
    pallas_call x1, Pallas kernels, body(): pl.pallas_call(trust_kernel, out_shape=shaped((1, len(layout))), in_specs...  6.26 us

profile of v5, /device:TPU:0, one launch (start us, length us, event | category | flops | bytes accessed | tf_op | source)
XLA Modules:
  0.0 302.9 jit_solution(5952756778940443770)
XLA Ops:
  0.6 65.0 %shard_map.152 = (bf16[512,2048]{1,0:T(8,128)(2,1)}, bf16[2048,512]{1,0:T(8,128)(2,1)}, bf16[512,1536]{1,0:T(8,128)(2,1)}, bf16[512,512]{1,0:T(8,128)(2,1)}, bf1...) custom-call(f32[5488,128]{1,0:T(8,128)} %bitcast.17, ...), custom_call_target="tpu_custom_call" | custom-call | tf_op jit(solution)/shard_map/pallas_call | solution.py:832
  65.6 73.6 %shard_map.153 = (f32[2048,512]{1,0:T(8,128)}, bf16[2048,1536]{1,0:T(8,128)(2,1)}, f32[4,8,512]{2,1,0:T(8,128)}, bf16[2048,512]{1,0:T(8,128)(2,1)}, bf16[2048,20...) custom-call(f32[2048,512]{1,0:T(8,128)} %get-tuple-element.61.h1.h1_, ...), custom_call_target="tpu_custom_call" | custom-call | flops 42949672960 | bytes 64837632 | tf_op jit(solution)/shard_map/pallas_call | solution.py:1416
  139.2 62.2 %shard_map.154 = (f32[2048,512]{1,0:T(8,128)}, f32[1,2048]{1,0:T(1,128)}, f32[2,512]{1,0:T(2,128)}, f32[2,512]{1,0:T(2,128)}, f32[1,512]{1,0:T(1,128)}, /*index=...) custom-call(bf16[2048,1536]{1,0:T(8,128)(2,1)} %get-tuple-element.71.q, ...), custom_call_target="tpu_custom_call", output_to_operand_aliasing={{7}: (14, {})} | custom-call | flops 38654705664 | bytes 77107200 | tf_op jit(solution)/shard_map/pallas_call | solution.py:1416
  201.4 85.1 %shard_map.155 = (bf16[5488,128]{1,0:T(8,128)(2,1)}, f32[40,128]{1,0:T(8,128)}, bf16[512,256]{1,0:T(8,128)(2,1)}, bf16[2,2,2,6000,128]{4,3,2,1,0:T(8,128)(2,1)}) custom-call(bf16[2,2,2,6000,128]{4,3,2,1,0:T(8,128)(2,1)} %bitcast.16, bf16[512,256]{1,0:T(8,128)(2,1)} %bitcast.23, ...), custom_call_target="tpu_custom_call", output_to_operand_aliasing={{3}: (0, {})} | custom-call | tf_op jit(solution)/shard_map/pallas_call | solution.py:1444
  286.5 8.8 %shard_map.156 = (f32[5488,128]{1,0:T(8,128)}, f32[5488,128]{1,0:T(8,128)}, f32[5488,128]{1,0:T(8,128)}, f32[5488,128]{1,0:T(8,128)}, f32[16,256]{1,0:T(8,128)},...) custom-call(s32[1]{0:T(128)} %bitcast.5.base, f32[40,128]{1,0:T(8,128)} %get-tuple-element.104.stats, ...), custom_call_target="tpu_custom_call" | custom-call | bytes 21667844 | tf_op jit(solution)/shard_map/pallas_call | solution.py:1416
  295.3 6.3 %shard_map.157 = f32[1,13]{1,0:T(1,128)} custom-call(f32[16,256]{1,0:T(8,128)} %get-tuple-element.112.norms_sq), custom_call_target="tpu_custom_call" | custom-call | tf_op jit(solution)/shard_map/pallas_call | solution.py:1713
  301.6 1.1 copy.22

commit v6 on v5

--- a/solution.py
+++ b/solution.py
@@ -678,7 +678,7 @@
     latent, norms, hid_bias, out_bias, w_q, w_o, w_kv, tok_norm, tok_normed, episode, rank, counts,
     kvf_out, co_out, lse_out, hot_lanes, h1,
     whole, stage, all_ids, keys, m_up_one, m_down_one, m_qkv, m_so, m_up_two, m_down_two,
-    episodes_held, h1_held, h1_sem, send, recv, key_send, key_recv, id_send, id_recv, out_sem,
+    episodes_held, h1_held, h1_sem, master_held, load_sem, send, recv, key_send, key_recv, id_send, id_recv, out_sem,
 ):
     place = Place()
     shard = master.shape[0]
@@ -686,6 +686,12 @@
     gather = Gather(place, whole, shard, chunks, send, recv)
     exchange = KeyExchange(place, keys, key_send, key_recv)
     at = flat_rows_of()
+    loads = [
+        pltpu.make_async_copy(master.at[pl.ds(row, count), :], master_held.at[pl.ds(row, count), :], load_sem.at[k])
+        for k, (row, count) in enumerate(chunks)
+    ]
+    for copy in loads:
+        copy.start()
     partners = [place.lat_other(d) for d in range(1, 8)] + [place.z_near]
     greet(partners)
     all_ids[pl.ds(place.me, 1)] = ids[...][None]
@@ -694,12 +700,20 @@
         for d in range(1, 8)
     ]
     own_at = place.me * shard
-    for row, count in chunks:
-        whole[pl.ds(pl.multiple_of(own_at + row, 16), count), :] = master[row : row + count, :].astype(BF)
+
+    def cast(first, last):
+        for k in range(first, last):
+            row, count = chunks[k]
+            loads[k].wait()
+            at_row = pl.multiple_of(own_at + row, 16)
+            whole[pl.ds(at_row, count), :] = master_held[row : row + count, :].astype(BF)
+
+    cast(0, 5)
     met(partners)
     for copy in id_copies:
         copy.start()
     gather.play("a0", "a1", "a2", "a3", "a4")
+    cast(5, len(chunks))
 
     for copy in id_copies:
         copy.wait_recv()
@@ -851,7 +865,7 @@
             shaped((frames, 16, LANES)),
             shaped((frames * LAT, D)),
         ],
-        in_specs=[vmem] * 4,
+        in_specs=[anywhere] + [vmem] * 3,
         out_specs=[anywhere] * 6 + [vmem] * 16 + [anywhere],
         scratch_shapes=[
             pltpu.VMEM((8 * shard, LANES), BF),
@@ -864,6 +878,8 @@
             pltpu.VMEM((8, D), F32),
             pltpu.VMEM((frames, LAT, D), F32),
             dma((frames,)),
+            pltpu.VMEM((shard, LANES), F32),
+            dma((len(chunks),)),
             dma((7, len(chunks))), dma((7, len(chunks))), dma((8,)), dma((8,)), dma((7,)), dma((7,)), dma((6,)),
         ],
         compiler_params=pltpu.CompilerParams(
@@ -872,7 +888,7 @@
     )(master_rows, token_rows, ids, episodes)
 
 
-FCHUNK = 512
+FCHUNK = 1024
 
 
 def to_flat(stage, matrix):
@@ -885,15 +901,11 @@
 def feed_forward(rows, gain, bias, up_bias, down_bias, w_up, w_down, act_ref, slope_ref, normed_ref, total_ref):
     xhat, rstd = norm_stats(rows)
     normed_ref[...] = (xhat * gain + bias).astype(BF)
-    total_ref[...] = rows + down_bias
-
-    for c in range(2):
-        at = slice(c * FF // 2, (c + 1) * FF // 2)
-        act, slope = gelu_pair(mm(normed_ref[...], w_up[:, at]) + up_bias[:, at])
-        act = act.astype(BF)
-        act_ref[:, at] = act
-        slope_ref[:, at] = slope.astype(BF)
-        total_ref[...] += mm(act, w_down[at, :])
+    act, slope = gelu_pair(mm(normed_ref[...], w_up[...]) + up_bias[...])
+    act = act.astype(BF)
+    act_ref[...] = act
+    slope_ref[...] = slope.astype(BF)
+    total_ref[...] = rows + down_bias + mm(act, w_down[...])
 
 
 def feed_back(grad_ref, normed_ref, xhat, rstd, gain, act, slope, w_up, w_down, acc_up, acc_down, dhid, dnorm, dout, work):

time: 307 us -> 305 us (level)
  no operation moved by 1% of the time
where the time goes in v6:
time: 305 us; the launch traced here: 301 us
  Pallas kernels  299 us (98%)
    pallas_call x3, Pallas kernels, call(): pl.pallas_call(kernel, grid=(grid,), in_specs=in_specs, out_specs=list(ou...  143 us
    pallas_call x1, Pallas kernels, reduce_all(): pl.pallas_call(functools.partial(reduce_kernel, shard, bias_owner, bias_r...  85.2 us
    pallas_call x1, Pallas kernels, begin_all(): pl.pallas_call(functools.partial(begin_kernel, chunks), out_shape=[shaped...  64.2 us
    pallas_call x1, Pallas kernels, body(): pl.pallas_call(trust_kernel, out_shape=shaped((1, len(layout))), in_specs...  6.26 us

profile of v6, /device:TPU:0, one launch (start us, length us, event | category | flops | bytes accessed | tf_op | source)
XLA Modules:
  0.0 300.7 jit_solution(18097016811767657841)
XLA Ops:
  0.6 64.2 %shard_map.152 = (bf16[512,2048]{1,0:T(8,128)(2,1)}, bf16[2048,512]{1,0:T(8,128)(2,1)}, bf16[512,1536]{1,0:T(8,128)(2,1)}, bf16[512,512]{1,0:T(8,128)(2,1)}, bf1...) custom-call(f32[5488,128]{1,0:T(8,128)} %bitcast.17, ...), custom_call_target="tpu_custom_call" | custom-call | tf_op jit(solution)/shard_map/pallas_call | solution.py:846
  64.8 72.6 %shard_map.153 = (f32[2048,512]{1,0:T(8,128)}, bf16[2048,1536]{1,0:T(8,128)(2,1)}, f32[4,8,512]{2,1,0:T(8,128)}, bf16[2048,512]{1,0:T(8,128)(2,1)}, bf16[2048,20...) custom-call(f32[2048,512]{1,0:T(8,128)} %get-tuple-element.61.h1.h1_, ...), custom_call_target="tpu_custom_call" | custom-call | flops 42949672960 | bytes 64837632 | tf_op jit(solution)/shard_map/pallas_call | solution.py:1428
  137.4 61.7 %shard_map.154 = (f32[2048,512]{1,0:T(8,128)}, f32[1,2048]{1,0:T(1,128)}, f32[2,512]{1,0:T(2,128)}, f32[2,512]{1,0:T(2,128)}, f32[1,512]{1,0:T(1,128)}, /*index=...) custom-call(bf16[2048,1536]{1,0:T(8,128)(2,1)} %get-tuple-element.71.q, ...), custom_call_target="tpu_custom_call", output_to_operand_aliasing={{7}: (14, {})} | custom-call | flops 38654705664 | bytes 77107200 | tf_op jit(solution)/shard_map/pallas_call | solution.py:1428
  199.1 85.2 %shard_map.155 = (bf16[5488,128]{1,0:T(8,128)(2,1)}, f32[40,128]{1,0:T(8,128)}, bf16[512,256]{1,0:T(8,128)(2,1)}, bf16[2,2,2,6000,128]{4,3,2,1,0:T(8,128)(2,1)}) custom-call(bf16[2,2,2,6000,128]{4,3,2,1,0:T(8,128)(2,1)} %bitcast.16, bf16[512,256]{1,0:T(8,128)(2,1)} %bitcast.23, ...), custom_call_target="tpu_custom_call", output_to_operand_aliasing={{3}: (0, {})} | custom-call | tf_op jit(solution)/shard_map/pallas_call | solution.py:1456
  284.3 8.8 %shard_map.156 = (f32[5488,128]{1,0:T(8,128)}, f32[5488,128]{1,0:T(8,128)}, f32[5488,128]{1,0:T(8,128)}, f32[5488,128]{1,0:T(8,128)}, f32[16,256]{1,0:T(8,128)},...) custom-call(s32[1]{0:T(128)} %bitcast.5.base, f32[40,128]{1,0:T(8,128)} %get-tuple-element.104.stats, ...), custom_call_target="tpu_custom_call" | custom-call | bytes 21667844 | tf_op jit(solution)/shard_map/pallas_call | solution.py:1428
  293.1 6.3 %shard_map.157 = f32[1,13]{1,0:T(1,128)} custom-call(f32[16,256]{1,0:T(8,128)} %get-tuple-element.112.norms_sq), custom_call_target="tpu_custom_call" | custom-call | tf_op jit(solution)/shard_map/pallas_call | solution.py:1725
  299.4 1.1 copy.22

commit v7 on v6

--- a/solution.py
+++ b/solution.py
@@ -814,10 +814,10 @@
     big = (
         (up_one, m_up_one, at["w_up"], D, FF),
         (down_one, m_down_one, at["w_down"], FF, D),
+        (up_two, m_up_two, at["w_up"] + D * FF // LANES, D, FF),
+        (down_two, m_down_two, at["w_down"] + D * FF // LANES, FF, D),
         (qkv_w, m_qkv, at["w_qkv"], D, 3 * D),
         (so_w, m_so, at["w_so"], D, D),
-        (up_two, m_up_two, at["w_up"] + D * FF // LANES, D, FF),
-        (down_two, m_down_two, at["w_down"] + D * FF // LANES, FF, D),
     )
     outs = []
     for j, (out, held, row, rows, cols) in enumerate(big):

time: 305 us -> 305 us (level)
  no operation moved by 1% of the time
where the time goes in v7:
time: 305 us; the launch traced here: 301 us
  Pallas kernels  299 us (98%)
    pallas_call x3, Pallas kernels, call(): pl.pallas_call(kernel, grid=(grid,), in_specs=in_specs, out_specs=list(ou...  143 us
    pallas_call x1, Pallas kernels, reduce_all(): pl.pallas_call(functools.partial(reduce_kernel, shard, bias_owner, bias_r...  85.2 us
    pallas_call x1, Pallas kernels, begin_all(): pl.pallas_call(functools.partial(begin_kernel, chunks), out_shape=[shaped...  64.1 us
    pallas_call x1, Pallas kernels, body(): pl.pallas_call(trust_kernel, out_shape=shaped((1, len(layout))), in_specs...  6.25 us

profile of v7, /device:TPU:0, one launch (start us, length us, event | category | flops | bytes accessed | tf_op | source)
XLA Modules:
  0.0 300.6 jit_solution(6071771169351949095)
XLA Ops:
  0.6 64.1 %shard_map.152 = (bf16[512,2048]{1,0:T(8,128)(2,1)}, bf16[2048,512]{1,0:T(8,128)(2,1)}, bf16[512,1536]{1,0:T(8,128)(2,1)}, bf16[512,512]{1,0:T(8,128)(2,1)}, bf1...) custom-call(f32[5488,128]{1,0:T(8,128)} %bitcast.17, ...), custom_call_target="tpu_custom_call" | custom-call | tf_op jit(solution)/shard_map/pallas_call | solution.py:846
  64.8 72.6 %shard_map.153 = (f32[2048,512]{1,0:T(8,128)}, bf16[2048,1536]{1,0:T(8,128)(2,1)}, f32[4,8,512]{2,1,0:T(8,128)}, bf16[2048,512]{1,0:T(8,128)(2,1)}, bf16[2048,20...) custom-call(f32[2048,512]{1,0:T(8,128)} %get-tuple-element.61.h1.h1_, ...), custom_call_target="tpu_custom_call" | custom-call | flops 42949672960 | bytes 64837632 | tf_op jit(solution)/shard_map/pallas_call | solution.py:1428
  137.4 61.7 %shard_map.154 = (f32[2048,512]{1,0:T(8,128)}, f32[1,2048]{1,0:T(1,128)}, f32[2,512]{1,0:T(2,128)}, f32[2,512]{1,0:T(2,128)}, f32[1,512]{1,0:T(1,128)}, /*index=...) custom-call(bf16[2048,1536]{1,0:T(8,128)(2,1)} %get-tuple-element.71.q, ...), custom_call_target="tpu_custom_call", output_to_operand_aliasing={{7}: (14, {})} | custom-call | flops 38654705664 | bytes 77107200 | tf_op jit(solution)/shard_map/pallas_call | solution.py:1428
  199.0 85.2 %shard_map.155 = (bf16[5488,128]{1,0:T(8,128)(2,1)}, f32[40,128]{1,0:T(8,128)}, bf16[512,256]{1,0:T(8,128)(2,1)}, bf16[2,2,2,6000,128]{4,3,2,1,0:T(8,128)(2,1)}) custom-call(bf16[2,2,2,6000,128]{4,3,2,1,0:T(8,128)(2,1)} %bitcast.16, bf16[512,256]{1,0:T(8,128)(2,1)} %bitcast.23, ...), custom_call_target="tpu_custom_call", output_to_operand_aliasing={{3}: (0, {})} | custom-call | tf_op jit(solution)/shard_map/pallas_call | solution.py:1456
  284.3 8.8 %shard_map.156 = (f32[5488,128]{1,0:T(8,128)}, f32[5488,128]{1,0:T(8,128)}, f32[5488,128]{1,0:T(8,128)}, f32[5488,128]{1,0:T(8,128)}, f32[16,256]{1,0:T(8,128)},...) custom-call(s32[1]{0:T(128)} %bitcast.5.base, f32[40,128]{1,0:T(8,128)} %get-tuple-element.104.stats, ...), custom_call_target="tpu_custom_call" | custom-call | bytes 21667844 | tf_op jit(solution)/shard_map/pallas_call | solution.py:1428
  293.1 6.3 %shard_map.157 = f32[1,13]{1,0:T(1,128)} custom-call(f32[16,256]{1,0:T(8,128)} %get-tuple-element.112.norms_sq), custom_call_target="tpu_custom_call" | custom-call | tf_op jit(solution)/shard_map/pallas_call | solution.py:1725
  299.3 1.1 copy.22
